TPU v7x, 128 devices: a whole 4x4x4 slice. The times are simulated.
128 devices in a mesh: seq: 16 (over z_hi, x, core), batch: 8 (over y, z_lo).
Axes of the slice: x: 4, y: 4, z: 4 (z_hi: 2, z_lo: 2; z = z_hi * 2 + z_lo), core: 2. Of those that a mesh axis runs over, the one named last changes fastest.
Arguments:
- tokens: bfloat16 [8, 2048, 1024], P('batch', 'seq')
- doc_lengths: int32 [8, 4], P('batch'), may hold values from 0 to 2048, as said below
- block_order: int32 [32], replicated, may hold values from 0 to 31, each once
- small_params: bfloat16 [13312], P(('seq', 'batch'))
- w_qkv: bfloat16 [1024, 3072], P(('seq', 'batch')), may hold values from -0.1875 to 0.1875
- w_out: bfloat16 [1024, 1024], P(('seq', 'batch')), may hold values from -0.75 to 0.75
- w_up: bfloat16 [1024, 4096], P(('seq', 'batch')), may hold values from -0.1875 to 0.1875
- w_down: bfloat16 [4096, 1024], P(('seq', 'batch')), may hold values from -0.09375 to 0.09375
- cotangent: bfloat16 [8, 2048, 1024], P('batch', 'seq'), may hold values from -6 to 6
Outputs:
- mixed: bfloat16 [8, 2048, 1024], P('batch', 'seq')
- grad_tokens: bfloat16 [8, 2048, 1024], P('batch', 'seq')
- grad_small: float32 [13312], P(('seq', 'batch'))
- grad_qkv: float32 [1024, 3072], P(('seq', 'batch'))
- grad_out: float32 [1024, 1024], P(('seq', 'batch'))
- grad_up: float32 [1024, 4096], P(('seq', 'batch'))
- grad_down: float32 [4096, 1024], P(('seq', 'batch'))
Inputs may be any that keep to these rules, and one draw needn't show every extreme that they name: `doc_lengths`: each row's entries sum to 2048; some rows are one document (2048 then zeros), the others are cut into 4 documents, some possibly empty.
All inputs are finite; a program needn't handle non-finite values.
Results may differ from a plain program's by a relative error of at most 0.018.
Values may be sent and summed in bfloat16 or wider, within the bound.
A program may use at most 192 MiB of HBM per device.

v0:
```python
from functools import partial

import jax
import jax.numpy as jnp
from jax import lax
from jax.sharding import PartitionSpec as P

HD = 64
ROT = 16


EPS = 1e-05
NEG = -1e30


def side_by_side(arrays, axis, dim, along):
    ends, at = ([], 0)
    for a in arrays[:-1]:
        at += a.shape[along]
        ends.append(at)
    both = jnp.concatenate(arrays, axis=along)
    return tuple(jnp.split(lax.all_gather(both, axis, axis=dim, tiled=True), ends, axis=along))


def laid_out(pieces, dim):
    shape = list(pieces.shape[1:])
    shape[dim] *= pieces.shape[0]
    return jnp.moveaxis(pieces, 0, dim).reshape(shape)


def gather_together(arrays, axis, dims):
    flat = jnp.concatenate([a.reshape(-1) for a in arrays])
    lines, at, done = (lax.all_gather(flat, axis), 0, [])
    for a, dim in zip(arrays, dims):
        pieces = lines[:, at : at + a.size].reshape(-1, *a.shape)
        done.append(laid_out(pieces, dim))
        at += a.size
    return tuple(done)


def split_up(array, dim, devices):
    shape = array.shape
    pieces = array.reshape(*shape[:dim], devices, shape[dim] // devices, *shape[dim + 1 :])
    return jnp.moveaxis(pieces, dim, 0)


def sum_together(arrays, axis, dims):
    devices = lax.axis_size(axis)
    pieces = [split_up(a, dim, devices) for a, dim in zip(arrays, dims)]
    lines = jnp.concatenate([b.reshape(devices, -1) for b in pieces], axis=1)
    width = max(16, -(-lines.shape[1] // 1024) * 8)
    lines = jnp.pad(lines, ((0, 0), (0, width * 128 - lines.shape[1]))).reshape(-1, 128)
    flat, at, done = (lax.psum_scatter(lines, axis, tiled=True).reshape(-1), 0, [])
    for b in pieces:
        part = b[0]
        done.append(flat[at : at + part.size].reshape(part.shape))
        at += part.size
    return tuple(done)


def in_one_piece(arrays, axis, dim, along):
    ends, at = ([], 0)
    for a in arrays[:-1]:
        at += a.shape[along]
        ends.append(at)
    both = jnp.concatenate(arrays, axis=along)
    return tuple(
        jnp.split(lax.psum_scatter(both, axis, scatter_dimension=dim, tiled=True), ends, axis=along)
    )


def sent_and_summed(array, axis, dim):
    devices = lax.axis_size(axis)
    pieces = lax.all_to_all(split_up(array, dim, devices), axis, 0, 0, tiled=True)
    return jnp.sum(pieces.astype(jnp.float32), axis=0)


def side_by_side_2(arrays, axis, dim, along):
    both = jnp.concatenate(arrays, axis=along)
    filled, at, done = (sent_and_summed(both, axis, dim), 0, [])
    for a in arrays:
        done.append(lax.slice_in_dim(filled, at, at + a.shape[along], axis=along))
        at += a.shape[along]
    return tuple(done)


def positions_of(block_order, lengths, count, block):
    index = jnp.arange(count, dtype=jnp.int32)
    slots = jnp.arange(block_order.shape[0], dtype=jnp.int32)
    placed = jnp.sum(
        jnp.where((index // block)[:, None] == slots[None, :], block_order[None, :], 0), axis=1
    )
    where = placed * block + index % block
    ends = jnp.cumsum(lengths)
    docs = jnp.sum((where[:, None] >= ends[None, :]).astype(jnp.int32), axis=1)
    firsts = ends - lengths
    number = jnp.arange(lengths.shape[0], dtype=jnp.int32)
    begin = jnp.sum(jnp.where(docs[:, None] == number[None, :], firsts[None, :], 0), axis=1)
    return (where, docs, where - begin)


def rotate(part, relpos):
    half = ROT // 2
    rates = 10000.0 ** (-2.0 * jnp.arange(half, dtype=jnp.float32) / ROT)
    angle = relpos.astype(jnp.float32)[:, None] * rates[None, :]
    cosine = jnp.cos(angle)[:, None, :]
    sine = jnp.sin(angle)[:, None, :]
    front = part[..., :half]
    latter = part[..., half:ROT]
    return jnp.concatenate(
        [front * cosine - latter * sine, latter * cosine + front * sine, part[..., ROT:]], axis=-1
    )


def split_small(small, width, inner):
    return (
        small[:width],
        small[width : 2 * width],
        small[2 * width : 3 * width],
        small[3 * width : 4 * width],
        small[4 * width : 7 * width],
        small[7 * width : 8 * width],
        small[8 * width : 8 * width + inner],
        small[8 * width + inner :],
    )


def contract_rows(left, right):
    return lax.dot_general(
        left, right, (((0,), (0,)), ((), ())), preferred_element_type=jnp.float32
    )


def times_transposed(left, right):
    return lax.dot_general(
        left, right, (((1,), (1,)), ((), ())), preferred_element_type=jnp.float32
    )


def allowed_of(query_where, query_docs, key_where, key_docs):
    return (query_docs[:, None] == key_docs[None, :]) & (key_where[None, :] <= query_where[:, None])


def scores_of(query, key_block, scale):
    return jnp.einsum("qhd,khd->hqk", query, key_block, preferred_element_type=jnp.float32) * scale


def blocked(keys, values, key_where, key_docs):
    count, heads, size = keys.shape
    span = min(512, count)
    blocks = count // span
    return (
        span,
        (
            keys.reshape(blocks, span, heads, size),
            values.reshape(blocks, span, heads, size),
            key_where.reshape(blocks, span),
            key_docs.reshape(blocks, span),
        ),
    )


def forward_attention(query, keys, values, query_where, query_docs, key_where, key_docs, scale):
    rows, heads, size = query.shape
    span, items = blocked(keys, values, key_where, key_docs)

    def total_step(carry, item):
        key_block, value_block, block_where, block_docs = item
        allowed = allowed_of(query_where, query_docs, block_where, block_docs)

        def total_work(state):
            top, total = state
            scores = jnp.where(allowed[None], scores_of(query, key_block, scale), NEG)
            peak = jnp.maximum(top, jnp.max(scores, axis=-1))
            expos = jnp.where(allowed[None], jnp.exp(scores - peak[..., None]), 0.0)
            return (peak, total * jnp.exp(top - peak) + jnp.sum(expos, axis=-1))

        return (lax.cond(jnp.any(allowed), total_work, lambda state: state, carry), None)

    start = (jnp.full((heads, rows), NEG, jnp.float32), jnp.zeros((heads, rows), jnp.float32))
    (top, total), _ = lax.scan(total_step, start, items)
    log_total = top + jnp.log(total)

    def value_step(carry, item):
        key_block, value_block, block_where, block_docs = item
        allowed = allowed_of(query_where, query_docs, block_where, block_docs)

        def value_work(summed):
            probs = jnp.where(
                allowed[None],
                jnp.exp(scores_of(query, key_block, scale) - log_total[..., None]),
                0.0,
            )
            return summed + jnp.einsum(
                "hqk,khd->qhd",
                probs.astype(jnp.bfloat16),
                value_block,
                preferred_element_type=jnp.float32,
            )

        return (lax.cond(jnp.any(allowed), value_work, lambda summed: summed, carry), None)

    heads_out, _ = lax.scan(value_step, jnp.zeros((rows, heads, size), jnp.float32), items)
    return (heads_out, log_total)


def backward_attention(
    query, keys, values, grad_heads, log_total, query_where, query_docs, key_where, key_docs, scale
):
    rows, heads, size = query.shape
    count = keys.shape[0]
    span, items = blocked(keys, values, key_where, key_docs)

    def probs_of(key_block, allowed):
        return jnp.where(
            allowed[None], jnp.exp(scores_of(query, key_block, scale) - log_total[..., None]), 0.0
        )

    def delta_step(carry, item):
        key_block, value_block, block_where, block_docs = item
        allowed = allowed_of(query_where, query_docs, block_where, block_docs)

        def delta_work(summed):
            probs = probs_of(key_block, allowed)
            pulled = jnp.einsum(
                "qhd,khd->hqk", grad_heads, value_block, preferred_element_type=jnp.float32
            )
            return summed + jnp.sum(probs * pulled, axis=-1)

        return (lax.cond(jnp.any(allowed), delta_work, lambda summed: summed, carry), None)

    delta, _ = lax.scan(delta_step, jnp.zeros((heads, rows), jnp.float32), items)

    def grad_step(carry, item):
        key_block, value_block, block_where, block_docs = item
        allowed = allowed_of(query_where, query_docs, block_where, block_docs)

        def grad_work(grad_query):
            probs = probs_of(key_block, allowed)
            grad_value = jnp.einsum(
                "hqk,qhd->khd",
                probs.astype(jnp.bfloat16),
                grad_heads,
                preferred_element_type=jnp.float32,
            )
            pulled = jnp.einsum(
                "qhd,khd->hqk", grad_heads, value_block, preferred_element_type=jnp.float32
            )
            grad_scores = (probs * (pulled - delta[..., None])).astype(jnp.bfloat16)
            grad_query = (
                grad_query
                + jnp.einsum(
                    "hqk,khd->qhd", grad_scores, key_block, preferred_element_type=jnp.float32
                )
                * scale
            )
            grad_key = (
                jnp.einsum("hqk,qhd->khd", grad_scores, query, preferred_element_type=jnp.float32)
                * scale
            )
            return (grad_query, grad_key, grad_value)

        def skip(grad_query):
            empty = jnp.zeros((span, heads, size), jnp.float32)
            return (grad_query, empty, empty)

        grad_query, grad_key, grad_value = lax.cond(jnp.any(allowed), grad_work, skip, carry)
        return (grad_query, (grad_key, grad_value))

    grad_query, (grad_keys, grad_values) = lax.scan(
        grad_step, jnp.zeros((rows, heads, size), jnp.float32), items
    )
    return (
        grad_query,
        grad_keys.reshape(count, heads * size),
        grad_values.reshape(count, heads * size),
    )


def local(tokens, doc_lengths, block_order, small_params, w_qkv, w_out, w_up, w_down, cotangent):
    rows = tokens.shape[1]
    width = tokens.shape[2]
    inner = w_up.shape[1]
    heads = width // HD
    lanes = lax.axis_size("seq")
    count = rows * lanes
    mine = lax.axis_index("seq")
    scale = HD ** (-0.5)
    key_where, key_docs, key_rel = positions_of(block_order, doc_lengths[0], count, rows // 2)
    query_where = lax.dynamic_slice_in_dim(key_where, mine * rows, rows)
    query_docs = lax.dynamic_slice_in_dim(key_docs, mine * rows, rows)
    query_rel = lax.dynamic_slice_in_dim(key_rel, mine * rows, rows)
    qkv_full, out_full, small_full = (
        *side_by_side((w_qkv, w_out), ("seq", "batch"), 0, 1),
        lax.all_gather(small_params, ("seq", "batch"), axis=0, tiled=True),
    )
    up_full, down_full = gather_together((w_up, w_down), ("seq", "batch"), (0, 0))
    pieces = split_small(small_full.astype(jnp.float32), width, inner)
    gain_one, shift_one, gain_two, shift_two, bias_qkv, bias_out, bias_up, bias_down = pieces
    inputs = tokens[0].astype(jnp.float32)
    centred = inputs - jnp.mean(inputs, axis=-1, keepdims=True)
    inverse = lax.rsqrt(jnp.mean(centred * centred, axis=-1, keepdims=True) + EPS)
    normed = centred * inverse
    first = (normed * gain_one + shift_one).astype(jnp.bfloat16)
    second = (normed * gain_two + shift_two).astype(jnp.bfloat16)
    projected = (jnp.dot(first, qkv_full, preferred_element_type=jnp.float32) + bias_qkv).reshape(
        rows, 3, heads, HD
    )
    query = rotate(projected[:, 0], query_rel).astype(jnp.bfloat16)
    keyrot = rotate(projected[:, 1], query_rel).astype(jnp.bfloat16).reshape(rows, width)
    value = projected[:, 2].astype(jnp.bfloat16).reshape(rows, width)
    keys_all, values_all = side_by_side((keyrot, value), "seq", 0, 1)
    keys_all = keys_all.reshape(count, heads, HD)
    values_all = values_all.reshape(count, heads, HD)
    heads_out, log_total = forward_attention(
        query, keys_all, values_all, query_where, query_docs, key_where, key_docs, scale
    )
    attn_heads = heads_out.reshape(rows, width).astype(jnp.bfloat16)
    attention = jnp.dot(attn_heads, out_full, preferred_element_type=jnp.float32) + bias_out
    hidden = jnp.dot(second, up_full, preferred_element_type=jnp.float32) + bias_up
    active = jax.nn.gelu(hidden, approximate=False).astype(jnp.bfloat16)
    feed = jnp.dot(active, down_full, preferred_element_type=jnp.float32) + bias_down
    mixed = (inputs + attention + feed).astype(jnp.bfloat16)
    up_back, down_back = gather_together((w_up, w_down), ("seq", "batch"), (0, 0))
    grad_y = cotangent[0]
    grad_float = grad_y.astype(jnp.float32)
    grad_active = times_transposed(grad_y, down_back)
    gelu_value, gelu_back = jax.vjp(partial(jax.nn.gelu, approximate=False), hidden)
    grad_hidden = gelu_back(grad_active)[0].astype(jnp.bfloat16)
    grad_second = times_transposed(grad_hidden, up_back)
    grad_down = contract_rows(active, grad_y)
    grad_up = contract_rows(second, grad_hidden)
    part_up, part_down = (
        lax.psum_scatter(
            grad_up.astype(jnp.bfloat16), "seq", scatter_dimension=0, tiled=True
        ).astype(jnp.float32),
        lax.psum_scatter(
            grad_down.astype(jnp.bfloat16), "seq", scatter_dimension=0, tiled=True
        ).astype(jnp.float32),
    )
    summed_up, summed_down = tuple(
        (
            part.astype(jnp.float32)
            for part in sum_together(
                (part_up.astype(jnp.bfloat16), part_down.astype(jnp.bfloat16)), "batch", (0, 0)
            )
        )
    )
    qkv_back, out_back, small_back = (
        *side_by_side((w_qkv, w_out), ("seq", "batch"), 0, 1),
        lax.all_gather(small_params, ("seq", "batch"), axis=0, tiled=True),
    )
    gains_back = split_small(small_back.astype(jnp.float32), width, inner)
    gain_one_back, gain_two_back = (gains_back[0], gains_back[2])
    grad_out = contract_rows(attn_heads, grad_y)
    grad_heads = times_transposed(grad_y, out_back).astype(jnp.bfloat16).reshape(rows, heads, HD)
    keys_back, values_back = side_by_side((keyrot, value), "seq", 0, 1)
    keys_back = keys_back.reshape(count, heads, HD)
    values_back = values_back.reshape(count, heads, HD)
    grad_query, grad_keys, grad_values = backward_attention(
        query,
        keys_back,
        values_back,
        grad_heads,
        log_total,
        query_where,
        query_docs,
        key_where,
        key_docs,
        scale,
    )
    grad_key, grad_value = tuple(
        (
            part.astype(jnp.float32)
            for part in in_one_piece(
                (grad_keys.astype(jnp.bfloat16), grad_values.astype(jnp.bfloat16)), "seq", 0, 1
            )
        )
    )
    turned_query = rotate(grad_query, -query_rel)
    turned_key = rotate(grad_key.reshape(rows, heads, HD), -query_rel)
    grad_projected = jnp.stack(
        [turned_query, turned_key, grad_value.reshape(rows, heads, HD)], axis=1
    )
    grad_projected = grad_projected.reshape(rows, 3 * width).astype(jnp.bfloat16)
    grad_qkv = contract_rows(first, grad_projected)
    grad_first = times_transposed(grad_projected, qkv_back)
    merged = grad_first * gain_one_back + grad_second * gain_two_back
    grad_norm = inverse * (
        merged
        - jnp.mean(merged, axis=-1, keepdims=True)
        - normed * jnp.mean(merged * normed, axis=-1, keepdims=True)
    )
    grad_tokens = (grad_float + grad_norm).astype(jnp.bfloat16)
    dy_total = jnp.sum(grad_float, axis=0)
    grad_small = jnp.concatenate(
        [
            jnp.sum(grad_first * normed, axis=0),
            jnp.sum(grad_first, axis=0),
            jnp.sum(grad_second * normed, axis=0),
            jnp.sum(grad_second, axis=0),
            jnp.sum(grad_projected.astype(jnp.float32), axis=0),
            dy_total,
            jnp.sum(grad_hidden.astype(jnp.float32), axis=0),
            dy_total,
        ]
    )
    part_qkv, part_out, part_small = (
        *tuple(
            (
                part.astype(jnp.float32)
                for part in in_one_piece(
                    (grad_qkv.astype(jnp.bfloat16), grad_out.astype(jnp.bfloat16)), "seq", 0, 1
                )
            )
        ),
        lax.psum_scatter(
            grad_small.astype(jnp.bfloat16), "seq", scatter_dimension=0, tiled=True
        ).astype(jnp.float32),
    )
    summed_qkv, summed_out, summed_small = (
        *side_by_side_2(
            (part_qkv.astype(jnp.bfloat16), part_out.astype(jnp.bfloat16)), "batch", 0, 1
        ),
        sent_and_summed(part_small.astype(jnp.bfloat16), "batch", 0),
    )
    return (
        mixed[None],
        grad_tokens[None],
        summed_small,
        summed_qkv,
        summed_out,
        summed_up,
        summed_down,
    )


def solution(mesh):
    placed = (
        P("batch", "seq", None),
        P("batch", None),
        P(),
        P(("seq", "batch")),
        P(("seq", "batch"), None),
        P(("seq", "batch"), None),
        P(("seq", "batch"), None),
        P(("seq", "batch"), None),
        P("batch", "seq", None),
    )
    return jax.shard_map(
        local,
        mesh=mesh,
        in_specs=placed,
        out_specs=(
            P("batch", "seq", None),
            P("batch", "seq", None),
            P(("seq", "batch")),
            P(("seq", "batch"), None),
            P(("seq", "batch"), None),
            P(("seq", "batch"), None),
            P(("seq", "batch"), None),
        ),
        check_vma=False,
    )
```

profile of v0, /device:TPU:1, one launch (start us, length us, event | category | flops | bytes accessed | tf_op | source)
XLA Modules:
  0.0 1211.2 jit_solution(3384940021703741474)
XLA Ops:
  9.6 69.1 %all-reduce = bf16[13312]{0:T(1024)(128)(2,1)S(1)} all-reduce(bf16[13312]{0:T(1024)(128)(2,1)S(1)} %dynamic-update-slice), channel_id=1, replica_groups=mesh['seq'=16,'batch'=8] {'seq','batch'}, use_global_device_ids=true, to_apply=%add | all-reduce | flops 13312 | bytes 53248
  84.9 241.2 %all-gather.5.cloned.1.call-done = bf16[1024,4096]{1,0:T(8,128)(2,1)} async-done(((bf16[8,4096]{1,0:T(8,128)(2,1)}), bf16[1024,4096]{1,0:T(8,128)(2,1)}) %all-gather.5.cloned.1.call-update) | async-done | bytes 8388624 | tf_op jit(solution)/shard_map/all_gather | solution.py:22
  326.1 4.0 fusion.56
  333.3 3.0 fusion.81
  336.3 76.5 %all-gather.7.cloned.1.call-done = bf16[2048,2048]{0,1:T(8,128)(2,1)} async-done(((bf16[128,2048]{0,1:T(8,128)(2,1)}), bf16[2048,2048]{0,1:T(8,128)(2,1)}) %all-gather.7.cloned.1.call-update) | async-done | bytes 8388624 | tf_op jit(solution)/shard_map/all_gather | solution.py:22
  412.8 6.0 fusion.163
  418.8 7.8 reshape_reshape.22
  426.6 5.2 copy.62
  431.8 7.8 reshape_reshape.23
  439.7 5.1 copy.63
  444.8 19.6 %while.55 = (s32[]{:T(128)}, f32[16,128]{1,0:T(8,128)S(1)}, f32[16,128]{1,0:T(8,128)S(1)}, s32[128]{0:T(128)S(1)}, s32[4,512]{1,0:T(4,128)S(1)}, /*index=5*/s32[...) while((s32[]{:T(128)}, f32[16,128]{1,0:T(8,128)S(1)}, ...), condition=%wide.region_12.13_spmd, body=%wide.region_6.12_spmd.sunk | while | flops 142872576 | bytes 10016455 | solution.py:181
  446.4 3.3 conditional.8
  451.3 3.3 conditional.8
  456.2 3.3 conditional.8
  461.1 3.3 conditional.8
  464.4 25.8 %while.57 = (s32[]{:T(128)}, f32[16,128]{1,0:T(8,128)S(1)}, s32[128]{0:T(128)S(1)}, s32[4,512]{1,0:T(4,128)S(1)}, s32[4,512]{1,0:T(4,128)S(1)}, /*index=5*/s32[1...) while((s32[]{:T(128)}, f32[16,128]{1,0:T(8,128)S(1)}, ...), condition=%wide.region_23.24_spmd, body=%wide.region_18.23_spmd.sunk | while | flops 273940480 | bytes 11196615 | solution.py:232
  466.0 4.9 conditional.10
  472.4 4.9 conditional.10
  478.8 4.9 conditional.10
  485.3 4.9 conditional.10
  487.3 2.9 fusion.19
  490.3 51.0 %while.58 = (s32[]{:T(128)}, f32[128,16,64]{0,2,1:T(8,128)S(1)}, bf16[4,512,16,64]{1,3,2,0:T(8,128)(2,1)}, bf16[4,512,16,64]{1,3,2,0:T(8,128)(2,1)}, s32[128]{0:...) while((s32[]{:T(128)}, f32[128,16,64]{0,2,1:T(8,128)S(1)}, ...), condition=%wide.region_28.29_spmd, body=%wide.region_24.28_spmd.sunk | while | flops 683147264 | bytes 30645500 | solution.py:270
  492.1 9.6 conditional.11
  494.1 2.9 fusion.27
  504.8 9.6 conditional.11
  517.5 9.6 conditional.11
  530.2 9.6 conditional.11
  541.3 5.8 copy.68
  547.0 3.3 copy.83
  550.4 3.5 copy.69
  553.9 3.3 copy.84
  557.2 8.4 pad_maximum_fusion
  565.6 12.4 %copy.77 = bf16[2048,2048]{1,0:T(8,128)(2,1)} copy(bf16[2048,2048]{0,1:T(8,128)(2,1)} %pad_maximum_fusion) | data formatting | bytes 16777216
  578.1 162.0 %all-gather.9.cloned.1.call-done = bf16[8388608]{0:T(1024)(128)(2,1)} async-done(((bf16[65536]{0:T(1024)(128)(2,1)}), bf16[8388608]{0:T(1024)(128)(2,1)}) %all-gather.9.cloned.1.call-update) | async-done | bytes 16777232 | tf_op jit(solution)/shard_map/all_gather | solution.py:33
  740.1 20.5 %reshape.337 = bf16[128,65536]{1,0:T(8,128)(2,1)} reshape(bf16[8388608]{0:T(1024)(128)(2,1)} %all-gather.9.cloned.1.call-done) | data formatting | bytes 33554432 | tf_op jit(solution)/shard_map/all_gather | solution.py:33
  760.6 12.6 %fusion.162 = (bf16[128,32768]{1,0:T(8,128)(2,1)}, bf16[128,32768]{1,0:T(8,128)(2,1)}) fusion(bf16[128,65536]{1,0:T(8,128)(2,1)} %reshape.337), kind=kLoop, calls=%fused_computation.246 | loop fusion | bytes 33554432 | tf_op jit(solution)/shard_map/slice | solution.py:35
  773.2 13.6 %reshape_reshape.24 = bf16[1024,4096]{1,0:T(8,128)(2,1)} reshape(bf16[128,32768]{1,0:T(8,128)(2,1)} %get-tuple-element.757) | data formatting | bytes 16777216 | tf_op jit(solution)/shard_map/reshape;reshape | solution.py:28
  786.8 13.6 %reshape_reshape.25 = bf16[4096,1024]{1,0:T(8,128)(2,1)} reshape(bf16[128,32768]{1,0:T(8,128)(2,1)} %get-tuple-element.756) | data formatting | bytes 16777216 | tf_op jit(solution)/shard_map/reshape;reshape | solution.py:28
  800.4 8.4 multiply_convert_fusion
  808.8 7.5 fusion.166
  817.3 5.7 convolution_convert_fusion.1
  823.1 5.6 convolution_convert_fusion
  829.5 18.6 %while.56 = (s32[]{:T(128)}, f32[128,16,64]{0,2,1:T(8,128)S(1)}, s32[128]{0:T(128)S(1)}, s32[4,512]{1,0:T(4,128)S(1)}, s32[4,512]{1,0:T(4,128)S(1)}, /*index=5*/...) while((s32[]{:T(128)}, f32[128,16,64]{0,2,1:T(8,128)S(1)}, ...), condition=%wide.region_17.18_spmd, body=%wide.region_13.17_spmd.sunk | while | flops 273022976 | bytes 3561655 | solution.py:203
  831.4 3.0 conditional.9
  831.4 3.0 fusion.8
  836.0 3.0 conditional.9
  836.0 3.0 fusion.8
  840.5 3.0 conditional.9
  840.5 3.0 fusion.8
  845.0 3.0 conditional.9
  845.0 3.0 fusion.8
  854.9 4.7 convolution_convert_fusion.2
  859.6 8.9 pad_maximum_fusion.1
  870.4 5.5 convolution_add_fusion.1
  878.8 5.9 fusion.52
  884.6 67.0 %reduce-scatter.10.cloned.1.call-done = bf16[64,4096]{1,0:T(8,128)(2,1)} async-done(((bf16[1024,4096]{1,0:T(8,128)(2,1)}), bf16[64,4096]{1,0:T(8,128)(2,1)}) %reduce-scatter.10.cloned.1.call-update) | async-done | bytes 524304 | tf_op jit(solution)/shard_map/reduce_scatter | solution.py:334
  952.9 104.2 %reduce-scatter.12.cloned.1.call-done = bf16[256,1024]{1,0:T(8,128)(2,1)} async-done(((bf16[4096,1024]{1,0:T(8,128)(2,1)}), bf16[256,1024]{1,0:T(8,128)(2,1)}) %reduce-scatter.12.cloned.1.call-update) | async-done | bytes 524304 | tf_op jit(solution)/shard_map/reduce_scatter | solution.py:337
  1060.0 6.5 fusion.154
  1066.6 61.5 %all-reduce.1 = bf16[13312]{0:T(1024)(128)(2,1)S(1)} all-reduce(bf16[13312]{0:T(1024)(128)(2,1)S(1)} %constant_dynamic-update-slice_fusion.2), channel_id=4, replica_groups=mesh['seq'=16,'batch'=8] {'seq'}, use_global_device_ids=true, to_apply=%region_39.40.clone | all-reduce | flops 13312 | bytes 53248
  1128.8 4.4 all-to-all-start
  1133.2 4.9 all-to-all-done
  1138.1 24.8 %reduce-scatter.8.cloned.1.call-done = bf16[64,4096]{1,0:T(8,128)(2,1)} async-done(((bf16[1024,4096]{1,0:T(8,128)(2,1)}), bf16[64,4096]{1,0:T(8,128)(2,1)}) %reduce-scatter.8.cloned.1.call-update) | async-done | bytes 524304 | tf_op jit(solution)/shard_map/reduce_scatter | solution.py:68
  1162.9 4.0 all-to-all-start.1
  1168.4 32.1 %reduce-scatter.14.cloned.1.call-done = bf16[512,128]{1,0:T(8,128)(2,1)} async-done(((bf16[4096,128]{1,0:T(8,128)(2,1)}), bf16[512,128]{1,0:T(8,128)(2,1)}) %reduce-scatter.14.cloned.1.call-update) | async-done | bytes 131088 | tf_op jit(solution)/shard_map/reduce_scatter | solution.py:53
  (231 shorter events, 119.7 us)
Async XLA Ops:
  7.2 318.9 %all-gather.5.cloned.1.call-start = ((), (), s32[]{:S(2)}) async-start(), calls=%async_computation.7 | async-start | bytes 8454144 | tf_op jit(solution)/shard_map/all_gather | solution.py:22
  8.7 404.1 %all-gather.7.cloned.1.call-start = ((), (), s32[]{:S(2)}) async-start(), calls=%async_computation.8 | async-start | bytes 8912896 | tf_op jit(solution)/shard_map/all_gather | solution.py:22
  84.9 245.1 %copy-start.7 = (f32[1024]{0:T(1024)}, f32[1024]{0:T(1024)S(1)}, u32[]{:S(2)}) copy-start(f32[1024]{0:T(1024)S(1)} %get-tuple-element.780) | copy-start | bytes 12292
  84.9 245.1 %copy-start.10 = (f32[1024]{0:T(1024)}, f32[1024]{0:T(1024)S(1)}, u32[]{:S(2)}) copy-start(f32[1024]{0:T(1024)S(1)} %get-tuple-element.781) | copy-start | bytes 12292
  330.6 1.2 copy-start.13
  330.7 1.2 copy-start.14
  330.7 2.6 copy-start.5
  331.8 408.3 %all-gather.9.cloned.1.call-start = ((), (), s32[]{:S(2)}) async-start(), calls=%async_computation.13 | async-start | bytes 16908288 | tf_op jit(solution)/shard_map/all_gather | solution.py:33
  332.6 517.5 %reduce-scatter.16.cloned.1.call-start = ((), (), s32[]{:S(2)}) async-start(), calls=%async_computation.14 | async-start | bytes 8912896
  547.0 3.4 copy-start.4
  578.0 373.6 %reduce-scatter.10.cloned.1.call-start = ((), (), s32[]{:S(2)}) async-start(), calls=%async_computation.10 | async-start | bytes 8912896 | tf_op jit(solution)/shard_map/reduce_scatter | solution.py:334
  786.8 13.6 %copy-start.1 = (bf16[1,128,1024]{2,1,0:T(8,128)(2,1)S(1)}, bf16[1,128,1024]{2,1,0:T(8,128)(2,1)}, u32[]{:S(2)}) copy-start(bf16[1,128,1024]{2,1,0:T(8,128)(2,1)} %param.25) | copy-start | bytes 786436
  786.8 13.6 %copy-start.9 = (f32[1024]{0:T(1024)S(1)}, f32[1024]{0:T(1024)}, u32[]{:S(2)}) copy-start(f32[1024]{0:T(1024)} %get-tuple-element.783) | copy-start | bytes 12292
  786.8 13.6 %copy-start.12 = (f32[1024]{0:T(1024)S(1)}, f32[1024]{0:T(1024)}, u32[]{:S(2)}) copy-start(f32[1024]{0:T(1024)} %get-tuple-element.784) | copy-start | bytes 12292
  800.4 8.4 copy-start
  800.4 8.4 copy-start.6
  816.3 1.0 copy-start.2
  823.0 234.0 %reduce-scatter.12.cloned.1.call-start = ((), (), s32[]{:S(2)}) async-start(), calls=%async_computation.11 | async-start | bytes 8912896 | tf_op jit(solution)/shard_map/reduce_scatter | solution.py:337
  828.7 334.2 %reduce-scatter.8.cloned.1.call-start = ((), (), s32[]{:S(2)}) async-start(), calls=%async_computation.9 | async-start | bytes 8912896 | tf_op jit(solution)/shard_map/reduce_scatter | solution.py:68
  850.1 2.3 copy-start.17
  850.1 2.3 copy-start.18
  852.3 2.6 copy-start.8
  852.3 2.6 copy-start.11
  868.5 0.7 copy-start.19
  868.5 1.9 copy-start.16
  868.5 332.0 %reduce-scatter.14.cloned.1.call-start = ((), (), s32[]{:S(2)}) async-start(), calls=%async_computation.12 | async-start | bytes 1179648 | tf_op jit(solution)/shard_map/reduce_scatter | solution.py:53
  870.4 5.5 copy-start.15
  1058.5 1.5 copy-start.3
  1128.8 9.3 all-to-all-start
  1162.9 39.9 %all-to-all-start.1 = ((bf16[8,8,4096]{2,1,0:T(8,128)(2,1)}), bf16[8,8,4096]{2,1,0:T(8,128)(2,1)S(1)}, u32[]{:S(2)}, u32[]{:S(2)}) async-start(bf16[8,8,4096]{2,1,0:T(8,128)(2,1)} %bitcast.267), calls=%async_computation.2 | async-start | bytes 1048576 | tf_op jit(solution)/shard_map/all_to_all | solution.py:74
Sparse Core Ops, SparseCore 0:
  10.3 315.7 all-gather.4
  331.9 80.8 all-gather.6
  415.1 324.9 all-gather.8
  744.3 101.8 reduce-scatter.15
  850.3 101.2 reduce-scatter.9
  955.8 101.2 reduce-scatter.11
  1061.4 101.4 reduce-scatter.7
  1165.3 35.2 reduce-scatter.13
where the time goes:
time: 1220 us; the launch traced here: 1210 us
  waiting for transfers between devices  713 us (58%)
  local copies, waits for them, and re-layouts  141 us (12%)
  matrix products  140 us (11%)
  blocking collectives  131 us (11%)
  other arithmetic  50.1 us (4%)
  between operations  15.5 us (1%)
    all_gather x2, waiting for transfers between devices, side_by_side(): lax.all_gather(both, axis, axis=dim, tiled=True)  318 us
    all_gather x1, waiting for transfers between devices, gather_together(): lines, at, done = (lax.all_gather(flat, axis), 0, [])  162 us
    unnamed x2, blocking collectives  131 us
    reduce_scatter x1, waiting for transfers between devices, local(): lax.psum_scatter(grad_down.astype(jnp.bfloat16), 'seq', scatter_dimension...  104 us
    reduce_scatter x1, waiting for transfers between devices, local(): lax.psum_scatter(grad_up.astype(jnp.bfloat16), 'seq', scatter_dimension=0...  67 us
    reduce_scatter x1, waiting for transfers between devices, sum_together(): lax.psum_scatter(lines, axis, tiled=True).reshape(-1)  32.1 us
    another operation x2, local copies, waits for them, and re-layouts, laid_out(): return jnp.moveaxis(pieces, 0, dim).reshape(shape)  27.1 us
    dot_general x12, matrix products, scores_of(): jnp.einsum('qhd,khd->hqk', query, key_block, preferred_element_type=jnp.f...  25.1 us
  transfers between devices with their start and end apart: 10, of which 8 were waited for; matrix products, arithmetic and copies ran while one was open for 26% of the time, Pallas kernels for 0%

commit v1 on v0

v1 whole, which is shorter than its diff:
```python
import jax
import jax.numpy as jnp
import numpy as np
from jax import lax
from jax.experimental import pallas as pl
from jax.experimental.pallas import tpu as pltpu
from jax.sharding import PartitionSpec as P

HD = 64
ROT = 16
EPS = 1e-05
NEG = -1e30
MESH = pl.DeviceIdType.MESH
BF = jnp.bfloat16
F32 = jnp.float32

SEQ = 16
BATCH = 8
TOK = 128
ROW = SEQ * TOK
D = 1024
HID = 256
PER = 104
QB = 256


def dot(a, b):
    return lax.dot_general(a, b, (((1,), (0,)), ((), ())), preferred_element_type=F32)


def dot_nt(a, b):
    return lax.dot_general(a, b, (((1,), (1,)), ((), ())), preferred_element_type=F32)


def dot_tn(a, b):
    return lax.dot_general(a, b, (((0,), (0,)), ((), ())), preferred_element_type=F32)


def iota(shape, dim):
    return lax.broadcasted_iota(jnp.int32, shape, dim)


def slot(z, x, c):
    return z * 8 + x * 2 + c


def rows_at(index, count):
    return pl.ds(pl.multiple_of(index * count, count), count)


def kernel(
    x_ref, dy_ref, ws_ref, wd_ref, wo_ref, rate_ref, inv_ref, order_ref, len_ref,
    mixed_ref, gtok_ref, gw_ref, gd_ref, go_ref, small_ref,
    nrm, dya, wst, wbuf, wd2, wo2, wob, rawq, rawu, cols, wcat, brow, drow,
    prj, act, dge, tabc, tabs, qs, ks, vs, qst, dos, dost, osort, ost,
    sbuf, dcat, dkt, dvt, dsort, stat,
    part_m, part_d, sib_m, half_m, full_m, zed_m, sib_d, half_d, full_d, zed_d,
    gdacc, gtu, gdsend, gosend, gdrecv, gorecv, gsend, grecv, gsum, gfin, smv, smr, smt, sma,
    ag_ss, ag_rs, rs_ss, rs_rs, sq_ss, sq_rs, bt_ss, bt_rs,
):
    s = lax.axis_index("seq")
    b = lax.axis_index("batch")
    z, x, c = s // 8, lax.rem(s // 2, 4), lax.rem(s, 2)
    xr, xl, xo = lax.rem(x + 1, 4), lax.rem(x + 3, 4), lax.rem(x + 2, 4)
    zo, co = 1 - z, 1 - c
    right, left = (slot(z, xr, c), b), (slot(z, xl, c), b)
    across, sibling = (slot(zo, x, c), b), (slot(z, x, co), b)

    def remote(src, dst, send, recv, device):
        return pltpu.make_async_remote_copy(
            src_ref=src, dst_ref=dst, send_sem=send, recv_sem=recv,
            device_id=device, device_id_type=MESH,
        )

    barrier = pltpu.get_barrier_semaphore()

    @pl.loop(1, SEQ)
    def _(j):
        pl.semaphore_signal(barrier, inc=1, device_id=(lax.rem(s + j, SEQ), b), device_id_type=MESH)

    @pl.loop(1, BATCH)
    def _(j):
        pl.semaphore_signal(barrier, inc=1, device_id=(s, lax.rem(b + j, BATCH)), device_id_type=MESH)

    def normed_of():
        inputs = x_ref[...].astype(F32)
        centred = inputs - jnp.mean(inputs, axis=-1, keepdims=True)
        inverse = lax.rsqrt(jnp.mean(centred * centred, axis=-1, keepdims=True) + EPS)
        return inputs, centred * inverse, inverse

    nrm[rows_at(s, TOK), :] = normed_of()[1].astype(BF)
    dya[rows_at(s, TOK), :] = dy_ref[...]
    wst[rows_at(s, 16), :] = ws_ref[rows_at(s, 16), :]
    wd2[rows_at(b, 32), :] = wd_ref[...]
    wo2[rows_at(b, 8), :] = wo_ref[...]
    pl.semaphore_wait(barrier, SEQ - 1 + BATCH - 1)

    def seq_copy(j, k, src, dst):
        return remote(src, dst, sq_ss.at[k, j], sq_rs.at[k, j], (lax.rem(s + j, SEQ), b))

    def batch_copy(j, k, src, dst):
        return remote(src, dst, bt_ss.at[k, j], bt_rs.at[k, j], (s, lax.rem(b + j, BATCH)))

    @pl.loop(1, SEQ)
    def _(j):
        peer = lax.rem(s + j, SEQ)
        seq_copy(j, 0, ws_ref.at[rows_at(peer, 16)], wst.at[rows_at(s, 16)]).start()

    class Gather:
        def __init__(self, buf, k):
            self.buf, self.k = buf, k

        def copy(self, e, index, device, low=0, count=TOK):
            at = self.buf.at[pl.ds(pl.multiple_of(index * TOK + low, 64), count)]
            return remote(at, at, ag_ss.at[self.k, e], ag_rs.at[self.k, e], device)

        def sends(self):
            own, far = s, slot(zo, x, c)
            return {
                0: (own, right, 0, TOK), 1: (own, left, 0, TOK),
                2: (own, across, 0, TOK), 3: (own, sibling, 0, TOK),
                4: (far, right, 0, TOK), 5: (far, left, 0, TOK), 6: (far, sibling, 0, TOK),
                7: (slot(z, xl, c), right, 0, 64), 8: (slot(z, xr, c), left, 64, 64),
                9: (slot(z, xl, c), sibling, 0, TOK), 10: (slot(z, xr, c), sibling, 0, TOK),
                11: (slot(zo, xl, c), right, 0, 64), 12: (slot(zo, xr, c), left, 64, 64),
                13: (slot(zo, xl, c), sibling, 0, TOK), 14: (slot(zo, xr, c), sibling, 0, TOK),
                15: (slot(z, xo, c), sibling, 0, TOK), 16: (slot(zo, xo, c), sibling, 0, TOK),
            }

        def receives(self):
            return {
                0: (slot(z, xl, c), 0, TOK), 1: (slot(z, xr, c), 0, TOK),
                2: (slot(zo, x, c), 0, TOK), 3: (slot(z, x, co), 0, TOK),
                4: (slot(zo, xl, c), 0, TOK), 5: (slot(zo, xr, c), 0, TOK), 6: (slot(zo, x, co), 0, TOK),
                7: (slot(z, xo, c), 0, 64), 8: (slot(z, xo, c), 64, 64),
                9: (slot(z, xl, co), 0, TOK), 10: (slot(z, xr, co), 0, TOK),
                11: (slot(zo, xo, c), 0, 64), 12: (slot(zo, xo, c), 64, 64),
                13: (slot(zo, xl, co), 0, TOK), 14: (slot(zo, xr, co), 0, TOK),
                15: (slot(z, xo, co), 0, TOK), 16: (slot(zo, xo, co), 0, TOK),
            }

        def start(self, *events):
            for e in events:
                index, device, low, count = self.sends()[e]
                self.copy(e, index, device, low, count).start()

        def wait(self, *events):
            for e in events:
                index, low, count = self.receives()[e]
                self.copy(e, index, right, low, count).wait_recv()

        def step(self, n):
            if n == 0:
                self.start(0, 1, 2, 3)
            elif n == 1:
                self.wait(2)
                self.start(4, 5, 6)
                self.wait(0)
                self.start(7, 9)
                self.wait(1)
                self.start(8, 10)
            elif n == 2:
                self.wait(4)
                self.start(11, 13)
                self.wait(5)
                self.start(12, 14)
            elif n == 3:
                self.wait(7, 8)
                self.start(15)
                self.wait(11, 12)
                self.start(16)
            else:
                self.wait(3, 6, 9, 10, 13, 14, 15, 16)

        def drain(self):
            for e, (index, device, low, count) in self.sends().items():
                self.copy(e, index, device, low, count).wait_send()

    normed_gather = Gather(nrm, 0)
    dy_gather = Gather(dya, 1)
    normed_gather.step(0)

    @pl.loop(1, SEQ)
    def _(j):
        giver = lax.rem(s + SEQ - j, SEQ)
        seq_copy(j, 0, wst.at[rows_at(giver, 16)], wst.at[rows_at(giver, 16)]).wait_recv()

    wbuf[rows_at(b, 256), :] = wst[...]

    @pl.loop(1, BATCH)
    def _(j):
        batch_copy(j, 0, wst, wbuf.at[rows_at(b, 256)]).start()
        batch_copy(j, 1, wd_ref, wd2.at[rows_at(b, 32)]).start()
        batch_copy(j, 2, wo_ref, wo2.at[rows_at(b, 8)]).start()

    normed_gather.step(1)

    ends = [len_ref[0]]
    for k in range(1, 4):
        ends.append(ends[-1] + len_ref[k])

    def begin_of(where):
        begin = jnp.zeros_like(where)
        for end in ends:
            begin = jnp.maximum(begin, jnp.where(where >= end, end, 0))
        return begin

    @pl.loop(0, 8)
    def _(i):
        where = i * QB + iota((QB, 128), 0)
        angle = (where - begin_of(where)).astype(F32) * rate_ref[0:1, :]
        lane = lax.rem(iota((QB, 128), 1), 64)
        sine = jnp.sin(angle)
        tabc[rows_at(i, QB), :] = jnp.where(lane < ROT, jnp.cos(angle), 1.0)
        sine = jnp.where(lane < ROT // 2, -sine, sine)
        tabs[rows_at(i, QB), :] = jnp.where(lane < ROT, sine, 0.0)

    def partner_of(part):
        lane = lax.rem(iota(part.shape, 1), 64)
        return jnp.where(lane < ROT // 2, pltpu.roll(part, 120, 1), pltpu.roll(part, 8, 1))

    normed_gather.step(2)
    normed_gather.step(3)
    dy_gather.step(0)

    @pl.loop(1, BATCH)
    def _(j):
        giver = lax.rem(b + BATCH - j, BATCH)
        batch_copy(j, 0, wbuf.at[rows_at(giver, 256)], wbuf.at[rows_at(giver, 256)]).wait_recv()
        batch_copy(j, 1, wd2.at[rows_at(giver, 32)], wd2.at[rows_at(giver, 32)]).wait_recv()
        batch_copy(j, 2, wo2.at[rows_at(giver, 8)], wo2.at[rows_at(giver, 8)]).wait_recv()

    wob[...] = wo2[...].astype(BF)

    @pl.loop(0, SEQ)
    def _(i):
        for j in range(BATCH):
            block = wbuf[pl.ds(pl.multiple_of(j * 256 + i * 16, 16), 16), :].astype(F32)
            at = pl.ds(pl.multiple_of(i * 64 + j * 8, 8), 8)
            rawu[at, :] = block[0:8, :]
            rawq[at, :] = block[8:16, :]

    def small_window(start, count):
        return rawq[start : start + count, 128:256].astype(BF)

    for k, start in enumerate((0, 72, 152, 232)):
        number = k * D + iota((D, 128), 0)
        line = (iota((D, 128), 1) + start) * 13
        hot = ((line <= number) & (number < line + 13)).astype(F32).astype(BF)
        found = dot(hot, small_window(start, 128))
        place = number - 13 * jnp.floor((number.astype(F32) + 0.5) * (1.0 / 13.0)).astype(jnp.int32)
        found = jnp.where(iota((D, 128), 1) == place + 64, found, 0.0)
        cols[:, k : k + 1] = jnp.sum(found, axis=1, keepdims=True)

    def small_row(number, start, count):
        width = number.shape[1]
        line = (iota((count, width), 0) + start) * 13
        hot = ((line <= number) & (number < line + 13)).astype(F32).astype(BF)
        found = dot_tn(small_window(start, count), hot)
        place = number - 13 * jnp.floor((number.astype(F32) + 0.5) * (1.0 / 13.0)).astype(jnp.int32)
        found = jnp.where(iota((128, width), 0) == place + 64, found, 0.0)
        return jnp.sum(found, axis=0, keepdims=True)

    lane = iota((1, 256), 1)
    number_q = 4 * D + (lane // 64) * D + s * 64 + lax.rem(lane, 64)
    bias_q = small_row(jnp.where(lane < 192, number_q, -100), 312, 448)
    bias_u = small_row(8 * D + s * HID + lane, 624, 328)
    keep = iota((128, 256), 1) < 192
    row_q, row_u = bias_q, bias_u
    for i in range(8):
        at = slice(i * 128, i * 128 + 128)
        wq = jnp.where(keep, rawq[at, :], 0.0)
        wu = rawu[at, :]
        wcat[at, 0:256] = (wq * cols[at, 0:1]).astype(BF)
        wcat[at, 256:512] = (wu * cols[at, 2:3]).astype(BF)
        row_q = row_q + jnp.sum(wq * cols[at, 1:2], axis=0, keepdims=True)
        row_u = row_u + jnp.sum(wu * cols[at, 3:4], axis=0, keepdims=True)
    brow[:, 0:256] = row_q
    brow[:, 256:512] = row_u
    wide = iota((1, D), 1)
    drow[...] = small_row(7 * D + wide, 544, 128) + small_row(12 * D + wide, 896, 128)

    normed_gather.step(4)

    @pl.loop(0, 8)
    def _(i):
        at = rows_at(i, QB)
        out = dot(nrm[at, :], wcat[...]) + brow[...]
        prj[pl.ds(i * 4, 4)] = out[:, 0:256].reshape(4, 64, 256)
        hidden = out[:, 256:512]
        share = 0.5 * (1.0 + lax.erf(hidden * (2.0**-0.5)))
        act[at, :] = (hidden * share).astype(BF)
        dge[at, :] = share + hidden * jnp.exp(-0.5 * hidden * hidden) * ((2.0 * np.pi) ** -0.5)

    dy_gather.step(1)

    @pl.loop(0, 32)
    def _(i):
        at = rows_at(i, 64)
        come = prj[inv_ref[i]]
        part = come[:, 0:128]
        part = part * tabc[at, :] + partner_of(part) * tabs[at, :]
        qs[at, :] = (part[:, 0:64].astype(BF) * 0.125).astype(BF)
        ks[at, :] = pltpu.roll(part, 64, 1)[:, 0:64].astype(BF)
        vs[at, :] = come[:, 128:192].astype(BF)

    def masked(scores, i, j):
        q_at = i * QB + iota((QB, 1), 0)
        k_at = j * QB + iota((1, QB), 1)
        allowed = (k_at >= begin_of(q_at)) & (k_at <= q_at)
        return jnp.where(allowed, scores, NEG)

    @pl.loop(0, 8)
    def _(i):
        at = rows_at(i, QB)

        def scores_step(j, top):
            scores = masked(dot_nt(qs[at, :], ks[rows_at(j, QB), :]), i, j)
            sbuf[:, rows_at(j, QB)] = scores
            return jnp.maximum(top, jnp.maximum(scores[:, 0:128], scores[:, 128:256]))

        top = lax.fori_loop(0, i + 1, scores_step, jnp.full((QB, 128), NEG, F32))
        top = jnp.max(top, axis=1, keepdims=True)

        def value_step(j, carry):
            total, summed = carry
            expos = jnp.exp(sbuf[:, rows_at(j, QB)] - top)
            summed = summed + dot(expos.astype(BF), vs[rows_at(j, QB), :])
            return total + (expos[:, 0:128] + expos[:, 128:256]), summed

        total, summed = lax.fori_loop(
            0, i + 1, value_step, (jnp.zeros((QB, 128), F32), jnp.zeros((QB, HD), F32))
        )
        total = jnp.sum(total, axis=1, keepdims=True)
        out = summed / total
        osort[pl.ds(i * 4, 4)] = out.reshape(4, 64, HD)
        stat[at, 64:65] = top + jnp.log(total)

    dy_gather.step(2)

    @pl.loop(0, 32)
    def _(j):
        ost[rows_at(j, 64), :] = osort[order_ref[j]].astype(BF)

    class Scatter:
        def __init__(self, part, sib, half, full, zed, k):
            self.part, self.sib, self.half, self.full, self.zed, self.k = part, sib, half, full, zed, k
            self.order = [(zo, xo), (zo, xr), (zo, xl), (zo, x), (z, xo), (z, xr), (z, xl), (z, x)]

        def copy(self, e, src, dst, device):
            return remote(src, dst, rs_ss.at[self.k, e], rs_rs.at[self.k, e], device)

        def chip(self, n):
            return pl.ds(pl.multiple_of((self.order[n][0] * 4 + self.order[n][1]) * 256, 256), 256)

        def at(self, n, core, low=0, count=TOK):
            zz, xx = self.order[n]
            return pl.ds(pl.multiple_of(slot(zz, xx, core) * TOK + low, 64), count)

        def out(self, e):
            part, sib, half, full = self.part, self.sib, self.half, self.full
            if e < 8:
                return part.at[self.at(e, co)], sib.at[rows_at(e, TOK)], sibling
            if e == 16:
                return part.at[self.at(3, c)], self.zed, across
            g, kind = (e - 8) // 4, (e - 8) % 4
            if kind == 0:
                return part.at[self.at(4 * g, c, 0, 64)], half.at[rows_at(2 * g, 64)], left
            if kind == 1:
                return part.at[self.at(4 * g, c, 64, 64)], half.at[rows_at(2 * g + 1, 64)], right
            if kind == 2:
                return part.at[self.at(4 * g + 1, c)], full.at[rows_at(2 * g, TOK)], right
            return part.at[self.at(4 * g + 2, c)], full.at[rows_at(2 * g + 1, TOK)], left

        def start(self, e):
            self.copy(e, *self.out(e)).start()

        def wait(self, e):
            src, dst, device = self.out(e)
            self.copy(e, dst, dst, device).wait_recv()

        def add_sibling(self, n):
            self.wait(n)
            at = self.at(n, c)
            self.part[at, :] = (
                self.part[at, :].astype(F32) + self.sib[n * TOK : n * TOK + TOK, :].astype(F32)
            ).astype(BF)

        def add_half(self, n, e, low, index):
            self.wait(e)
            at = self.at(n, c, low, 64)
            self.part[at, :] = (
                self.part[at, :].astype(F32) + self.half[index * 64 : index * 64 + 64, :].astype(F32)
            ).astype(BF)

        def full_sum(self, n, g):
            self.wait(8 + 4 * g + 2)
            self.wait(8 + 4 * g + 3)
            total = self.part[self.at(n, c), :].astype(F32)
            for index in (2 * g, 2 * g + 1):
                total = total + self.full[index * TOK : index * TOK + TOK, :].astype(F32)
            return total

        def step(self, n):
            if n == 0 or n == 3:
                g = n // 3
                self.add_sibling(4 * g)
                self.start(8 + 4 * g)
                self.start(8 + 4 * g + 1)
                self.add_sibling(4 * g + 1)
                self.add_sibling(4 * g + 2)
            elif n == 1 or n == 4:
                g = n // 4
                self.add_half(4 * g + 1, 8 + 4 * g + 1, 64, 2 * g + 1)
                self.start(8 + 4 * g + 2)
                self.add_half(4 * g + 2, 8 + 4 * g, 0, 2 * g)
                self.start(8 + 4 * g + 3)
                self.add_sibling(4 * g + 3)
            elif n == 2:
                self.part[self.at(3, c), :] = self.full_sum(3, 0).astype(BF)
                self.start(16)

        def result(self):
            total = self.full_sum(7, 1)
            self.wait(16)
            return total + self.zed[...].astype(F32)

        def drain(self):
            for e in range(17):
                self.copy(e, *self.out(e)).wait_send()

    mixed_sum = Scatter(part_m, sib_m, half_m, full_m, zed_m, 0)
    dn_sum = Scatter(part_d, sib_d, half_d, full_d, zed_d, 1)

    for n in range(8):
        at = mixed_sum.chip(n)
        part_m[at, :] = (dot(act[at, :], wd2[...]) + dot(ost[at, :], wob[...])).astype(BF)
        mixed_sum.start(n)

    dy_gather.step(3)
    mixed_sum.step(0)
    dy_gather.step(4)
    mixed_sum.step(1)

    @pl.loop(0, 8)
    def _(i):
        at = rows_at(i, QB)
        dy = dya[at, :]
        dcat[at, 256:512] = (dot_nt(dy, wd2[...]) * dge[at, :]).astype(BF)
        dost[pl.ds(i * 4, 4)] = dot_nt(dy, wob[...]).astype(BF).reshape(4, 64, HD)

    mixed_sum.step(2)
    mixed_sum.step(3)

    @pl.loop(0, 32)
    def _(i):
        dos[rows_at(i, 64), :] = dost[inv_ref[i]]

    gdacc[...] = jnp.zeros_like(gdacc)
    gtu[...] = jnp.zeros_like(gtu)

    @pl.loop(0, 4)
    def _(i):
        at = rows_at(i, 512)
        gdacc[0:256, :] += dot_tn(act[at, :], dya[at, :])
        gdacc[256:320, :] += dot_tn(ost[at, :], dya[at, :])

    gdsend[...] = gdacc[0:256, :].astype(BF)
    gosend[...] = gdacc[256:320, :]
    gdrecv[rows_at(b, 32), :] = gdsend[rows_at(b, 32), :]
    gorecv[rows_at(b, 8), :] = gosend[rows_at(b, 8), :]

    @pl.loop(1, BATCH)
    def _(j):
        peer = lax.rem(b + j, BATCH)
        batch_copy(j, 3, gdsend.at[rows_at(peer, 32)], gdrecv.at[rows_at(b, 32)]).start()
        batch_copy(j, 4, gosend.at[rows_at(peer, 8)], gorecv.at[rows_at(b, 8)]).start()

    mixed_sum.step(4)

    @pl.loop(0, 4)
    def _(i):
        at = rows_at(i, 512)
        gtu[...] += dot_tn(dcat[at, 256:512], nrm[at, :])

    mixed_ref[...] = (mixed_sum.result() + x_ref[...].astype(F32) + drow[...]).astype(BF)

    @pl.loop(0, 8)
    def _(i):
        at = rows_at(i, QB)
        stat[at, 65:66] = jnp.sum(
            dos[at, :].astype(F32) * osort[pl.ds(i * 4, 4)].reshape(QB, HD), axis=1, keepdims=True
        )
        qst[0:64, at] = qs[at, :].T
        qst[64:128, at] = dos[at, :].T

    dkt[...] = jnp.zeros_like(dkt)
    dvt[...] = jnp.zeros_like(dvt)

    @pl.loop(0, 8)
    def _(i):
        at = rows_at(i, QB)

        def step(j, dq):
            k_at = rows_at(j, QB)
            scores = masked(dot_nt(qs[at, :], ks[k_at, :]), i, j)
            probs = jnp.exp(scores - stat[at, 64:65])
            pulled = dot_nt(dos[at, :], vs[k_at, :])
            grads = (probs * (pulled - stat[at, 65:66])).astype(BF)
            dkt[:, k_at] += dot(qst[0:64, at], grads)
            dvt[:, k_at] += dot(qst[64:128, at], probs.astype(BF))
            return dq + dot(grads, ks[k_at, :])

        stat[at, 0:64] = lax.fori_loop(0, i + 1, step, jnp.zeros((QB, HD), F32)) * 0.125

    @pl.loop(0, 8)
    def _(i):
        at = rows_at(i, QB)
        both = jnp.concatenate([stat[at, 0:64], dkt[:, at].T], axis=1)
        both = both * tabc[at, :] - partner_of(both) * tabs[at, :]
        last = jnp.concatenate([dvt[:, at].T, jnp.zeros((QB, 64), F32)], axis=1)
        whole = jnp.concatenate([both, last], axis=1).astype(BF)
        dsort[pl.ds(i * 4, 4)] = whole.reshape(4, 64, 256)

    @pl.loop(0, 32)
    def _(j):
        dcat[rows_at(j, 64), 0:256] = dsort[order_ref[j]]

    for n in range(8):
        at = dn_sum.chip(n)
        part_d[at, :] = dot_nt(dcat[at, :], wcat[...]).astype(BF)
        dn_sum.start(n)
    dn_sum.step(0)

    gdacc[0:256, :] = jnp.zeros((256, D), F32)

    @pl.loop(0, 4)
    def _(i):
        at = rows_at(i, 512)
        gdacc[0:256, :] += dot_tn(dcat[at, 0:256], nrm[at, :])

    def total_step(i, total):
        return total + jnp.sum(dcat[rows_at(i, QB), :].astype(F32), axis=0, keepdims=True)

    sums = lax.fori_loop(0, 8, total_step, jnp.zeros((1, 512), F32))
    sum_q, sum_u = sums[:, 0:256], sums[:, 256:512]

    dn_sum.step(1)

    for i in range(4):
        at = slice(i * 256, i * 256 + 256)
        grad_q = gdacc[0:256, at].T
        grad_u = gtu[:, at].T
        pieces = [
            jnp.sum(grad_q * rawq[at, :], axis=1, keepdims=True),
            jnp.sum(sum_q * rawq[at, :], axis=1, keepdims=True),
            jnp.sum(grad_u * rawu[at, :], axis=1, keepdims=True),
            jnp.sum(sum_u * rawu[at, :], axis=1, keepdims=True),
        ]
        spread = jnp.zeros((256, 128), F32)
        for k in range(4):
            spread = jnp.where(iota((256, 128), 1) == k, pieces[k], spread)
        smv[:, at] = spread.T[0:8, :]
        grad_q = grad_q * cols[at, 0:1] + cols[at, 1:2] * sum_q
        grad_u = grad_u * cols[at, 2:3] + cols[at, 3:4] * sum_u
        for m in range(32):
            place = ((m % 8) * 16 + (i * 4 + m // 8)) * 16
            gsend[place : place + 16, :] = jnp.concatenate(
                [grad_u[m * 8 : m * 8 + 8, :], grad_q[m * 8 : m * 8 + 8, :]], axis=0
            ).astype(BF)

    smv[4:5, :] = jnp.sum(dy_ref[...].astype(F32), axis=0, keepdims=True)
    smv[5:6, 0:256] = sum_q
    smv[5:6, 256:512] = sum_u
    smv[5:6, 512:1024] = jnp.zeros((1, 512), F32)
    smr[rows_at(b, 8), :] = smv[...]
    grecv[rows_at(b, 256), :] = gsend[rows_at(b, 256), :]

    @pl.loop(1, BATCH)
    def _(j):
        peer = lax.rem(b + j, BATCH)
        batch_copy(j, 5, gsend.at[rows_at(peer, 256)], grecv.at[rows_at(b, 256)]).start()
        batch_copy(j, 6, smv, smr.at[rows_at(b, 8)]).start()

    dn_sum.step(2)
    dn_sum.step(3)

    @pl.loop(1, BATCH)
    def _(j):
        giver = lax.rem(b + BATCH - j, BATCH)
        batch_copy(j, 3, gdrecv.at[rows_at(giver, 32)], gdrecv.at[rows_at(giver, 32)]).wait_recv()
        batch_copy(j, 4, gorecv.at[rows_at(giver, 8)], gorecv.at[rows_at(giver, 8)]).wait_recv()

    total_d = gdrecv[0:32, :].astype(F32)
    total_o = gorecv[0:8, :]
    for k in range(1, BATCH):
        total_d = total_d + gdrecv[k * 32 : k * 32 + 32, :].astype(F32)
        total_o = total_o + gorecv[k * 8 : k * 8 + 8, :]
    gd_ref[...] = total_d
    go_ref[...] = total_o

    dn_sum.step(4)

    @pl.loop(1, BATCH)
    def _(j):
        giver = lax.rem(b + BATCH - j, BATCH)
        batch_copy(j, 5, grecv.at[rows_at(giver, 256)], grecv.at[rows_at(giver, 256)]).wait_recv()
        batch_copy(j, 6, smr.at[rows_at(giver, 8)], smr.at[rows_at(giver, 8)]).wait_recv()

    total_w = grecv[0:256, :].astype(F32)
    total_s = smr[0:8, :]
    for k in range(1, BATCH):
        total_w = total_w + grecv[k * 256 : k * 256 + 256, :].astype(F32)
        total_s = total_s + smr[k * 8 : k * 8 + 8, :]
    gsum[...] = total_w.astype(BF)
    gfin[rows_at(s, 16), :] = gsum[rows_at(s, 16), :]
    smt[...] = total_s
    sma[rows_at(s, 8), :] = total_s

    @pl.loop(1, SEQ)
    def _(j):
        peer = lax.rem(s + j, SEQ)
        seq_copy(j, 1, gsum.at[rows_at(peer, 16)], gfin.at[rows_at(s, 16)]).start()
        seq_copy(j, 2, smt, sma.at[rows_at(s, 8)]).start()

    merged = dn_sum.result()
    _, normed, inverse = normed_of()
    grad_norm = inverse * (
        merged
        - jnp.mean(merged, axis=-1, keepdims=True)
        - normed * jnp.mean(merged * normed, axis=-1, keepdims=True)
    )
    gtok_ref[...] = (dy_ref[...].astype(F32) + grad_norm).astype(BF)

    @pl.loop(1, SEQ)
    def _(j):
        giver = lax.rem(s + SEQ - j, SEQ)
        seq_copy(j, 1, gfin.at[rows_at(giver, 16)], gfin.at[rows_at(giver, 16)]).wait_recv()
        seq_copy(j, 2, sma.at[rows_at(giver, 8)], sma.at[rows_at(giver, 8)]).wait_recv()

    gw_ref[...] = gfin[...].astype(F32)
    small_ref[...] = sma[...]

    normed_gather.drain()
    dy_gather.drain()
    mixed_sum.drain()
    dn_sum.drain()

    @pl.loop(1, SEQ)
    def _(j):
        peer = lax.rem(s + j, SEQ)
        seq_copy(j, 0, ws_ref.at[rows_at(peer, 16)], wst.at[rows_at(s, 16)]).wait_send()
        seq_copy(j, 1, gsum.at[rows_at(peer, 16)], gfin.at[rows_at(s, 16)]).wait_send()
        seq_copy(j, 2, smt, sma.at[rows_at(s, 8)]).wait_send()

    @pl.loop(1, BATCH)
    def _(j):
        peer = lax.rem(b + j, BATCH)
        batch_copy(j, 0, wst, wbuf.at[rows_at(b, 256)]).wait_send()
        batch_copy(j, 1, wd_ref, wd2.at[rows_at(b, 32)]).wait_send()
        batch_copy(j, 2, wo_ref, wo2.at[rows_at(b, 8)]).wait_send()
        batch_copy(j, 3, gdsend.at[rows_at(peer, 32)], gdrecv.at[rows_at(b, 32)]).wait_send()
        batch_copy(j, 4, gosend.at[rows_at(peer, 8)], gorecv.at[rows_at(b, 8)]).wait_send()
        batch_copy(j, 5, gsend.at[rows_at(peer, 256)], grecv.at[rows_at(b, 256)]).wait_send()
        batch_copy(j, 6, smv, smr.at[rows_at(b, 8)]).wait_send()


def layer(x, dy, ws, wd, wo, rate, inv, order, lengths):
    vmem = pl.BlockSpec(memory_space=pltpu.VMEM)
    smem = pl.BlockSpec(memory_space=pltpu.SMEM)
    scratch = [
        ((ROW, D), BF), ((ROW, D), BF), ((256, 256), BF), ((2048, 256), BF),
        ((256, D), BF), ((64, D), F32), ((64, D), BF),
        ((D, 256), F32), ((D, 256), F32), ((D, 128), F32), ((D, 512), BF),
        ((1, 512), F32), ((1, D), F32),
        ((32, 64, 256), F32), ((ROW, HID), BF), ((ROW, HID), F32),
        ((ROW, 128), F32), ((ROW, 128), F32),
        ((ROW, HD), BF), ((ROW, HD), BF), ((ROW, HD), BF), ((128, ROW), BF),
        ((ROW, HD), BF), ((32, 64, HD), BF), ((32, 64, HD), F32), ((ROW, HD), BF),
        ((QB, ROW), F32), ((ROW, 512), BF), ((HD, ROW), F32), ((HD, ROW), F32),
        ((32, 64, 256), BF), ((ROW, 128), F32),
        ((ROW, D), BF), ((ROW, D), BF),
        ((8 * TOK, D), BF), ((4 * 64, D), BF), ((4 * TOK, D), BF), ((TOK, D), BF),
        ((8 * TOK, D), BF), ((4 * 64, D), BF), ((4 * TOK, D), BF), ((TOK, D), BF),
        ((320, D), F32), ((256, D), F32),
        ((256, D), BF), ((64, D), F32), ((256, D), BF), ((64, D), F32),
        ((2048, 256), BF), ((2048, 256), BF), ((256, 256), BF), ((256, 256), BF),
        ((8, D), F32), ((64, D), F32), ((8, D), F32), ((128, D), F32),
    ]
    shapes = [pltpu.VMEM(shape, dtype) for shape, dtype in scratch]
    shapes += [
        pltpu.SemaphoreType.DMA((2, 17)), pltpu.SemaphoreType.DMA((2, 17)),
        pltpu.SemaphoreType.DMA((2, 17)), pltpu.SemaphoreType.DMA((2, 17)),
        pltpu.SemaphoreType.DMA((3, SEQ)), pltpu.SemaphoreType.DMA((3, SEQ)),
        pltpu.SemaphoreType.DMA((7, BATCH)), pltpu.SemaphoreType.DMA((7, BATCH)),
    ]
    return pl.pallas_call(
        kernel,
        out_shape=(
            jax.ShapeDtypeStruct((TOK, D), BF),
            jax.ShapeDtypeStruct((TOK, D), BF),
            jax.ShapeDtypeStruct((256, 256), F32),
            jax.ShapeDtypeStruct((32, D), F32),
            jax.ShapeDtypeStruct((8, D), F32),
            jax.ShapeDtypeStruct((128, D), F32),
        ),
        in_specs=[vmem] * 6 + [smem] * 3,
        out_specs=(vmem,) * 6,
        scratch_shapes=shapes,
        compiler_params=pltpu.CompilerParams(
            collective_id=0, has_side_effects=True, vmem_limit_bytes=62 * 2**20
        ),
    )(x, dy, ws, wd, wo, rate, inv, order, lengths)


def local(tokens, doc_lengths, block_order, small_params, w_qkv, w_out, w_up, w_down, cotangent):
    place = lax.axis_index("seq") * BATCH + lax.axis_index("batch")
    up = w_up.reshape(8, SEQ, HID).transpose(1, 0, 2)
    qkv = w_qkv.reshape(8, 3, SEQ, HD).transpose(2, 0, 1, 3).reshape(SEQ, 8, 3 * HD)
    extra = jnp.pad(small_params.reshape(8, 13), ((0, 0), (0, 51)))
    extra = jnp.broadcast_to(extra[None], (SEQ, 8, 64))
    sent = jnp.concatenate([up, jnp.concatenate([qkv, extra], axis=2)], axis=1).reshape(SEQ * 16, 256)
    rates = np.float32(10000.0) ** (-2.0 * (np.arange(128) % 8).astype(np.float32) / ROT)
    rate = jnp.asarray(np.broadcast_to(rates.astype(np.float32), (8, 128)))
    index = jnp.arange(32, dtype=jnp.int32)
    inverse = jnp.sum(jnp.where(block_order[None, :] == index[:, None], index[None, :], 0), axis=1)
    mixed, grad_tokens, grad_w, grad_down, grad_out, small = layer(
        tokens[0], cotangent[0], sent, w_down, w_out.astype(F32), rate,
        inverse.astype(jnp.int32), block_order, doc_lengths[0],
    )
    grad_w = grad_w.reshape(SEQ, 2, 8, 256)
    grad_up = grad_w[:, 0].transpose(1, 0, 2).reshape(8, SEQ * HID)
    grad_qkv = grad_w[:, 1, :, : 3 * HD].reshape(SEQ, 8, 3, HD)
    grad_qkv = grad_qkv.transpose(1, 2, 0, 3).reshape(8, 3 * D)
    small = small.reshape(SEQ, 8, D)
    lines = jnp.sum(small[:, 0:5], axis=0)
    bias_qkv = small[:, 5, : 3 * HD].reshape(SEQ, 3, HD).transpose(1, 0, 2).reshape(-1)
    bias_up = small[:, 5, 256:512].reshape(-1)
    grad_small = jnp.concatenate(
        [lines[0], lines[1], lines[2], lines[3], bias_qkv, lines[4], bias_up, lines[4]]
    )
    grad_small = lax.dynamic_slice_in_dim(grad_small, place * PER, PER)
    return (mixed[None], grad_tokens[None], grad_small, grad_qkv, grad_out, grad_up, grad_down)


def solution(mesh):
    placed = (
        P("batch", "seq", None),
        P("batch", None),
        P(),
        P(("seq", "batch")),
        P(("seq", "batch"), None),
        P(("seq", "batch"), None),
        P(("seq", "batch"), None),
        P(("seq", "batch"), None),
        P("batch", "seq", None),
    )
    return jax.shard_map(
        local,
        mesh=mesh,
        in_specs=placed,
        out_specs=(
            P("batch", "seq", None),
            P("batch", "seq", None),
            P(("seq", "batch")),
            P(("seq", "batch"), None),
            P(("seq", "batch"), None),
            P(("seq", "batch"), None),
            P(("seq", "batch"), None),
        ),
        check_vma=False,
    )
```

time: 1220 us -> 181 us (0.15)
  waiting for transfers between devices: 713 us -> 0 us
  Pallas kernels: 0 us -> 164 us
  matrix products: 140 us -> 0 us
  blocking collectives: 131 us -> 0 us
  local copies, waits for them, and re-layouts: 141 us -> 10.5 us
  other arithmetic: 50.1 us -> 3.08 us
  between operations: 15.5 us -> 0.8 us
    all_gather x3 -> x0, waiting for transfers between devices: 480 us -> none  [the longest x2 318 us: side_by_side(): lax.all_gather(both, axis, axis=dim, tiled=True)]
    reduce_scatter x4 -> x0, waiting for transfers between devices: 228 us -> none  [the longest x1 104 us: local(): lax.psum_scatter(grad_down.astype(jnp.bfloat16), 'seq', scatter_dimension...]
    pallas_call x0 -> x1, Pallas kernels: none -> 164 us  [layer(): pl.pallas_call(kernel, out_shape=(jax.ShapeDtypeStruct((TOK, D), BF), jax...]
    dot_general x48 -> x0, matrix products: 140 us -> none  [the longest x12 25.1 us: scores_of(): jnp.einsum('qhd,khd->hqk', query, key_block, preferred_element_type=jnp.f...]
    unnamed x2 -> x0, blocking collectives: 131 us -> none
    another operation x10 -> x3, local copies, waits for them, and re-layouts: 45.5 us -> 0.81 us  [the longest x2 27.1 us: laid_out(): return jnp.moveaxis(pieces, 0, dim).reshape(shape)]
    all_gather x1 -> x0, local copies, waits for them, and re-layouts: 20.5 us -> none  [gather_together(): lines, at, done = (lax.all_gather(flat, axis), 0, [])]
    concatenate x7 -> x2, other arithmetic: 20.4 us -> 0.76 us  [the longest x1 0.68 us: local(): jnp.concatenate([up, jnp.concatenate([qkv, extra], axis=2)], axis=1)]
  transfers between devices with their start and end apart: 10 -> 0, of which waited for: 8 -> 0; matrix products, arithmetic and copies ran while one was open for 26% -> 0% of each run, Pallas kernels for 0% -> 0%
where the time goes in v1:
time: 181 us; the launch traced here: 178 us
  Pallas kernels  164 us (91%)
  local copies, waits for them, and re-layouts  10.5 us (6%)
  other arithmetic  3.08 us (2%)
    pallas_call x1, Pallas kernels, layer(): pl.pallas_call(kernel, out_shape=(jax.ShapeDtypeStruct((TOK, D), BF), jax...  164 us
    unnamed x33, local copies, waits for them, and re-layouts  4.38 us

profile of v1, /device:TPU:1, one launch (start us, length us, event | category | flops | bytes accessed | tf_op | source)
XLA Modules:
  0.0 178.1 jit_solution(11005067658842083079)
XLA Ops:
  0.6 0.9 reshape.47
  1.6 0.1 copy.36
  1.6 0.0 copy-start.7
  1.6 0.0 copy-start.4
  1.7 0.1 reshape.48
  1.8 0.5 copy-done.7
  2.3 0.1 reshape.49
  2.4 0.1 fusion.2
  2.5 0.0 copy-done.4
  2.5 0.0 copy-start.6
  2.5 0.7 maximum_maximum_fusion
  3.2 0.0 copy-done.6
  3.2 0.0 copy-start.9
  3.2 0.6 convert_element_type.5.wo_ref
  3.8 0.0 copy-done.9
  3.9 0.6 select_reduce_fusion.inv_ref
  4.5 0.0 copy-start.8
  4.5 0.7 copy-done.8
  5.1 0.6 jit_solution_.3.rate_ref
  5.7 163.8 %shard_map.153 = (bf16[128,1024]{1,0:T(8,128)(2,1)}, bf16[128,1024]{1,0:T(8,128)(2,1)}, f32[256,256]{1,0:T(8,128)}, f32[32,1024]{1,0:T(8,128)}, f32[8,1024]{1,0:T(8,128)}, /*index=5*/f32[128,1024]{1,0:T(8,128)}) custom-call(bf16[128,1024]{1,0:T(8,128)(2,1)} %bitcast.43, bf16[128,1024]{1,0:T(8,128)(2,1)} %bitcast.44, bf16[256,256]{1,0:T(8,128)(2,1)} %bitcast.42, ...), custom_call_target="tpu_custom_call" | custom-call | tf_op jit(solution)/shard_map/pallas_call | solution.py:697
  169.5 1.1 slice_reduce_fusion
  170.6 0.0 copy-start.2
  170.7 0.9 slice.46
  171.6 0.1 reshape_squeeze.9
  171.7 0.1 reshape.52
  171.8 0.9 slice.48
  172.8 0.6 dynamic_slice.3
  173.4 0.0 copy-done.2
  173.4 0.1 reshape_squeeze.11
  173.5 0.1 copy.32
  173.6 0.0 copy-start.1
  173.6 0.8 reshape.54
  174.4 0.7 slice.50
  175.1 0.0 copy-done.1
  175.1 0.0 copy-start
  175.1 0.7 copy.48
  175.8 0.3 copy-done
  176.1 0.0 copy-start.5
  176.1 0.0 copy-start.3
  176.1 0.7 copy.49
  176.8 0.1 copy-done.5
  176.9 0.6 copy.50
  177.5 0.0 copy-done.3
  177.5 0.7 copy.51
  (12 shorter events, 0.1 us)
Async XLA Ops:
  1.6 0.7 copy-start.7
  1.6 0.8 copy-start.4
  2.5 0.7 copy-start.6
  3.2 0.7 copy-start.9
  4.5 0.7 copy-start.8
  170.6 2.7 %copy-start.2 = (f32[256,256]{1,0:T(8,128)S(1)}, f32[256,256]{1,0:T(8,128)}, u32[]{:S(2)}) copy-start(f32[256,256]{1,0:T(8,128)} %get-tuple-element.16) | copy-start | bytes 786436
  173.6 1.4 copy-start.1
  175.1 1.0 copy-start
  176.1 0.8 copy-start.5
  176.1 1.4 copy-start.3

commit v2 on v1

v2 whole, which is shorter than its diff:
```python
import jax
import jax.numpy as jnp
import numpy as np
from jax import lax
from jax.experimental import pallas as pl
from jax.experimental.pallas import tpu as pltpu
from jax.sharding import PartitionSpec as P

HD = 64
ROT = 16
EPS = 1e-05
NEG = -1e30
MESH = pl.DeviceIdType.MESH
BF = jnp.bfloat16
F32 = jnp.float32

SEQ = 16
BATCH = 8
TOK = 128
ROW = SEQ * TOK
D = 1024
HID = 256
PER = 104
QB = 256
AB = 512


def dot(a, b):
    return lax.dot_general(a, b, (((1,), (0,)), ((), ())), preferred_element_type=F32)


def dot_nt(a, b):
    return lax.dot_general(a, b, (((1,), (1,)), ((), ())), preferred_element_type=F32)


def dot_tn(a, b):
    return lax.dot_general(a, b, (((0,), (0,)), ((), ())), preferred_element_type=F32)


def iota(shape, dim):
    return lax.broadcasted_iota(jnp.int32, shape, dim)


def slot(z, x, c):
    return z * 8 + x * 2 + c


def rows_at(index, count):
    return pl.ds(pl.multiple_of(index * count, count), count)


def kernel(
    x_ref, dy_ref, wq_ref, wo_ref, wu_ref, wd_ref, sp_ref, order_ref, len_ref,
    mixed_ref, gtok_ref, gu_ref, gq_ref, gd_ref, go_ref, small_ref,
    nrm, dya, wsend, wst, wbuf, wd2, wos, wo2, wob, rawq, rawu, cols, wcat, brow, drow,
    prj, act, dge, tabc, tabs, qa, ka, va, kat, vat, qat, doa, doat, dost, osort, ost,
    dcat, dkt, dvt, dsort, dqs,
    part, sib_m, half_m, full_m, zed_m, sib_d, half_d, full_d, zed_d,
    gdacc, gtu, gdsend, gosend, gdrecv, gorecv,
    gusend, gurecv, gusum, gufin, gqsend, gqrecv, gqsum, gqfin,
    flat, fsend, frecv, fsum, fall,
    inv_ref, ag_ss, ag_rs, rs_ss, rs_rs, sq_ss, sq_rs, bt_ss, bt_rs,
):
    s = lax.axis_index("seq")
    b = lax.axis_index("batch")
    z, x, c = s // 8, lax.rem(s // 2, 4), lax.rem(s, 2)
    xr, xl, xo = lax.rem(x + 1, 4), lax.rem(x + 3, 4), lax.rem(x + 2, 4)
    zo, co = 1 - z, 1 - c
    right, left = (slot(z, xr, c), b), (slot(z, xl, c), b)
    across, sibling = (slot(zo, x, c), b), (slot(z, x, co), b)

    def remote(src, dst, send, recv, device):
        return pltpu.make_async_remote_copy(
            src_ref=src, dst_ref=dst, send_sem=send, recv_sem=recv,
            device_id=device, device_id_type=MESH,
        )

    barrier = pltpu.get_barrier_semaphore()

    @pl.loop(1, SEQ)
    def _(j):
        pl.semaphore_signal(barrier, inc=1, device_id=(lax.rem(s + j, SEQ), b), device_id_type=MESH)

    @pl.loop(1, BATCH)
    def _(j):
        pl.semaphore_signal(barrier, inc=1, device_id=(s, lax.rem(b + j, BATCH)), device_id_type=MESH)

    def normed_of():
        inputs = x_ref[...].astype(F32)
        centred = inputs - jnp.mean(inputs, axis=-1, keepdims=True)
        inverse = lax.rsqrt(jnp.mean(centred * centred, axis=-1, keepdims=True) + EPS)
        return inputs, centred * inverse, inverse

    nrm[rows_at(s, TOK), :] = normed_of()[1].astype(BF)
    dya[rows_at(s, TOK), :] = dy_ref[...]

    def pair(one, two):
        return jnp.where(iota((8, 128), 1) < 64, one, two)

    small = jnp.concatenate([sp_ref[...].astype(F32), jnp.zeros((1, 128 - PER), F32)], axis=1)
    extra = jnp.where(
        iota((8, 128), 0) == 0, pltpu.roll(small, 64, 1), jnp.where(iota((8, 128), 0) == 1, small, 0.0)
    )
    wide_q = wq_ref[...].astype(F32)
    wide_u = wu_ref[...].astype(F32)
    for k in range(SEQ):
        at = slice(k // 2 * 128, k // 2 * 128 + 128)
        q, kk, v = (wide_q[:, n * D : n * D + D][:, at] for n in range(3))
        turned = [pltpu.roll(part_of, 64, 1) for part_of in (q, kk, v)]
        q, kk, v = (q, turned[1], v) if k % 2 == 0 else (turned[0], kk, turned[2])
        low = jnp.concatenate([pair(q, kk), pair(v, extra)], axis=1)
        block = jnp.concatenate([wide_u[:, k * HID : k * HID + HID], low], axis=0)
        wsend[k * 16 : k * 16 + 16, :] = block.astype(BF)

    wst[rows_at(s, 16), :] = wsend[rows_at(s, 16), :]
    wos[...] = wo_ref[...].astype(F32)
    wd2[rows_at(b, 32), :] = wd_ref[...]
    wo2[rows_at(b, 8), :] = wos[...]

    @pl.loop(0, 32)
    def _(i):
        place = jnp.int32(0)
        for j in range(32):
            place = place + jnp.where(order_ref[j] == i, j, 0)
        inv_ref[i] = jnp.minimum(place, 31)

    pl.semaphore_wait(barrier, SEQ - 1 + BATCH - 1)

    def seq_copy(j, k, src, dst):
        return remote(src, dst, sq_ss.at[k, j], sq_rs.at[k, j], (lax.rem(s + j, SEQ), b))

    def batch_copy(j, k, src, dst):
        return remote(src, dst, bt_ss.at[k, j], bt_rs.at[k, j], (s, lax.rem(b + j, BATCH)))

    @pl.loop(1, SEQ)
    def _(j):
        peer = lax.rem(s + j, SEQ)
        seq_copy(j, 0, wsend.at[rows_at(peer, 16)], wst.at[rows_at(s, 16)]).start()

    class Gather:
        def __init__(self, buf, k):
            self.buf, self.k = buf, k

        def copy(self, e, index, device, low=0, count=TOK):
            at = self.buf.at[pl.ds(pl.multiple_of(index * TOK + low, 64), count)]
            return remote(at, at, ag_ss.at[self.k, e], ag_rs.at[self.k, e], device)

        def sends(self):
            own, far = s, slot(zo, x, c)
            return {
                0: (own, right, 0, TOK), 1: (own, left, 0, TOK),
                2: (own, across, 0, TOK), 3: (own, sibling, 0, TOK),
                4: (far, right, 0, TOK), 5: (far, left, 0, TOK), 6: (far, sibling, 0, TOK),
                7: (slot(z, xl, c), right, 0, 64), 8: (slot(z, xr, c), left, 64, 64),
                9: (slot(z, xl, c), sibling, 0, TOK), 10: (slot(z, xr, c), sibling, 0, TOK),
                11: (slot(zo, xl, c), right, 0, 64), 12: (slot(zo, xr, c), left, 64, 64),
                13: (slot(zo, xl, c), sibling, 0, TOK), 14: (slot(zo, xr, c), sibling, 0, TOK),
                15: (slot(z, xo, c), sibling, 0, TOK), 16: (slot(zo, xo, c), sibling, 0, TOK),
            }

        def receives(self):
            return {
                0: (slot(z, xl, c), 0, TOK), 1: (slot(z, xr, c), 0, TOK),
                2: (slot(zo, x, c), 0, TOK), 3: (slot(z, x, co), 0, TOK),
                4: (slot(zo, xl, c), 0, TOK), 5: (slot(zo, xr, c), 0, TOK), 6: (slot(zo, x, co), 0, TOK),
                7: (slot(z, xo, c), 0, 64), 8: (slot(z, xo, c), 64, 64),
                9: (slot(z, xl, co), 0, TOK), 10: (slot(z, xr, co), 0, TOK),
                11: (slot(zo, xo, c), 0, 64), 12: (slot(zo, xo, c), 64, 64),
                13: (slot(zo, xl, co), 0, TOK), 14: (slot(zo, xr, co), 0, TOK),
                15: (slot(z, xo, co), 0, TOK), 16: (slot(zo, xo, co), 0, TOK),
            }

        def start(self, *events):
            for e in events:
                index, device, low, count = self.sends()[e]
                self.copy(e, index, device, low, count).start()

        def wait(self, *events):
            for e in events:
                index, low, count = self.receives()[e]
                self.copy(e, index, right, low, count).wait_recv()

        def step(self, n):
            if n == 0:
                self.start(0, 1, 2, 3)
            elif n == 1:
                self.wait(2)
                self.start(4, 5, 6)
                self.wait(0)
                self.start(7, 9)
                self.wait(1)
                self.start(8, 10)
            elif n == 2:
                self.wait(4)
                self.start(11, 13)
                self.wait(5)
                self.start(12, 14)
            elif n == 3:
                self.wait(7, 8)
                self.start(15)
                self.wait(11, 12)
                self.start(16)
            else:
                self.wait(3, 6, 9, 10, 13, 14, 15, 16)

        def drain(self):
            for e, (index, device, low, count) in self.sends().items():
                self.copy(e, index, device, low, count).wait_send()

    normed_gather = Gather(nrm, 0)
    dy_gather = Gather(dya, 1)
    normed_gather.step(0)

    ends = [len_ref[0, 0]]
    for k in range(1, 4):
        ends.append(ends[-1] + len_ref[0, k])

    def begin_of(where):
        begin = jnp.zeros_like(where)
        for end in ends:
            begin = jnp.maximum(begin, jnp.where(where >= end, end, 0))
        return begin

    def doc_of(where):
        doc = jnp.zeros_like(where)
        for end in ends:
            doc = doc + jnp.where(where >= end, 1, 0)
        return doc

    def partner_of(part):
        lane = lax.rem(iota(part.shape, 1), 64)
        return jnp.where(lane < ROT // 2, pltpu.roll(part, 120, 1), pltpu.roll(part, 8, 1))

    rate = jnp.zeros((1, 128), F32)
    for k in range(ROT // 2):
        value = float(np.float32(10000.0) ** np.float32(-2.0 * k / ROT))
        rate = jnp.where(lax.rem(iota((1, 128), 1), 8) == k, value, rate)

    @pl.loop(1, SEQ)
    def _(j):
        giver = lax.rem(s + SEQ - j, SEQ)
        seq_copy(j, 0, wst.at[rows_at(giver, 16)], wst.at[rows_at(giver, 16)]).wait_recv()

    wbuf[rows_at(b, 256), :] = wst[...]

    @pl.loop(1, BATCH)
    def _(j):
        batch_copy(j, 0, wst, wbuf.at[rows_at(b, 256)]).start()

    @pl.loop(0, 8)
    def _(i):
        where = i * QB + iota((QB, 128), 0)
        angle = (where - begin_of(where)).astype(F32) * rate
        lane = lax.rem(iota((QB, 128), 1), 64)
        sine = jnp.sin(angle)
        tabc[rows_at(i, QB), :] = jnp.where(lane < ROT, jnp.cos(angle), 1.0)
        sine = jnp.where(lane < ROT // 2, -sine, sine)
        tabs[rows_at(i, QB), :] = jnp.where(lane < ROT, sine, 0.0)

    normed_gather.step(1)

    @pl.loop(1, BATCH)
    def _(j):
        batch_copy(j, 1, wd_ref, wd2.at[rows_at(b, 32)]).start()
        batch_copy(j, 2, wos, wo2.at[rows_at(b, 8)]).start()

    normed_gather.step(2)
    normed_gather.step(3)
    dy_gather.step(0)

    @pl.loop(1, BATCH)
    def _(j):
        giver = lax.rem(b + BATCH - j, BATCH)
        batch_copy(j, 0, wbuf.at[rows_at(giver, 256)], wbuf.at[rows_at(giver, 256)]).wait_recv()

    @pl.loop(0, SEQ)
    def _(i):
        for j in range(BATCH):
            block = wbuf[pl.ds(pl.multiple_of(j * 256 + i * 16, 16), 16), :].astype(F32)
            at = pl.ds(pl.multiple_of(i * 64 + j * 8, 8), 8)
            rawu[at, :] = block[0:8, :]
            rawq[at, :] = block[8:16, :]

    def small_window(start, count):
        return rawq[start : start + count, 128:256].astype(BF)

    def hot_of(line, number):
        low = (line // 8) * PER + lax.rem(line, 8) * 64
        high = jnp.where(lax.rem(line, 8) == 0, low + 64, low + PER - 64)
        high = jnp.where(lax.rem(line, 8) < 2, high, low)
        return ((low <= number) & (number < high)).astype(F32).astype(BF)

    def place_of(number):
        owner = jnp.floor((number.astype(F32) + 0.5) * (1.0 / PER)).astype(jnp.int32)
        place = number - PER * owner
        return 64 + jnp.where(place >= 64, place - 64, place)

    for k, start in enumerate((0, 72, 152, 232)):
        number = k * D + iota((D, 128), 0)
        found = dot(hot_of(iota((1, 128), 1) + start, number), small_window(start, 128))
        found = jnp.where(iota((D, 128), 1) == place_of(number), found, 0.0)
        cols[:, k : k + 1] = jnp.sum(found, axis=1, keepdims=True)

    def small_row(number, start, count):
        found = dot_tn(small_window(start, count), hot_of(iota((count, 1), 0) + start, number))
        found = jnp.where(iota((128, number.shape[1]), 0) == place_of(number), found, 0.0)
        return jnp.sum(found, axis=0, keepdims=True)

    lane = iota((1, 256), 1)
    number_q = 4 * D + (lane // 64) * D + s * 64 + lax.rem(lane, 64)
    bias_q = small_row(jnp.where(lane < 192, number_q, -1000), 312, 240)
    bias_u = small_row(8 * D + s * HID + lane, 624, 328)
    keep = iota((128, 256), 1) < 192
    row_q, row_u = bias_q, bias_u
    for i in range(8):
        at = slice(i * 128, i * 128 + 128)
        wq = jnp.where(keep, rawq[at, :], 0.0)
        wu = rawu[at, :]
        wcat[at, 0:256] = (wq * cols[at, 0:1]).astype(BF)
        wcat[at, 256:512] = (wu * cols[at, 2:3]).astype(BF)
        row_q = row_q + jnp.sum(wq * cols[at, 1:2], axis=0, keepdims=True)
        row_u = row_u + jnp.sum(wu * cols[at, 3:4], axis=0, keepdims=True)
    brow[:, 0:256] = row_q
    brow[:, 256:512] = row_u
    wide = iota((1, D), 1)
    drow[...] = small_row(7 * D + wide, 544, 128) + small_row(12 * D + wide, 896, 128)

    normed_gather.step(4)

    @pl.loop(0, 8)
    def _(i):
        at = rows_at(i, QB)
        out = dot(nrm[at, :], wcat[:, 0:256]) + brow[:, 0:256]
        prj[pl.ds(i * 4, 4)] = out.reshape(4, 64, 256)

    dy_gather.step(1)

    def pieces_of(value):
        high = value.astype(BF).astype(F32)
        mid = (value - high).astype(BF).astype(F32)
        return high, mid, value - high - mid

    def with_lanes(base, first, values):
        lane = iota(base.shape, 1)
        for k, value in enumerate(values):
            base = jnp.where(lane == first + k, value, base)
        return base

    @pl.loop(0, 32)
    def _(i):
        at = rows_at(i, 64)
        come = prj[inv_ref[i]]
        both = come[:, 0:128]
        both = both * tabc[at, :] + partner_of(both) * tabs[at, :]
        lane = iota((64, 128), 1)
        own = doc_of(i * 64 + iota((64, 1), 0)) == lane - 64
        front = lane < 64
        qa[at, :] = jnp.where(front, both * 0.125, jnp.where(own | (lane >= 68), 0.0, NEG)).astype(BF)
        tail = jnp.where(lane < 68, own.astype(F32), (lane < 71).astype(F32))
        ka[at, :] = jnp.where(front, pltpu.roll(both, 64, 1), tail).astype(BF)
        va[at, :] = jnp.where(front, come[:, 128:256], (lane < 67).astype(F32)).astype(BF)

    @pl.loop(0, 8)
    def _(i):
        at = rows_at(i, QB)
        kat[:, at] = ka[at, :].T
        vat[:, at] = va[at, :].T
        qat[:, at] = qa[at, :].T[0:64, :]

    lower = iota((AB, AB), 1) <= iota((AB, AB), 0)

    @pl.loop(0, ROW // AB)
    def _(i):
        at = rows_at(i, AB)

        def step(j, carry, masked):
            top, total = carry
            k_at = rows_at(j, AB)
            scores = dot(qa[at, :], kat[:, k_at])
            if masked:
                scores = jnp.where(lower, scores, NEG)
            peak = jnp.maximum(top, jnp.max(scores, axis=1, keepdims=True))
            expos = jnp.exp(scores - peak).astype(BF)
            return peak, total * jnp.exp(top - peak) + dot(expos, va[k_at, :])

        start = (jnp.full((AB, 1), NEG, F32), jnp.zeros((AB, 128), F32))
        carry = lax.fori_loop(0, i, lambda j, carry: step(j, carry, False), start)
        top, total = step(i, carry, True)
        norm = total[:, 64:65]
        osort[pl.ds(i * (AB // 64), AB // 64)] = (total / norm)[:, 0:64].reshape(AB // 64, 64, HD)
        qa[at, :] = with_lanes(qa[at, :].astype(F32), 68, pieces_of(-(top + jnp.log(norm)))).astype(BF)

    dy_gather.step(2)

    @pl.loop(0, 8)
    def _(i):
        at = rows_at(i, QB)
        hidden = dot(nrm[at, :], wcat[:, 256:512]) + brow[:, 256:512]
        share = 0.5 * (1.0 + lax.erf(hidden * (2.0**-0.5)))
        act[at, :] = (hidden * share).astype(BF)
        dge[at, :] = share + hidden * jnp.exp(-0.5 * hidden * hidden) * ((2.0 * np.pi) ** -0.5)

    dy_gather.step(3)

    @pl.loop(0, 32)
    def _(j):
        ost[rows_at(j, 64), :] = osort[order_ref[j]].astype(BF)

    @pl.loop(1, BATCH)
    def _(j):
        giver = lax.rem(b + BATCH - j, BATCH)
        batch_copy(j, 1, wd2.at[rows_at(giver, 32)], wd2.at[rows_at(giver, 32)]).wait_recv()
        batch_copy(j, 2, wo2.at[rows_at(giver, 8)], wo2.at[rows_at(giver, 8)]).wait_recv()

    wob[...] = wo2[...].astype(BF)

    class Scatter:
        def __init__(self, part, sib, half, full, zed, k):
            self.part, self.sib, self.half, self.full, self.zed, self.k = part, sib, half, full, zed, k
            self.order = [(zo, xo), (zo, xr), (zo, xl), (zo, x), (z, xo), (z, xr), (z, xl), (z, x)]

        def copy(self, e, src, dst, device):
            return remote(src, dst, rs_ss.at[self.k, e], rs_rs.at[self.k, e], device)

        def chip(self, n):
            return pl.ds(pl.multiple_of((self.order[n][0] * 4 + self.order[n][1]) * 256, 256), 256)

        def at(self, n, core, low=0, count=TOK):
            zz, xx = self.order[n]
            return pl.ds(pl.multiple_of(slot(zz, xx, core) * TOK + low, 64), count)

        def out(self, e):
            part, sib, half, full = self.part, self.sib, self.half, self.full
            if e < 8:
                return part.at[self.at(e, co)], sib.at[rows_at(e, TOK)], sibling
            if e == 16:
                return part.at[self.at(3, c)], self.zed, across
            g, kind = (e - 8) // 4, (e - 8) % 4
            if kind == 0:
                return part.at[self.at(4 * g, c, 0, 64)], half.at[rows_at(2 * g, 64)], left
            if kind == 1:
                return part.at[self.at(4 * g, c, 64, 64)], half.at[rows_at(2 * g + 1, 64)], right
            if kind == 2:
                return part.at[self.at(4 * g + 1, c)], full.at[rows_at(2 * g, TOK)], right
            return part.at[self.at(4 * g + 2, c)], full.at[rows_at(2 * g + 1, TOK)], left

        def start(self, e):
            self.copy(e, *self.out(e)).start()

        def wait(self, e):
            src, dst, device = self.out(e)
            self.copy(e, dst, dst, device).wait_recv()

        def add_sibling(self, n):
            self.wait(n)
            at = self.at(n, c)
            self.part[at, :] = (
                self.part[at, :].astype(F32) + self.sib[n * TOK : n * TOK + TOK, :].astype(F32)
            ).astype(BF)

        def add_half(self, n, e, low, index):
            self.wait(e)
            at = self.at(n, c, low, 64)
            self.part[at, :] = (
                self.part[at, :].astype(F32) + self.half[index * 64 : index * 64 + 64, :].astype(F32)
            ).astype(BF)

        def full_sum(self, n, g):
            self.wait(8 + 4 * g + 2)
            self.wait(8 + 4 * g + 3)
            total = self.part[self.at(n, c), :].astype(F32)
            for index in (2 * g, 2 * g + 1):
                total = total + self.full[index * TOK : index * TOK + TOK, :].astype(F32)
            return total

        def step(self, n):
            if n == 0 or n == 3:
                g = n // 3
                self.add_sibling(4 * g)
                self.start(8 + 4 * g)
                self.start(8 + 4 * g + 1)
                self.add_sibling(4 * g + 1)
                self.add_sibling(4 * g + 2)
            elif n == 1 or n == 4:
                g = n // 4
                self.add_half(4 * g + 1, 8 + 4 * g + 1, 64, 2 * g + 1)
                self.start(8 + 4 * g + 2)
                self.add_half(4 * g + 2, 8 + 4 * g, 0, 2 * g)
                self.start(8 + 4 * g + 3)
                self.add_sibling(4 * g + 3)
            elif n == 2:
                self.part[self.at(3, c), :] = self.full_sum(3, 0).astype(BF)
                self.start(16)

        def result(self):
            total = self.full_sum(7, 1)
            self.wait(16)
            return total + self.zed[...].astype(F32)

        def drain(self):
            for e in range(17):
                self.copy(e, *self.out(e)).wait_send()

    mixed_sum = Scatter(part, sib_m, half_m, full_m, zed_m, 0)
    dn_sum = Scatter(part, sib_d, half_d, full_d, zed_d, 1)

    for n in range(8):
        at = mixed_sum.chip(n)
        part[at, :] = (dot(act[at, :], wd2[...]) + dot(ost[at, :], wob[...])).astype(BF)
        mixed_sum.start(n)

    mixed_sum.step(0)
    dy_gather.step(4)

    @pl.loop(0, 8)
    def _(i):
        at = rows_at(i, QB)
        dy = dya[at, :]
        dcat[at, 256:512] = (dot_nt(dy, wd2[...]) * dge[at, :]).astype(BF)
        dost[pl.ds(i * 4, 4)] = dot_nt(dy, wob[...]).astype(BF).reshape(4, 64, HD)

    mixed_sum.step(1)
    mixed_sum.step(3)

    gdacc[...] = jnp.zeros_like(gdacc)

    @pl.loop(0, 4)
    def _(i):
        at = rows_at(i, 512)
        gdacc[0:256, :] += dot_tn(act[at, :], dya[at, :])
        gdacc[256:320, :] += dot_tn(ost[at, :], dya[at, :])

    gdsend[...] = gdacc[0:256, :].astype(BF)
    gosend[...] = gdacc[256:320, :]
    gdrecv[rows_at(b, 32), :] = gdsend[rows_at(b, 32), :]
    gorecv[rows_at(b, 8), :] = gosend[rows_at(b, 8), :]

    @pl.loop(1, BATCH)
    def _(j):
        peer = lax.rem(b + j, BATCH)
        batch_copy(j, 3, gdsend.at[rows_at(peer, 32)], gdrecv.at[rows_at(b, 32)]).start()
        batch_copy(j, 4, gosend.at[rows_at(peer, 8)], gorecv.at[rows_at(b, 8)]).start()

    mixed_sum.step(2)
    mixed_sum.step(4)

    gtu[...] = jnp.zeros_like(gtu)

    @pl.loop(0, 4)
    def _(i):
        at = rows_at(i, 512)
        gtu[...] += dot_tn(dcat[at, 256:512], nrm[at, :])

    def column_sum(low):
        def add(i, total):
            return total + jnp.sum(dcat[rows_at(i, QB), low : low + 256].astype(F32), axis=0, keepdims=True)

        return lax.fori_loop(0, 8, add, jnp.zeros((1, 256), F32))

    def to_flat(line, values):
        for k in range(values.shape[1] // 128):
            flat[line + k : line + k + 1, :] = values[:, k * 128 : k * 128 + 128]

    def hand_out(gt, raw, sums, k, send, recv, copy_k):
        for i in range(4):
            at = slice(i * 256, i * 256 + 256)
            grad = gt[0:256, at].T
            gain = jnp.sum(grad * raw[at, :], axis=1, keepdims=True)
            shift = jnp.sum(sums * raw[at, :], axis=1, keepdims=True)
            lane = iota((256, 128), 1)
            spread = jnp.where(lane == 0, gain, jnp.where(lane == 1, shift, 0.0)).T
            to_flat(k * 8 + i * 2, spread[0:1, :])
            to_flat(k * 8 + 8 + i * 2, spread[1:2, :])
            grad = grad * cols[at, k : k + 1] + cols[at, k + 1 : k + 2] * sums
            for m in range(8):
                for h in range(2):
                    place = m * 128 + i * 32 + h * 16
                    first, second = (h * 2) * 64 + m * 8, (h * 2 + 1) * 64 + m * 8
                    send[place : place + 16, :] = jnp.concatenate(
                        [grad[first : first + 8, :], grad[second : second + 8, :]], axis=0
                    ).astype(BF)
        recv[rows_at(b, 128), :] = send[rows_at(b, 128), :]

        @pl.loop(1, BATCH)
        def _(j):
            peer = lax.rem(b + j, BATCH)
            batch_copy(j, copy_k, send.at[rows_at(peer, 128)], recv.at[rows_at(b, 128)]).start()

    def sum_rows(recv, total_ref, final, copy_k, seq_k):
        @pl.loop(1, BATCH)
        def _(j):
            giver = lax.rem(b + BATCH - j, BATCH)
            batch_copy(j, copy_k, recv.at[rows_at(giver, 128)], recv.at[rows_at(giver, 128)]).wait_recv()

        total = recv[0:128, :].astype(F32)
        for k in range(1, BATCH):
            total = total + recv[k * 128 : k * 128 + 128, :].astype(F32)
        total_ref[...] = total
        final[rows_at(s, 8), :] = total_ref[rows_at(s, 8), :]

        @pl.loop(1, SEQ)
        def _(j):
            peer = lax.rem(s + j, SEQ)
            seq_copy(j, seq_k, total_ref.at[rows_at(peer, 8)], final.at[rows_at(s, 8)]).start()

    sum_u = column_sum(256)
    hand_out(gtu, rawu, sum_u, 2, gusend, gurecv, 5)

    @pl.loop(0, 8)
    def _(i):
        at = rows_at(i, QB)
        come = [dost[inv_ref[i * 4 + k]] for k in range(4)]
        grads = jnp.concatenate(come, axis=0).astype(F32)
        past = osort[pl.ds(i * 4, 4)].reshape(QB, HD)
        delta = jnp.sum(grads * past, axis=1, keepdims=True)
        wide = jnp.concatenate([grads, jnp.zeros((QB, 64), F32)], axis=1)
        wide = with_lanes(wide, 64, pieces_of(-delta)).astype(BF)
        doa[at, :] = wide
        doat[:, at] = wide.T[0:64, :]

    dkt[...] = jnp.zeros_like(dkt)
    dvt[...] = jnp.zeros_like(dvt)
    mixed_ref[...] = (mixed_sum.result() + x_ref[...].astype(F32) + drow[...]).astype(BF)

    @pl.loop(0, ROW // AB)
    def _(i):
        at = rows_at(i, AB)

        def step(j, dq, masked):
            k_at = rows_at(j, AB)
            probs = jnp.exp(dot(qa[at, :], kat[:, k_at]))
            if masked:
                probs = jnp.where(lower, probs, 0.0)
            grads = (probs * dot(doa[at, :], vat[:, k_at])).astype(BF)
            dkt[:, k_at] += dot(qat[:, at], grads)
            dvt[:, k_at] += dot(doat[:, at], probs.astype(BF))
            return dq + dot(grads, ka[k_at, :])

        dq = lax.fori_loop(0, i, lambda j, dq: step(j, dq, False), jnp.zeros((AB, 128), F32))
        dqs[at, :] = step(i, dq, True) * 0.125

    @pl.loop(0, 8)
    def _(i):
        at = rows_at(i, QB)
        both = jnp.concatenate([dqs[at, 0:64], dkt[:, at].T], axis=1)
        both = both * tabc[at, :] - partner_of(both) * tabs[at, :]
        last = jnp.concatenate([dvt[:, at].T, jnp.zeros((QB, 64), F32)], axis=1)
        whole = jnp.concatenate([both, last], axis=1).astype(BF)
        dsort[pl.ds(i * 4, 4)] = whole.reshape(4, 64, 256)

    @pl.loop(0, 32)
    def _(j):
        dcat[rows_at(j, 64), 0:256] = dsort[order_ref[j]]

    mixed_sum.drain()
    for n in range(8):
        at = dn_sum.chip(n)
        part[at, :] = dot_nt(dcat[at, :], wcat[...]).astype(BF)
        dn_sum.start(n)
    dn_sum.step(0)
    dn_sum.step(3)

    gdacc[0:256, :] = jnp.zeros((256, D), F32)

    @pl.loop(0, 4)
    def _(i):
        at = rows_at(i, 512)
        gdacc[0:256, :] += dot_tn(dcat[at, 0:256], nrm[at, :])

    dn_sum.step(1)
    sum_q = column_sum(0)
    hand_out(gdacc, rawq, sum_q, 0, gqsend, gqrecv, 6)

    def low_half(part_of):
        return jnp.concatenate([part_of[:, 0:64], jnp.zeros((1, 64), F32)], axis=1)

    flat[32:56, :] = jnp.zeros((24, 128), F32)
    flat[64:96, :] = jnp.zeros((32, 128), F32)
    flat[104:112, :] = jnp.zeros((8, 128), F32)
    upper = lax.rem(s, 2) == 1
    spans = (sum_q[:, 0:128], pltpu.roll(sum_q[:, 0:128], 64, 1), sum_q[:, 128:256])
    for k in range(3):
        mine = low_half(spans[k])
        mine = jnp.where(upper, pltpu.roll(mine, 64, 1), mine)
        flat[pl.ds(32 + k * 8 + s // 2, 1), :] = mine
    flat[pl.ds(64 + 2 * s, 1), :] = sum_u[:, 0:128]
    flat[pl.ds(65 + 2 * s, 1), :] = sum_u[:, 128:256]
    dy_total = jnp.sum(dy_ref[...].astype(F32), axis=0, keepdims=True)
    to_flat(56, dy_total)
    to_flat(96, dy_total)
    for k in range(SEQ):
        fsend[k * 8 : k * 8 + 8, :] = flat[13 * k // 2 : 13 * k // 2 + 8, :]
    frecv[rows_at(s, 8), :] = fsend[rows_at(s, 8), :]

    @pl.loop(1, SEQ)
    def _(j):
        peer = lax.rem(s + j, SEQ)
        seq_copy(j, 3, fsend.at[rows_at(peer, 8)], frecv.at[rows_at(s, 8)]).start()

    dn_sum.step(4)
    dn_sum.step(2)

    sum_rows(gurecv, gusum, gufin, 5, 1)
    sum_rows(gqrecv, gqsum, gqfin, 6, 2)

    @pl.loop(1, SEQ)
    def _(j):
        giver = lax.rem(s + SEQ - j, SEQ)
        seq_copy(j, 3, frecv.at[rows_at(giver, 8)], frecv.at[rows_at(giver, 8)]).wait_recv()

    total = frecv[0:8, :]
    for k in range(1, SEQ):
        total = total + frecv[k * 8 : k * 8 + 8, :]
    fsum[...] = total
    fall[rows_at(b, 8), :] = total

    @pl.loop(1, BATCH)
    def _(j):
        batch_copy(j, 7, fsum, fall.at[rows_at(b, 8)]).start()

    @pl.loop(1, BATCH)
    def _(j):
        giver = lax.rem(b + BATCH - j, BATCH)
        batch_copy(j, 3, gdrecv.at[rows_at(giver, 32)], gdrecv.at[rows_at(giver, 32)]).wait_recv()
        batch_copy(j, 4, gorecv.at[rows_at(giver, 8)], gorecv.at[rows_at(giver, 8)]).wait_recv()

    total_d = gdrecv[0:32, :].astype(F32)
    total_o = gorecv[0:8, :]
    for k in range(1, BATCH):
        total_d = total_d + gdrecv[k * 32 : k * 32 + 32, :].astype(F32)
        total_o = total_o + gorecv[k * 8 : k * 8 + 8, :]
    gd_ref[...] = total_d
    go_ref[...] = total_o

    merged = dn_sum.result()
    _, normed, inverse = normed_of()
    grad_norm = inverse * (
        merged
        - jnp.mean(merged, axis=-1, keepdims=True)
        - normed * jnp.mean(merged * normed, axis=-1, keepdims=True)
    )
    gtok_ref[...] = (dy_ref[...].astype(F32) + grad_norm).astype(BF)

    @pl.loop(1, SEQ)
    def _(j):
        giver = lax.rem(s + SEQ - j, SEQ)
        seq_copy(j, 1, gufin.at[rows_at(giver, 8)], gufin.at[rows_at(giver, 8)]).wait_recv()
        seq_copy(j, 2, gqfin.at[rows_at(giver, 8)], gqfin.at[rows_at(giver, 8)]).wait_recv()

    @pl.loop(1, BATCH)
    def _(j):
        giver = lax.rem(b + BATCH - j, BATCH)
        batch_copy(j, 7, fall.at[rows_at(giver, 8)], fall.at[rows_at(giver, 8)]).wait_recv()

    gu_ref[...] = gufin[...]
    gq_ref[...] = gqfin[...]
    total = fall[0:8, :]
    for k in range(1, BATCH):
        total = total + fall[k * 8 : k * 8 + 8, :]
    small_ref[...] = total

    normed_gather.drain()
    dy_gather.drain()
    dn_sum.drain()

    @pl.loop(1, SEQ)
    def _(j):
        peer = lax.rem(s + j, SEQ)
        seq_copy(j, 0, wsend.at[rows_at(peer, 16)], wst.at[rows_at(s, 16)]).wait_send()
        seq_copy(j, 1, gusum.at[rows_at(peer, 8)], gufin.at[rows_at(s, 8)]).wait_send()
        seq_copy(j, 2, gqsum.at[rows_at(peer, 8)], gqfin.at[rows_at(s, 8)]).wait_send()
        seq_copy(j, 3, fsend.at[rows_at(peer, 8)], frecv.at[rows_at(s, 8)]).wait_send()

    @pl.loop(1, BATCH)
    def _(j):
        peer = lax.rem(b + j, BATCH)
        batch_copy(j, 0, wst, wbuf.at[rows_at(b, 256)]).wait_send()
        batch_copy(j, 1, wd_ref, wd2.at[rows_at(b, 32)]).wait_send()
        batch_copy(j, 2, wos, wo2.at[rows_at(b, 8)]).wait_send()
        batch_copy(j, 3, gdsend.at[rows_at(peer, 32)], gdrecv.at[rows_at(b, 32)]).wait_send()
        batch_copy(j, 4, gosend.at[rows_at(peer, 8)], gorecv.at[rows_at(b, 8)]).wait_send()
        batch_copy(j, 5, gusend.at[rows_at(peer, 128)], gurecv.at[rows_at(b, 128)]).wait_send()
        batch_copy(j, 6, gqsend.at[rows_at(peer, 128)], gqrecv.at[rows_at(b, 128)]).wait_send()
        batch_copy(j, 7, fsum, fall.at[rows_at(b, 8)]).wait_send()


def finish(
    mixed_ref, gtok_ref, gu_ref, gq_ref, gd_ref, go_ref, small_ref,
    mixed_out, gtok_out, small_out, qkv_out, out_out, up_out, down_out,
):
    s = lax.axis_index("seq")
    b = lax.axis_index("batch")
    mixed_out[...] = mixed_ref[...]
    gtok_out[...] = gtok_ref[...]
    out_out[...] = go_ref[...]
    down_out[...] = gd_ref[...]
    low = iota((8, 128), 1) < 64
    for k in range(SEQ):
        up_out[:, k * HID : k * HID + HID] = gu_ref[k * 8 : k * 8 + 8, :]
    for k in range(0, SEQ, 2):
        one, two = (gq_ref[n * 8 : n * 8 + 8, 0:128] for n in (k, k + 1))
        one_v, two_v = (gq_ref[n * 8 : n * 8 + 8, 128:256] for n in (k, k + 1))
        at = k * HD
        qkv_out[:, at : at + 128] = jnp.where(low, one, pltpu.roll(two, 64, 1))
        qkv_out[:, D + at : D + at + 128] = jnp.where(low, pltpu.roll(one, 64, 1), two)
        qkv_out[:, 2 * D + at : 2 * D + at + 128] = jnp.where(low, one_v, pltpu.roll(two_v, 64, 1))
    begin = b * PER + lax.rem(s, 2) * 64
    line = begin // 128
    both = jnp.concatenate([small_ref[pl.ds(line, 1), :], small_ref[pl.ds(line + 1, 1), :]], axis=1)
    both = pltpu.roll(jnp.broadcast_to(both, (8, 256)), 256 - lax.rem(begin, 128), 1)
    small_out[...] = both[0:1, 0:PER]


def layer(x, dy, wq, wo, wu, wd, sp, order, lengths):
    vmem = pl.BlockSpec(memory_space=pltpu.VMEM)
    smem = pl.BlockSpec(memory_space=pltpu.SMEM)
    scratch = [
        ((ROW, D), BF), ((ROW, D), BF), ((256, 256), BF), ((256, 256), BF), ((2048, 256), BF),
        ((256, D), BF), ((8, D), F32), ((64, D), F32), ((64, D), BF),
        ((D, 256), F32), ((D, 256), F32), ((D, 128), F32), ((D, 512), BF),
        ((1, 512), F32), ((1, D), F32),
        ((32, 64, 256), F32), ((ROW, HID), BF), ((ROW, HID), F32),
        ((ROW, 128), F32), ((ROW, 128), F32),
        ((ROW, 128), BF), ((ROW, 128), BF), ((ROW, 128), BF),
        ((128, ROW), BF), ((128, ROW), BF), ((64, ROW), BF), ((ROW, 128), BF), ((64, ROW), BF),
        ((32, 64, HD), BF), ((32, 64, HD), F32), ((ROW, HD), BF),
        ((ROW, 512), BF), ((HD, ROW), F32), ((HD, ROW), F32),
        ((32, 64, 256), BF), ((ROW, 128), F32),
        ((ROW, D), BF),
        ((8 * TOK, D), BF), ((4 * 64, D), BF), ((4 * TOK, D), BF), ((TOK, D), BF),
        ((8 * TOK, D), BF), ((4 * 64, D), BF), ((4 * TOK, D), BF), ((TOK, D), BF),
        ((320, D), F32), ((256, D), F32),
        ((256, D), BF), ((64, D), F32), ((256, D), BF), ((64, D), F32),
        ((D, 256), BF), ((D, 256), BF), ((128, 256), F32), ((128, 256), F32),
        ((D, 256), BF), ((D, 256), BF), ((128, 256), F32), ((128, 256), F32),
        ((112, 128), F32), ((128, 128), F32), ((128, 128), F32), ((8, 128), F32), ((64, 128), F32),
    ]
    shapes = [pltpu.VMEM(shape, dtype) for shape, dtype in scratch]
    shapes += [
        pltpu.SMEM((32,), jnp.int32),
        pltpu.SemaphoreType.DMA((2, 17)), pltpu.SemaphoreType.DMA((2, 17)),
        pltpu.SemaphoreType.DMA((2, 17)), pltpu.SemaphoreType.DMA((2, 17)),
        pltpu.SemaphoreType.DMA((4, SEQ)), pltpu.SemaphoreType.DMA((4, SEQ)),
        pltpu.SemaphoreType.DMA((8, BATCH)), pltpu.SemaphoreType.DMA((8, BATCH)),
    ]
    parts = pl.pallas_call(
        kernel,
        out_shape=(
            jax.ShapeDtypeStruct((TOK, D), BF),
            jax.ShapeDtypeStruct((TOK, D), BF),
            jax.ShapeDtypeStruct((128, 256), F32),
            jax.ShapeDtypeStruct((128, 256), F32),
            jax.ShapeDtypeStruct((32, D), F32),
            jax.ShapeDtypeStruct((8, D), F32),
            jax.ShapeDtypeStruct((8, 128), F32),
        ),
        in_specs=[vmem] * 7 + [smem] * 2,
        out_specs=(vmem,) * 7,
        scratch_shapes=shapes,
        compiler_params=pltpu.CompilerParams(
            collective_id=0, has_side_effects=True, vmem_limit_bytes=62 * 2**20
        ),
    )(x, dy, wq, wo, wu, wd, sp, order, lengths)
    return pl.pallas_call(
        finish,
        out_shape=(
            jax.ShapeDtypeStruct((TOK, D), BF),
            jax.ShapeDtypeStruct((TOK, D), BF),
            jax.ShapeDtypeStruct((1, PER), F32),
            jax.ShapeDtypeStruct((8, 3 * D), F32),
            jax.ShapeDtypeStruct((8, D), F32),
            jax.ShapeDtypeStruct((8, SEQ * HID), F32),
            jax.ShapeDtypeStruct((32, D), F32),
        ),
        in_specs=[vmem] * 7,
        out_specs=(vmem,) * 7,
    )(*parts)


def local(tokens, doc_lengths, block_order, small_params, w_qkv, w_out, w_up, w_down, cotangent):
    mixed, grad_tokens, grad_small, grad_qkv, grad_out, grad_up, grad_down = layer(
        tokens[0], cotangent[0], w_qkv, w_out, w_up, w_down,
        small_params.reshape(1, PER), block_order, doc_lengths,
    )
    return (
        mixed[None], grad_tokens[None], grad_small.reshape(PER), grad_qkv, grad_out, grad_up, grad_down,
    )


def solution(mesh):
    placed = (
        P("batch", "seq", None),
        P("batch", None),
        P(),
        P(("seq", "batch")),
        P(("seq", "batch"), None),
        P(("seq", "batch"), None),
        P(("seq", "batch"), None),
        P(("seq", "batch"), None),
        P("batch", "seq", None),
    )
    return jax.shard_map(
        local,
        mesh=mesh,
        in_specs=placed,
        out_specs=(
            P("batch", "seq", None),
            P("batch", "seq", None),
            P(("seq", "batch")),
            P(("seq", "batch"), None),
            P(("seq", "batch"), None),
            P(("seq", "batch"), None),
            P(("seq", "batch"), None),
        ),
        check_vma=False,
    )
```

time: 181 us -> 142 us (0.78); the launches traced: 178 us -> 142 us
  Pallas kernels: 164 us -> 141 us
  local copies, waits for them, and re-layouts: 10.5 us -> 0 us
  other arithmetic: 3.08 us -> 0 us
    pallas_call x1, Pallas kernels: 164 us -> 139 us  [layer(): pl.pallas_call(kernel, out_shape=(jax.ShapeDtypeStruct((TOK, D), BF), jax...]
    unnamed x33 -> x0, local copies, waits for them, and re-layouts: 4.38 us -> none
    slice x4 -> x0, local copies, waits for them, and re-layouts: 2.52 us -> none  [the longest x1 0.92 us: local(): small[:, 5, :3 * HD].reshape(SEQ, 3, HD).transpose(1, 0, 2).reshape(-1)]
    pallas_call x0 -> x1, Pallas kernels: none -> 2.12 us  [layer(): pl.pallas_call(finish, out_shape=(jax.ShapeDtypeStruct((TOK, D), BF), jax...]
    reshape x6 -> x0, local copies, waits for them, and re-layouts: 2.04 us -> none  [the longest x3 1.13 us: local(): w_qkv.reshape(8, 3, SEQ, HD).transpose(2, 0, 1, 3).reshape(SEQ, 8, 3 * HD)]
where the time goes in v2:
time: 142 us
  Pallas kernels  141 us (99%)
    pallas_call x1, Pallas kernels, layer(): pl.pallas_call(kernel, out_shape=(jax.ShapeDtypeStruct((TOK, D), BF), jax...  139 us

profile of v2, /device:TPU:1, one launch (start us, length us, event | category | flops | bytes accessed | tf_op | source)
XLA Modules:
  0.0 141.6 jit_solution(16118491631950941635)
XLA Ops:
  0.6 138.9 %shard_map.144 = (bf16[128,1024]{1,0:T(8,128)(2,1)}, bf16[128,1024]{1,0:T(8,128)(2,1)}, f32[128,256]{1,0:T(8,128)}, f32[128,256]{1,0:T(8,128)}, f32[32,1024]{1,0...) custom-call(bf16[128,1024]{1,0:T(8,128)(2,1)} %bitcast.6, bf16[128,1024]{1,0:T(8,128)(2,1)} %bitcast.7, ...), custom_call_target="tpu_custom_call" | custom-call | tf_op jit(solution)/shard_map/pallas_call | solution.py:846
  139.5 2.1 %shard_map.145 = (bf16[128,1024]{1,0:T(8,128)(2,1)}, bf16[128,1024]{1,0:T(8,128)(2,1)}, f32[1,104]{1,0:T(1,128)}, f32[8,3072]{1,0:T(8,128)}, f32[8,1024]{1,0:T(8...) custom-call(bf16[128,1024]{1,0:T(8,128)(2,1)} %get-tuple-element.21.mixed_ref, ...), custom_call_target="tpu_custom_call" | custom-call | tf_op jit(solution)/shard_map/pallas_call | solution.py:864

commit v3 on v2

v3 whole, which is shorter than its diff:
```python
import jax
import jax.numpy as jnp
import numpy as np
from jax import lax
from jax.experimental import pallas as pl
from jax.experimental.pallas import tpu as pltpu
from jax.sharding import PartitionSpec as P

HD = 64
ROT = 16
EPS = 1e-05
NEG = -1e30
MESH = pl.DeviceIdType.MESH
BF = jnp.bfloat16
F32 = jnp.float32

SEQ = 16
BATCH = 8
TOK = 128
ROW = SEQ * TOK
D = 1024
HID = 256
PER = 104
QB = 256
AB = 512


def dot(a, b):
    return lax.dot_general(a, b, (((1,), (0,)), ((), ())), preferred_element_type=F32)


def dot_nt(a, b):
    return lax.dot_general(a, b, (((1,), (1,)), ((), ())), preferred_element_type=F32)


def dot_tn(a, b):
    return lax.dot_general(a, b, (((0,), (0,)), ((), ())), preferred_element_type=F32)


def iota(shape, dim):
    return lax.broadcasted_iota(jnp.int32, shape, dim)


def slot(z, x, c):
    return z * 8 + x * 2 + c


def rows_at(index, count):
    return pl.ds(pl.multiple_of(index * count, count), count)


def kernel(
    x_ref, dy_ref, wq_ref, wo_ref, wu_ref, wd_ref, sp_ref, order_ref, len_ref,
    mixed_out, gtok_out, gu_out, gq_out, gd_out, go_out, small_out,
    mixed_ref, gtok_ref, gd_ref, go_ref, small_ref, nrm, dya, ssend, sgot, sall, wsend, wst, wbuf, wd2, wos, wo2, wob, rawq, rawu, cols, wcat, brow, drow,
    prj, act, dge, tabc, tabs, qa, ka, va, kat, vat, qat, doa, doat, dost, osort, ost,
    dcat, dkt, dvt, dsort, dqs,
    part_m, part_d, land_m, land_d, gdpair, gdland, gopair, goland, gupair, guland,
    gdacc, gtq, gtu, gdsend, gosend, gdrecv, gorecv,
    gusend, gurecv, gusum, gufin, gqsend, gqrecv, gqsum, gqfin,
    flat, fsend, frecv, fsum, fall,
    inv_ref, out_ss, ag_ss, ag_rs, rs_ss, rs_rs, sq_ss, sq_rs, bt_ss, bt_rs,
):
    s = lax.axis_index("seq")
    b = lax.axis_index("batch")
    z, x, c = s // 8, lax.rem(s // 2, 4), lax.rem(s, 2)
    xr, xl, xo = lax.rem(x + 1, 4), lax.rem(x + 3, 4), lax.rem(x + 2, 4)
    zo, co = 1 - z, 1 - c
    y, w = b // 2, lax.rem(b, 2)
    yr, yl, yo, wo_ = lax.rem(y + 1, 4), lax.rem(y + 3, 4), lax.rem(y + 2, 4), 1 - w
    right, left = (slot(z, xr, c), b), (slot(z, xl, c), b)
    across, sibling = (slot(zo, x, c), b), (slot(z, x, co), b)

    def remote(src, dst, send, recv, device):
        return pltpu.make_async_remote_copy(
            src_ref=src, dst_ref=dst, send_sem=send, recv_sem=recv,
            device_id=device, device_id_type=MESH,
        )

    barrier = pltpu.get_barrier_semaphore()

    @pl.loop(1, SEQ)
    def _(j):
        pl.semaphore_signal(barrier, inc=1, device_id=(lax.rem(s + j, SEQ), b), device_id_type=MESH)

    @pl.loop(1, BATCH)
    def _(j):
        pl.semaphore_signal(barrier, inc=1, device_id=(s, lax.rem(b + j, BATCH)), device_id_type=MESH)

    def normed_of():
        inputs = x_ref[...].astype(F32)
        centred = inputs - jnp.mean(inputs, axis=-1, keepdims=True)
        inverse = lax.rsqrt(jnp.mean(centred * centred, axis=-1, keepdims=True) + EPS)
        return inputs, centred * inverse, inverse

    nrm[rows_at(s, TOK), :] = normed_of()[1].astype(BF)
    dya[rows_at(s, TOK), :] = dy_ref[...]

    def pair(one, two):
        return jnp.where(iota((8, 128), 1) < 64, one, two)

    small = jnp.concatenate([sp_ref[...].astype(F32), jnp.zeros((1, 128 - PER), F32)], axis=1)
    ssend[...] = jnp.broadcast_to(small, (16, 128)).astype(BF)
    wide_q = wq_ref[...].astype(F32)
    wide_u = wu_ref[...].astype(F32)
    for k in range(SEQ):
        at = slice(k // 2 * 128, k // 2 * 128 + 128)
        q, kk, v = (wide_q[:, n * D : n * D + D][:, at] for n in range(3))
        turned = [pltpu.roll(part_of, 64, 1) for part_of in (q, kk, v)]
        q, kk, v = (q, turned[1], v) if k % 2 == 0 else (turned[0], kk, turned[2])
        low = jnp.concatenate([pair(q, kk), pair(v, jnp.zeros_like(v))], axis=1)
        block = jnp.concatenate([wide_u[:, k * HID : k * HID + HID], low], axis=0)
        wsend[k * 16 : k * 16 + 16, :] = block.astype(BF)

    wst[rows_at(s, 16), :] = wsend[rows_at(s, 16), :]
    sgot[rows_at(s, 16), :] = ssend[...]
    wos[...] = wo_ref[...].astype(F32)
    wd2[rows_at(b, 32), :] = wd_ref[...]
    wo2[rows_at(b, 8), :] = wos[...]

    pl.semaphore_wait(barrier, SEQ - 1 + BATCH - 1)

    def seq_copy(j, k, src, dst):
        return remote(src, dst, sq_ss.at[k], sq_rs.at[k], (lax.rem(s + j, SEQ), b))

    def seq_all(k, ref, count):
        ref = ref.at[pl.ds(0, (SEQ - 1) * count)]
        return seq_copy(1, k, ref, ref)

    def column_copy(j, k, src, dst):
        return remote(src, dst, bt_ss.at[k], bt_rs.at[k], (s, lax.rem(y + j, 4) * 2 + w))

    def column_start(k, send, recv, count):
        @pl.loop(1, 4)
        def _(j):
            peer = lax.rem(y + j, 4)
            column_copy(j, k, send.at[rows_at(peer, 2 * count)], recv.at[rows_at(y, 2 * count)]).start()

    def column_all(k, ref, count):
        ref = ref.at[pl.ds(0, 6 * count)]
        return column_copy(1, k, ref, ref)

    def pair_copy(k, pair, land, count):
        src = pair.at[rows_at(wo_, count)]
        return remote(src, land, bt_ss.at[k], bt_rs.at[k], (s, y * 2 + wo_))

    def column_sums(k, recv, pair, land, count):
        column_all(k, recv, count).wait_recv()
        total = recv[0 : 2 * count, :].astype(F32)
        for n in range(1, 4):
            total = total + recv[2 * n * count : 2 * (n + 1) * count, :].astype(F32)
        pair[...] = total.astype(pair.dtype)
        pair_copy(k + 5, pair, land, count).start()

    def pair_sum(k, pair, land, count):
        pair_copy(k + 5, pair, land, count).wait_recv()
        return pair[rows_at(w, count), :].astype(F32) + land[...].astype(F32)

    def batch_all(k, ref, count):
        ref = ref.at[pl.ds(0, (BATCH - 1) * count)]
        return batch_copy(1, k, ref, ref)

    def batch_copy(j, k, src, dst):
        return remote(src, dst, bt_ss.at[k], bt_rs.at[k], (s, lax.rem(b + j, BATCH)))

    @pl.loop(1, SEQ)
    def _(j):
        peer = lax.rem(s + j, SEQ)
        seq_copy(j, 0, wsend.at[rows_at(peer, 16)], wst.at[rows_at(s, 16)]).start()

    class Gather:
        def __init__(self, buf, k, size, slots, right, left, across, sibling=None):
            self.buf, self.k, self.size = buf, k, size
            own, far, of_left, of_right, far_left, far_right, opposite, far_opposite = slots[0]
            half = size // 2
            self.sends = {
                0: (own, right, 0, size), 1: (own, left, 0, size), 2: (own, across, 0, size),
                4: (far, right, 0, size), 5: (far, left, 0, size),
                7: (of_left, right, 0, half), 8: (of_right, left, half, half),
                11: (far_left, right, 0, half), 12: (far_right, left, half, half),
            }
            self.receives = {
                0: (of_left, 0, size), 1: (of_right, 0, size), 2: (far, 0, size),
                4: (far_left, 0, size), 5: (far_right, 0, size),
                7: (opposite, 0, half), 8: (opposite, half, half),
                11: (far_opposite, 0, half), 12: (far_opposite, half, half),
            }
            if sibling is not None:
                for e, n in ((3, 0), (6, 1), (9, 2), (10, 3), (13, 4), (14, 5), (15, 6), (16, 7)):
                    self.sends[e] = (slots[0][n], sibling, 0, size)
                    self.receives[e] = (slots[1][n], 0, size)

        def copy(self, e, index, device, low, count):
            at = self.buf.at[pl.ds(pl.multiple_of(index * self.size + low, self.size // 2), count)]
            return remote(at, at, ag_ss.at[self.k], ag_rs.at[self.k, e], device)

        def start(self, *events):
            for e in events:
                if e in self.sends:
                    self.copy(e, self.sends[e][0], *self.sends[e][1:]).start()

        def wait(self, *events):
            for e in events:
                if e in self.receives:
                    index, low, count = self.receives[e]
                    self.copy(e, index, self.sends[e][1], low, count).wait_recv()

        def step(self, n):
            if n == 0:
                self.start(0, 1, 2, 3)
            elif n == 1:
                self.wait(2)
                self.start(4, 5, 6)
                self.wait(0)
                self.start(7, 9)
                self.wait(1)
                self.start(8, 10)
            elif n == 2:
                self.wait(4)
                self.start(11, 13)
                self.wait(5)
                self.start(12, 14)
            elif n == 3:
                self.wait(7, 8)
                self.start(15)
                self.wait(11, 12)
                self.start(16)
            else:
                self.wait(3, 6, 9, 10, 13, 14, 15, 16)

        def drain(self):
            sent = self.buf.at[pl.ds(0, sum(what[3] for what in self.sends.values()))]
            remote(sent, sent, ag_ss.at[self.k], ag_rs.at[self.k, 0], right).wait_send()

    def row_slots(core):
        return [slot(p, q, core) for p, q in ((z, x), (zo, x), (z, xl), (z, xr), (zo, xl), (zo, xr), (z, xo), (zo, xo))]

    rows_slots = [q * 2 + p for p, q in ((w, y), (wo_, y), (w, yl), (w, yr), (wo_, yl), (wo_, yr), (w, yo), (wo_, yo))]

    normed_gather = Gather(nrm, 0, TOK, (row_slots(c), row_slots(co)), right, left, across, sibling)
    dy_gather = Gather(dya, 1, TOK, (row_slots(c), row_slots(co)), right, left, across, sibling)
    weight_gather = Gather(
        wbuf, 2, 256, (rows_slots,), (s, yr * 2 + w), (s, yl * 2 + w), (s, y * 2 + wo_)
    )
    @pl.loop(0, 32)
    def _(i):
        place = jnp.int32(0)
        for j in range(32):
            place = place + jnp.where(order_ref[j] == i, j, 0)
        inv_ref[i] = jnp.minimum(place, 31)

    normed_gather.step(0)

    @pl.loop(1, SEQ)
    def _(j):
        seq_copy(j, 4, ssend, sgot.at[rows_at(s, 16)]).start()

    outputs = (
        (mixed_ref, mixed_out), (gtok_ref, gtok_out), (gufin, gu_out), (gqfin, gq_out),
        (gd_ref, gd_out), (go_ref, go_out), (small_ref, small_out),
    )

    def output(n):
        return pltpu.make_async_copy(*outputs[n], out_ss.at[n])

    ends = [len_ref[0, 0]]
    for k in range(1, 4):
        ends.append(ends[-1] + len_ref[0, k])

    def begin_of(where):
        begin = jnp.zeros_like(where)
        for end in ends:
            begin = jnp.maximum(begin, jnp.where(where >= end, end, 0))
        return begin

    def doc_of(where):
        doc = jnp.zeros_like(where)
        for end in ends:
            doc = doc + jnp.where(where >= end, 1, 0)
        return doc

    def partner_of(part):
        lane = lax.rem(iota(part.shape, 1), 64)
        return jnp.where(lane < ROT // 2, pltpu.roll(part, 120, 1), pltpu.roll(part, 8, 1))

    rate = jnp.zeros((1, 128), F32)
    for k in range(ROT // 2):
        value = float(np.float32(10000.0) ** np.float32(-2.0 * k / ROT))
        rate = jnp.where(lax.rem(iota((1, 128), 1), 8) == k, value, rate)

    @pl.loop(0, 8)
    def _(i):
        where = i * QB + iota((QB, 128), 0)
        angle = (where - begin_of(where)).astype(F32) * rate
        lane = lax.rem(iota((QB, 128), 1), 64)
        sine = jnp.sin(angle)
        tabc[rows_at(i, QB), :] = jnp.where(lane < ROT, jnp.cos(angle), 1.0)
        sine = jnp.where(lane < ROT // 2, -sine, sine)
        tabs[rows_at(i, QB), :] = jnp.where(lane < ROT, sine, 0.0)

    seq_all(0, wst, 16).wait_recv()
    seq_all(4, sgot, 16).wait_recv()

    wbuf[rows_at(b, 256), :] = wst[...]
    weight_gather.step(0)
    lines = [sgot[k * 16 : k * 16 + 16, :].astype(F32)[0:1, :] for k in range(SEQ)]
    sall[rows_at(b, 16), :] = jnp.concatenate(lines, axis=0).astype(BF)

    @pl.loop(1, BATCH)
    def _(j):
        batch_copy(j, 0, sall.at[rows_at(b, 16)], sall.at[rows_at(b, 16)]).start()

    normed_gather.step(1)
    weight_gather.step(1)

    batch_all(0, sall, 16).wait_recv()

    def hot_of(line, number):
        low = (lax.rem(line, 16) * BATCH + line // 16) * PER
        return ((low <= number) & (number < low + PER)).astype(F32).astype(BF)

    def place_of(number):
        owner = jnp.floor((number.astype(F32) + 0.5) * (1.0 / PER)).astype(jnp.int32)
        return number - PER * owner

    for k in range(4):
        number = k * D + iota((D, 1), 0)
        found = dot(hot_of(iota((1, 128), 1), number), sall[...])
        found = jnp.where(iota((D, 128), 1) == place_of(number), found, 0.0)
        cols[:, k : k + 1] = jnp.sum(found, axis=1, keepdims=True)

    def small_row(number):
        found = dot_tn(sall[...], hot_of(iota((128, 1), 0), number))
        found = jnp.where(iota((128, number.shape[1]), 0) == place_of(number), found, 0.0)
        return jnp.sum(found, axis=0, keepdims=True)

    lane = iota((1, 256), 1)
    number_q = 4 * D + (lane // 64) * D + s * 64 + lax.rem(lane, 64)
    bias_q = small_row(jnp.where(lane < 192, number_q, -1000))
    bias_u = small_row(8 * D + s * HID + lane)
    wide = iota((1, D), 1)
    drow[...] = small_row(7 * D + wide) + small_row(12 * D + wide)

    dy_gather.start(2)
    weight_gather.step(2)
    normed_gather.step(2)
    dy_gather.start(0, 1)
    weight_gather.step(3)

    @pl.loop(0, SEQ)
    def _(i):
        for j in range(BATCH):
            block = wbuf[pl.ds(pl.multiple_of(j * 256 + i * 16, 16), 16), :].astype(F32)
            at = pl.ds(pl.multiple_of(i * 64 + j * 8, 8), 8)
            rawu[at, :] = block[0:8, :]
            rawq[at, :] = block[8:16, :]

    row_q, row_u = bias_q, bias_u
    for i in range(8):
        at = slice(i * 128, i * 128 + 128)
        wq, wu = rawq[at, :], rawu[at, :]
        wcat[at, 0:256] = (wq * cols[at, 0:1]).astype(BF)
        wcat[at, 256:512] = (wu * cols[at, 2:3]).astype(BF)
        row_q = row_q + jnp.sum(wq * cols[at, 1:2], axis=0, keepdims=True)
        row_u = row_u + jnp.sum(wu * cols[at, 3:4], axis=0, keepdims=True)
    brow[:, 0:256] = row_q
    brow[:, 256:512] = row_u

    normed_gather.step(3)
    dy_gather.wait(2)
    dy_gather.start(4, 5, 3, 6)
    normed_gather.step(4)

    @pl.loop(0, 4)
    def _(i):
        out = dot(nrm[rows_at(i, 512), :], wcat[:, 0:256]) + brow[:, 0:256]
        prj[pl.ds(i * 8, 8)] = out.reshape(8, 64, 256)

    @pl.loop(1, BATCH)
    def _(j):
        batch_copy(j, 1, wd_ref, wd2.at[rows_at(b, 32)]).start()
        batch_copy(j, 2, wos, wo2.at[rows_at(b, 8)]).start()

    def pieces_of(value):
        high = value.astype(BF).astype(F32)
        mid = (value - high).astype(BF).astype(F32)
        return high, mid, value - high - mid

    def with_lanes(base, first, values):
        lane = iota(base.shape, 1)
        for k, value in enumerate(values):
            base = jnp.where(lane == first + k, value, base)
        return base

    def blocks_of(ref, order, i):
        return jnp.concatenate([ref[order[i * 4 + k]] for k in range(4)], axis=0)

    @pl.loop(0, 8)
    def _(i):
        at = rows_at(i, QB)
        come = blocks_of(prj, inv_ref, i)
        both = come[:, 0:128]
        both = both * tabc[at, :] + partner_of(both) * tabs[at, :]
        lane = iota((QB, 128), 1)
        own = doc_of(i * QB + iota((QB, 128), 0)) == lane - 64
        front = lane < 64
        query = jnp.where(front, both * 0.125, jnp.where(own | (lane >= 68), 0.0, NEG)).astype(BF)
        tail = jnp.where(lane < 68, own.astype(F32), (lane < 71).astype(F32))
        key = jnp.where(front, pltpu.roll(both, 64, 1), tail).astype(BF)
        value = jnp.where(front, come[:, 128:256], (lane < 67).astype(F32)).astype(BF)
        qa[at, :], ka[at, :], va[at, :] = query, key, value
        qat[:, at] = query.T[0:64, :]
        kat[:, at] = key.T
        vat[:, at] = value.T

    dy_gather.wait(0)
    dy_gather.start(7)
    dy_gather.wait(1)
    dy_gather.start(8)

    lower = iota((AB, AB), 1) <= iota((AB, AB), 0)

    def attend(i):
        at = rows_at(i, AB)

        def step(j, carry, masked):
            top, total = carry
            k_at = rows_at(j, AB)
            scores = dot(qa[at, :], kat[:, k_at])
            if masked:
                scores = jnp.where(lower, scores, NEG)
            peak = jnp.maximum(top, jnp.max(scores, axis=1, keepdims=True))
            expos = jnp.exp(scores - peak).astype(BF)
            return peak, total * jnp.exp(top - peak) + dot(expos, va[k_at, :])

        start = (jnp.full((AB, 1), NEG, F32), jnp.zeros((AB, 128), F32))
        carry = lax.fori_loop(0, i, lambda j, carry: step(j, carry, False), start)
        top, total = step(i, carry, True)
        norm = total[:, 64:65]
        osort[pl.ds(i * (AB // 64), AB // 64)] = (total / norm)[:, 0:64].reshape(AB // 64, 64, HD)
        qa[at, :] = with_lanes(qa[at, :].astype(F32), 68, pieces_of(-(top + jnp.log(norm)))).astype(BF)

    pl.loop(0, 3)(attend)
    dy_gather.wait(4)
    dy_gather.start(11)
    dy_gather.wait(5)
    dy_gather.start(12, 9, 10)
    pl.loop(3, 4)(attend)

    @pl.loop(0, 4)
    def _(i):
        at = rows_at(i, 512)
        hidden = dot(nrm[at, :], wcat[:, 256:512]) + brow[:, 256:512]
        share = 0.5 * (1.0 + lax.erf(hidden * (2.0**-0.5)))
        act[at, :] = (hidden * share).astype(BF)
        dge[at, :] = share + hidden * jnp.exp(-0.5 * hidden * hidden) * ((2.0 * np.pi) ** -0.5)

    dy_gather.wait(7, 8, 11, 12)
    dy_gather.start(13, 14, 15, 16)

    @pl.loop(0, 8)
    def _(j):
        ost[rows_at(j, QB), :] = blocks_of(osort, order_ref, j).astype(BF)

    batch_all(1, wd2, 32).wait_recv()
    batch_all(2, wo2, 8).wait_recv()

    wob[...] = wo2[...].astype(BF)

    class Scatter:
        def __init__(self, part, land, k):
            self.part, self.land, self.k = part, land, k
            self.order = [(zo, xo), (zo, xr), (zo, xl), (zo, x), (z, xo), (z, xr), (z, xl), (z, x)]
            table = [(n, co, 0, TOK, sibling, None) for n in range(8)]
            for g in (0, 4):
                table += [
                    (g, c, 0, 64, left, g + 2), (g, c, 64, 64, right, g + 1),
                    (g + 1, c, 0, 64, right, g + 3), (g + 2, c, 64, 64, left, g + 3),
                    (g + 1, c, 64, 64, right, g + 3), (g + 2, c, 0, 64, left, g + 3),
                ]
            table += [(3, c, 0, TOK, across, 7)]
            self.table, self.begin, at = table, [], 0
            for entry in table:
                self.begin.append(at)
                at += entry[3]

        def chip(self, n):
            return pl.ds(pl.multiple_of((self.order[n][0] * 4 + self.order[n][1]) * 256, 256), 256)

        def at(self, n, core, low, count):
            zz, xx = self.order[n]
            return pl.ds(pl.multiple_of(slot(zz, xx, core) * TOK + low, 16), count)

        def copy(self, e, src, dst, device):
            return remote(src, dst, rs_ss.at[self.k], rs_rs.at[self.k, e], device)

        def out(self, e):
            n, core, low, count, device, _ = self.table[e]
            return self.part.at[self.at(n, core, low, count)], self.land.at[pl.ds(self.begin[e], count)], device

        def start(self, *events):
            for e in events:
                self.copy(e, *self.out(e)).start()

        def wait(self, e):
            src, dst, device = self.out(e)
            self.copy(e, dst, dst, device).wait_recv()

        def landed(self, e):
            self.wait(e)
            return self.land[self.begin[e] : self.begin[e] + self.table[e][3], :].astype(F32)

        def add(self, *events):
            for e in events:
                n, core, low, count, _, to = self.table[e]
                to = e if e < 8 else to
                at = self.at(to, c, low, count)
                self.part[at, :] = (self.part[at, :].astype(F32) + self.landed(e)).astype(BF)

        def step(self, n):
            if n == 0 or n == 1:
                self.add(4 * n)
                self.start(8 + 6 * n, 9 + 6 * n)
            elif n == 2 or n == 3:
                g = n - 2
                self.add(4 * g + 1, 4 * g + 2)
                self.start(10 + 6 * g, 11 + 6 * g)
                self.add(4 * g + 3)
            elif n == 4 or n == 5:
                g = n - 4
                self.add(8 + 6 * g, 9 + 6 * g)
                self.start(12 + 6 * g, 13 + 6 * g)
            else:
                self.add(10, 11, 12, 13)
                self.start(20)

        def result(self):
            total = self.part[self.at(7, c, 0, TOK), :].astype(F32)
            low = total[0:64, :] + self.landed(16) + self.landed(19)
            high = total[64:TOK, :] + self.landed(17) + self.landed(18)
            return jnp.concatenate([low, high], axis=0) + self.landed(20)

        def drain(self):
            sent = self.part.at[pl.ds(0, sum(entry[3] for entry in self.table))]
            self.copy(0, sent, sent, sibling).wait_send()

    mixed_sum = Scatter(part_m, land_m, 0)
    dn_sum = Scatter(part_d, land_d, 1)

    for n in range(8):
        at = mixed_sum.chip(n)
        part_m[at, :] = (dot(act[at, :], wd2[...]) + dot(ost[at, :], wob[...])).astype(BF)
        mixed_sum.start(n)

    dy_gather.step(4)

    @pl.loop(0, 4)
    def _(i):
        at = rows_at(i, 512)
        dy = dya[at, :]
        dcat[at, 256:512] = (dot_nt(dy, wd2[...]) * dge[at, :]).astype(BF)
        dost[pl.ds(i * 8, 8)] = dot_nt(dy, wob[...]).astype(BF).reshape(8, 64, HD)

    mixed_sum.step(0)
    mixed_sum.step(2)
    mixed_sum.step(1)
    mixed_sum.step(3)

    gdacc[...] = jnp.zeros_like(gdacc)

    @pl.loop(0, 4)
    def _(i):
        at = rows_at(i, 512)
        gdacc[0:256, :] += dot_tn(act[at, :], dya[at, :])
        gdacc[256:320, :] += dot_tn(ost[at, :], dya[at, :])

    gdsend[...] = gdacc[0:256, :].astype(BF)
    gosend[...] = gdacc[256:320, :]
    gdrecv[rows_at(y, 64), :] = gdsend[rows_at(y, 64), :]
    gorecv[rows_at(y, 16), :] = gosend[rows_at(y, 16), :]
    column_start(3, gdsend, gdrecv, 32)
    column_start(4, gosend, gorecv, 8)

    def column_sum(low):
        def add(i, total):
            return total + jnp.sum(dcat[rows_at(i, QB), low : low + 256].astype(F32), axis=0, keepdims=True)

        return lax.fori_loop(0, 8, add, jnp.zeros((1, 256), F32))

    def to_flat(line, values):
        for k in range(values.shape[1] // 128):
            flat[line + k : line + k + 1, :] = values[:, k * 128 : k * 128 + 128]

    def hand_out(gt, raw, sums, k, send):
        for i in range(4):
            at = slice(i * 256, i * 256 + 256)
            grad = gt[0:256, at].T
            gain = jnp.sum(grad * raw[at, :], axis=1, keepdims=True)
            shift = jnp.sum(sums * raw[at, :], axis=1, keepdims=True)
            lane = iota((256, 128), 1)
            spread = jnp.where(lane == 0, gain, jnp.where(lane == 1, shift, 0.0)).T
            to_flat(k * 8 + i * 2, spread[0:1, :])
            to_flat(k * 8 + 8 + i * 2, spread[1:2, :])
            grad = grad * cols[at, k : k + 1] + cols[at, k + 1 : k + 2] * sums
            for m in range(8):
                for h in range(2):
                    place = m * 128 + i * 32 + h * 16
                    first, second = (h * 2) * 64 + m * 8, (h * 2 + 1) * 64 + m * 8
                    send[place : place + 16, :] = jnp.concatenate(
                        [grad[first : first + 8, :], grad[second : second + 8, :]], axis=0
                    ).astype(BF)
    def to_owners(total, total_ref, final, k):
        total_ref[...] = total
        final[rows_at(s, 8), :] = total_ref[rows_at(s, 8), :]

        @pl.loop(1, SEQ)
        def _(j):
            peer = lax.rem(s + j, SEQ)
            seq_copy(j, k, total_ref.at[rows_at(peer, 8)], final.at[rows_at(s, 8)]).start()

    gtu[...] = jnp.zeros_like(gtu)

    @pl.loop(0, 4)
    def _(i):
        at = rows_at(i, 512)
        gtu[...] += dot_tn(dcat[at, 256:512], nrm[at, :])

    sum_u = column_sum(256)
    mixed_sum.step(4)
    hand_out(gtu, rawu, sum_u, 2, gusend)
    gurecv[rows_at(y, 256), :] = gusend[rows_at(y, 256), :]
    column_start(5, gusend, gurecv, 128)


    @pl.loop(0, 8)
    def _(i):
        at = rows_at(i, QB)
        grads = blocks_of(dost, inv_ref, i).astype(F32)
        past = osort[pl.ds(i * 4, 4)].reshape(QB, HD)
        delta = jnp.sum(grads * past, axis=1, keepdims=True)
        wide = jnp.concatenate([grads, jnp.zeros((QB, 64), F32)], axis=1)
        wide = with_lanes(wide, 64, pieces_of(-delta)).astype(BF)
        doa[at, :] = wide
        doat[:, at] = wide.T[0:64, :]

    dkt[...] = jnp.zeros_like(dkt)
    dvt[...] = jnp.zeros_like(dvt)

    mixed_sum.step(5)

    @pl.loop(0, ROW // AB)
    def _(i):
        at = rows_at(i, AB)

        def step(j, dq, masked):
            k_at = rows_at(j, AB)
            probs = jnp.exp(dot(qa[at, :], kat[:, k_at]))
            if masked:
                probs = jnp.where(lower, probs, 0.0)
            grads = (probs * dot(doa[at, :], vat[:, k_at])).astype(BF)
            dkt[:, k_at] += dot(qat[:, at], grads)
            dvt[:, k_at] += dot(doat[:, at], probs.astype(BF))
            return dq + dot(grads, ka[k_at, :])

        dq = lax.fori_loop(0, i, lambda j, dq: step(j, dq, False), jnp.zeros((AB, 128), F32))
        dqs[at, :] = step(i, dq, True) * 0.125

    mixed_sum.step(6)
    column_sums(3, gdrecv, gdpair, gdland, 32)
    column_sums(4, gorecv, gopair, goland, 8)
    column_sums(5, gurecv, gupair, guland, 128)

    @pl.loop(0, 8)
    def _(i):
        at = rows_at(i, QB)
        both = jnp.concatenate([dqs[at, 0:64], dkt[:, at].T], axis=1)
        both = both * tabc[at, :] - partner_of(both) * tabs[at, :]
        last = jnp.concatenate([dvt[:, at].T, jnp.zeros((QB, 64), F32)], axis=1)
        whole = jnp.concatenate([both, last], axis=1).astype(BF)
        dsort[pl.ds(i * 4, 4)] = whole.reshape(4, 64, 256)

    @pl.loop(0, 8)
    def _(j):
        dcat[rows_at(j, QB), 0:256] = blocks_of(dsort, order_ref, j)

    for n in range(8):
        at = dn_sum.chip(n)
        part_d[at, :] = dot_nt(dcat[at, :], wcat[...]).astype(BF)
        dn_sum.start(n)
        if n == 3:
            dn_sum.step(0)

    dn_sum.step(2)

    gtq[...] = jnp.zeros_like(gtq)

    def add_gtq(i):
        at = rows_at(i, 512)
        gtq[...] += dot_tn(dcat[at, 0:256], nrm[at, :])

    pl.loop(0, 2)(add_gtq)
    dn_sum.step(1)
    dn_sum.step(3)
    pl.loop(2, 4)(add_gtq)

    sum_q = column_sum(0)
    dn_sum.step(4)
    hand_out(gtq, rawq, sum_q, 0, gqsend)
    gqrecv[rows_at(b, 128), :] = gqsend[rows_at(b, 128), :]

    @pl.loop(1, BATCH)
    def _(j):
        peer = lax.rem(b + j, BATCH)
        batch_copy(j, 6, gqsend.at[rows_at(peer, 128)], gqrecv.at[rows_at(b, 128)]).start()

    to_owners(pair_sum(5, gupair, guland, 128), gusum, gufin, 1)
    def low_half(part_of):
        return jnp.concatenate([part_of[:, 0:64], jnp.zeros((1, 64), F32)], axis=1)

    flat[32:56, :] = jnp.zeros((24, 128), F32)
    flat[64:96, :] = jnp.zeros((32, 128), F32)
    flat[104:112, :] = jnp.zeros((8, 128), F32)
    upper = lax.rem(s, 2) == 1
    spans = (sum_q[:, 0:128], pltpu.roll(sum_q[:, 0:128], 64, 1), sum_q[:, 128:256])
    for k in range(3):
        mine = low_half(spans[k])
        mine = jnp.where(upper, pltpu.roll(mine, 64, 1), mine)
        flat[pl.ds(32 + k * 8 + s // 2, 1), :] = mine
    flat[pl.ds(64 + 2 * s, 1), :] = sum_u[:, 0:128]
    flat[pl.ds(65 + 2 * s, 1), :] = sum_u[:, 128:256]
    dy_total = jnp.sum(dy_ref[...].astype(F32), axis=0, keepdims=True)
    to_flat(56, dy_total)
    to_flat(96, dy_total)
    for k in range(SEQ):
        fsend[k * 8 : k * 8 + 8, :] = flat[13 * k // 2 : 13 * k // 2 + 8, :]
    frecv[rows_at(s, 8), :] = fsend[rows_at(s, 8), :]

    @pl.loop(1, SEQ)
    def _(j):
        peer = lax.rem(s + j, SEQ)
        seq_copy(j, 3, fsend.at[rows_at(peer, 8)], frecv.at[rows_at(s, 8)]).start()

    dn_sum.step(5)
    dn_sum.step(6)
    batch_all(6, gqrecv, 128).wait_recv()
    total = gqrecv[0:128, :].astype(F32)
    for k in range(1, BATCH):
        total = total + gqrecv[k * 128 : k * 128 + 128, :].astype(F32)
    to_owners(total, gqsum, gqfin, 2)
    mixed_ref[...] = (mixed_sum.result() + x_ref[...].astype(F32) + drow[...]).astype(BF)
    output(0).start()

    seq_all(3, frecv, 8).wait_recv()

    total = frecv[0:8, :]
    for k in range(1, SEQ):
        total = total + frecv[k * 8 : k * 8 + 8, :]
    fsum[...] = total
    fall[rows_at(b, 8), :] = total

    @pl.loop(1, BATCH)
    def _(j):
        batch_copy(j, 7, fsum, fall.at[rows_at(b, 8)]).start()

    gd_ref[...] = pair_sum(3, gdpair, gdland, 32)
    go_ref[...] = pair_sum(4, gopair, goland, 8)
    output(4).start()
    output(5).start()

    merged = dn_sum.result()
    _, normed, inverse = normed_of()
    grad_norm = inverse * (
        merged
        - jnp.mean(merged, axis=-1, keepdims=True)
        - normed * jnp.mean(merged * normed, axis=-1, keepdims=True)
    )
    gtok_ref[...] = (dy_ref[...].astype(F32) + grad_norm).astype(BF)
    output(1).start()

    seq_all(1, gufin, 8).wait_recv()
    seq_all(2, gqfin, 8).wait_recv()

    batch_all(7, fall, 8).wait_recv()

    output(2).start()
    output(3).start()
    total = fall[0:8, :]
    for k in range(1, BATCH):
        total = total + fall[k * 8 : k * 8 + 8, :]
    small_ref[...] = total
    output(6).start()

    normed_gather.drain()
    dy_gather.drain()
    weight_gather.drain()
    mixed_sum.drain()
    dn_sum.drain()

    for k, ref, count in ((0, wst, 16), (1, gufin, 8), (2, gqfin, 8), (3, frecv, 8), (4, sgot, 16)):
        seq_all(k, ref, count).wait_send()
    for k, ref, count in (
        (0, sall, 16), (1, wd2, 32), (2, wo2, 8), (6, gqrecv, 128), (7, fall, 8),
    ):
        batch_all(k, ref, count).wait_send()
    for k, ref, pair, land, count in (
        (3, gdrecv, gdpair, gdland, 32), (4, gorecv, gopair, goland, 8), (5, gurecv, gupair, guland, 128),
    ):
        column_all(k, ref, count).wait_send()
        pair_copy(k + 5, pair, land, count).wait_send()

    for n in range(7):
        output(n).wait()


def finish(
    mixed_ref, gtok_ref, gu_ref, gq_ref, gd_ref, go_ref, small_ref,
    mixed_out, gtok_out, small_out, qkv_out, out_out, up_out, down_out,
):
    s = lax.axis_index("seq")
    b = lax.axis_index("batch")
    mixed_out[...] = mixed_ref[...]
    gtok_out[...] = gtok_ref[...]
    out_out[...] = go_ref[...]
    down_out[...] = gd_ref[...]
    low = iota((8, 128), 1) < 64
    for k in range(SEQ):
        up_out[:, k * HID : k * HID + HID] = gu_ref[k * 8 : k * 8 + 8, :]
    for k in range(0, SEQ, 2):
        one, two = (gq_ref[n * 8 : n * 8 + 8, 0:128] for n in (k, k + 1))
        one_v, two_v = (gq_ref[n * 8 : n * 8 + 8, 128:256] for n in (k, k + 1))
        at = k * HD
        qkv_out[:, at : at + 128] = jnp.where(low, one, pltpu.roll(two, 64, 1))
        qkv_out[:, D + at : D + at + 128] = jnp.where(low, pltpu.roll(one, 64, 1), two)
        qkv_out[:, 2 * D + at : 2 * D + at + 128] = jnp.where(low, one_v, pltpu.roll(two_v, 64, 1))
    begin = b * PER + lax.rem(s, 2) * 64
    line = begin // 128
    both = jnp.concatenate([small_ref[pl.ds(line, 1), :], small_ref[pl.ds(line + 1, 1), :]], axis=1)
    both = pltpu.roll(jnp.broadcast_to(both, (8, 256)), 256 - lax.rem(begin, 128), 1)
    small_out[...] = both[0:1, 0:PER]


def layer(x, dy, wq, wo, wu, wd, sp, order, lengths):
    vmem = pl.BlockSpec(memory_space=pltpu.VMEM)
    smem = pl.BlockSpec(memory_space=pltpu.SMEM)
    scratch = [
        ((TOK, D), BF), ((TOK, D), BF), ((32, D), F32), ((8, D), F32), ((8, 128), F32),
        ((ROW, D), BF), ((ROW, D), BF), ((16, 128), BF), ((256, 128), BF), ((128, 128), BF),
        ((256, 256), BF), ((256, 256), BF), ((2048, 256), BF),
        ((256, D), BF), ((8, D), F32), ((64, D), F32), ((64, D), BF),
        ((D, 256), F32), ((D, 256), F32), ((D, 128), F32), ((D, 512), BF),
        ((1, 512), F32), ((1, D), F32),
        ((32, 64, 256), F32), ((ROW, HID), BF), ((ROW, HID), F32),
        ((ROW, 128), F32), ((ROW, 128), F32),
        ((ROW, 128), BF), ((ROW, 128), BF), ((ROW, 128), BF),
        ((128, ROW), BF), ((128, ROW), BF), ((64, ROW), BF), ((ROW, 128), BF), ((64, ROW), BF),
        ((32, 64, HD), BF), ((32, 64, HD), F32), ((ROW, HD), BF),
        ((ROW, 512), BF), ((HD, ROW), F32), ((HD, ROW), F32),
        ((32, 64, 256), BF), ((ROW, 128), F32),
        ((ROW, D), BF), ((ROW, D), BF),
        ((1920, D), BF), ((1920, D), BF), ((64, D), BF), ((32, D), BF), ((16, D), F32), ((8, D), F32),
        ((256, 256), BF), ((128, 256), BF),
        ((320, D), F32), ((256, D), F32), ((256, D), F32),
        ((256, D), BF), ((64, D), F32), ((256, D), BF), ((64, D), F32),
        ((D, 256), BF), ((D, 256), BF), ((128, 256), F32), ((128, 256), F32),
        ((D, 256), BF), ((D, 256), BF), ((128, 256), F32), ((128, 256), F32),
        ((112, 128), F32), ((128, 128), F32), ((128, 128), F32), ((8, 128), F32), ((64, 128), F32),
    ]
    shapes = [pltpu.VMEM(shape, dtype) for shape, dtype in scratch]
    shapes += [
        pltpu.SMEM((32,), jnp.int32),
        pltpu.SemaphoreType.DMA((7,)),
        pltpu.SemaphoreType.DMA((3,)), pltpu.SemaphoreType.DMA((3, 17)),
        pltpu.SemaphoreType.DMA((2,)), pltpu.SemaphoreType.DMA((2, 21)),
        pltpu.SemaphoreType.DMA((5,)), pltpu.SemaphoreType.DMA((5,)),
        pltpu.SemaphoreType.DMA((11,)), pltpu.SemaphoreType.DMA((11,)),
    ]
    parts = pl.pallas_call(
        kernel,
        out_shape=(
            jax.ShapeDtypeStruct((TOK, D), BF),
            jax.ShapeDtypeStruct((TOK, D), BF),
            jax.ShapeDtypeStruct((128, 256), F32),
            jax.ShapeDtypeStruct((128, 256), F32),
            jax.ShapeDtypeStruct((32, D), F32),
            jax.ShapeDtypeStruct((8, D), F32),
            jax.ShapeDtypeStruct((8, 128), F32),
        ),
        in_specs=[vmem] * 7 + [smem] * 2,
        out_specs=(pl.BlockSpec(memory_space=pl.ANY),) * 7,
        scratch_shapes=shapes,
        compiler_params=pltpu.CompilerParams(
            collective_id=0, has_side_effects=True, vmem_limit_bytes=62 * 2**20
        ),
    )(x, dy, wq, wo, wu, wd, sp, order, lengths)
    return pl.pallas_call(
        finish,
        out_shape=(
            jax.ShapeDtypeStruct((TOK, D), BF),
            jax.ShapeDtypeStruct((TOK, D), BF),
            jax.ShapeDtypeStruct((1, PER), F32),
            jax.ShapeDtypeStruct((8, 3 * D), F32),
            jax.ShapeDtypeStruct((8, D), F32),
            jax.ShapeDtypeStruct((8, SEQ * HID), F32),
            jax.ShapeDtypeStruct((32, D), F32),
        ),
        in_specs=[vmem] * 7,
        out_specs=(vmem,) * 7,
    )(*parts)


def local(tokens, doc_lengths, block_order, small_params, w_qkv, w_out, w_up, w_down, cotangent):
    mixed, grad_tokens, grad_small, grad_qkv, grad_out, grad_up, grad_down = layer(
        tokens[0], cotangent[0], w_qkv, w_out, w_up, w_down,
        small_params.reshape(1, PER), block_order, doc_lengths,
    )
    return (
        mixed[None], grad_tokens[None], grad_small.reshape(PER), grad_qkv, grad_out, grad_up, grad_down,
    )


def solution(mesh):
    placed = (
        P("batch", "seq", None),
        P("batch", None),
        P(),
        P(("seq", "batch")),
        P(("seq", "batch"), None),
        P(("seq", "batch"), None),
        P(("seq", "batch"), None),
        P(("seq", "batch"), None),
        P("batch", "seq", None),
    )
    return jax.shard_map(
        local,
        mesh=mesh,
        in_specs=placed,
        out_specs=(
            P("batch", "seq", None),
            P("batch", "seq", None),
            P(("seq", "batch")),
            P(("seq", "batch"), None),
            P(("seq", "batch"), None),
            P(("seq", "batch"), None),
            P(("seq", "batch"), None),
        ),
        check_vma=False,
    )
```

time: 142 us -> 116 us (0.82)
  Pallas kernels: 141 us -> 116 us
    pallas_call x1, Pallas kernels: 139 us -> 113 us  [layer(): pl.pallas_call(kernel, out_shape=(jax.ShapeDtypeStruct((TOK, D), BF), jax...]
where the time goes in v3:
time: 116 us
  Pallas kernels  116 us (100%)
    pallas_call x1, Pallas kernels, layer(): pl.pallas_call(kernel, out_shape=(jax.ShapeDtypeStruct((TOK, D), BF), jax...  113 us

profile of v3, /device:TPU:1, one launch (start us, length us, event | category | flops | bytes accessed | tf_op | source)
XLA Modules:
  0.0 116.2 jit_solution(11869423522645437250)
XLA Ops:
  0.6 113.4 %shard_map.144 = (bf16[128,1024]{1,0:T(8,128)(2,1)}, bf16[128,1024]{1,0:T(8,128)(2,1)}, f32[128,256]{1,0:T(8,128)}, f32[128,256]{1,0:T(8,128)}, f32[32,1024]{1,0...) custom-call(bf16[128,1024]{1,0:T(8,128)(2,1)} %bitcast.6, bf16[128,1024]{1,0:T(8,128)(2,1)} %bitcast.7, ...), custom_call_target="tpu_custom_call" | custom-call | tf_op jit(solution)/shard_map/pallas_call | solution.py:877
  114.1 2.1 %shard_map.145 = (bf16[128,1024]{1,0:T(8,128)(2,1)}, bf16[128,1024]{1,0:T(8,128)(2,1)}, f32[1,104]{1,0:T(1,128)}, f32[8,3072]{1,0:T(8,128)}, f32[8,1024]{1,0:T(8...) custom-call(bf16[128,1024]{1,0:T(8,128)(2,1)} %get-tuple-element.21.mixed_ref, ...), custom_call_target="tpu_custom_call" | custom-call | tf_op jit(solution)/shard_map/pallas_call | solution.py:895

commit v4 on v3

--- a/solution.py
+++ b/solution.py
@@ -288,7 +288,7 @@
         value = float(np.float32(10000.0) ** np.float32(-2.0 * k / ROT))
         rate = jnp.where(lax.rem(iota((1, 128), 1), 8) == k, value, rate)
 
-    @pl.loop(0, 8)
+    @pl.loop(0, 8, unroll=2)
     def _(i):
         where = i * QB + iota((QB, 128), 0)
         angle = (where - begin_of(where)).astype(F32) * rate
@@ -298,6 +298,7 @@
         sine = jnp.where(lane < ROT // 2, -sine, sine)
         tabs[rows_at(i, QB), :] = jnp.where(lane < ROT, sine, 0.0)
 
+    normed_gather.step(1)
     seq_all(0, wst, 16).wait_recv()
     seq_all(4, sgot, 16).wait_recv()
 
@@ -310,7 +311,6 @@
     def _(j):
         batch_copy(j, 0, sall.at[rows_at(b, 16)], sall.at[rows_at(b, 16)]).start()
 
-    normed_gather.step(1)
     weight_gather.step(1)
 
     batch_all(0, sall, 16).wait_recv()
@@ -371,7 +371,7 @@
     dy_gather.start(4, 5, 3, 6)
     normed_gather.step(4)
 
-    @pl.loop(0, 4)
+    @pl.loop(0, 4, unroll=4)
     def _(i):
         out = dot(nrm[rows_at(i, 512), :], wcat[:, 0:256]) + brow[:, 0:256]
         prj[pl.ds(i * 8, 8)] = out.reshape(8, 64, 256)
@@ -395,7 +395,7 @@
     def blocks_of(ref, order, i):
         return jnp.concatenate([ref[order[i * 4 + k]] for k in range(4)], axis=0)
 
-    @pl.loop(0, 8)
+    @pl.loop(0, 8, unroll=4)
     def _(i):
         at = rows_at(i, QB)
         come = blocks_of(prj, inv_ref, i)
@@ -433,21 +433,23 @@
             expos = jnp.exp(scores - peak).astype(BF)
             return peak, total * jnp.exp(top - peak) + dot(expos, va[k_at, :])
 
-        start = (jnp.full((AB, 1), NEG, F32), jnp.zeros((AB, 128), F32))
-        carry = lax.fori_loop(0, i, lambda j, carry: step(j, carry, False), start)
-        top, total = step(i, carry, True)
+        carry = (jnp.full((AB, 1), NEG, F32), jnp.zeros((AB, 128), F32))
+        for j in range(i + 1):
+            carry = step(j, carry, j == i)
+        top, total = carry
         norm = total[:, 64:65]
         osort[pl.ds(i * (AB // 64), AB // 64)] = (total / norm)[:, 0:64].reshape(AB // 64, 64, HD)
         qa[at, :] = with_lanes(qa[at, :].astype(F32), 68, pieces_of(-(top + jnp.log(norm)))).astype(BF)
 
-    pl.loop(0, 3)(attend)
+    for i in range(3):
+        attend(i)
     dy_gather.wait(4)
     dy_gather.start(11)
     dy_gather.wait(5)
     dy_gather.start(12, 9, 10)
-    pl.loop(3, 4)(attend)
-
-    @pl.loop(0, 4)
+    attend(3)
+
+    @pl.loop(0, 4, unroll=4)
     def _(i):
         at = rows_at(i, 512)
         hidden = dot(nrm[at, :], wcat[:, 256:512]) + brow[:, 256:512]
@@ -484,9 +486,6 @@
                 self.begin.append(at)
                 at += entry[3]
 
-        def chip(self, n):
-            return pl.ds(pl.multiple_of((self.order[n][0] * 4 + self.order[n][1]) * 256, 256), 256)
-
         def at(self, n, core, low, count):
             zz, xx = self.order[n]
             return pl.ds(pl.multiple_of(slot(zz, xx, core) * TOK + low, 16), count)
@@ -547,14 +546,18 @@
     mixed_sum = Scatter(part_m, land_m, 0)
     dn_sum = Scatter(part_d, land_d, 1)
 
+    def halves_of(which):
+        return [(which, xo // 2), (which, 1 - xo // 2)]
+
+    for which, side in halves_of(zo) + halves_of(z):
+        at = rows_at(which * 2 + side, 512)
+        part_m[at, :] = (dot(act[at, :], wd2[...]) + dot(ost[at, :], wob[...])).astype(BF)
     for n in range(8):
-        at = mixed_sum.chip(n)
-        part_m[at, :] = (dot(act[at, :], wd2[...]) + dot(ost[at, :], wob[...])).astype(BF)
         mixed_sum.start(n)
 
     dy_gather.step(4)
 
-    @pl.loop(0, 4)
+    @pl.loop(0, 4, unroll=4)
     def _(i):
         at = rows_at(i, 512)
         dy = dya[at, :]
@@ -568,9 +571,9 @@
 
     gdacc[...] = jnp.zeros_like(gdacc)
 
-    @pl.loop(0, 4)
-    def _(i):
-        at = rows_at(i, 512)
+    @pl.loop(0, 2, unroll=2)
+    def _(i):
+        at = rows_at(i, 1024)
         gdacc[0:256, :] += dot_tn(act[at, :], dya[at, :])
         gdacc[256:320, :] += dot_tn(ost[at, :], dya[at, :])
 
@@ -620,9 +623,9 @@
 
     gtu[...] = jnp.zeros_like(gtu)
 
-    @pl.loop(0, 4)
-    def _(i):
-        at = rows_at(i, 512)
+    @pl.loop(0, 2, unroll=2)
+    def _(i):
+        at = rows_at(i, 1024)
         gtu[...] += dot_tn(dcat[at, 256:512], nrm[at, :])
 
     sum_u = column_sum(256)
@@ -632,7 +635,7 @@
     column_start(5, gusend, gurecv, 128)
 
 
-    @pl.loop(0, 8)
+    @pl.loop(0, 8, unroll=4)
     def _(i):
         at = rows_at(i, QB)
         grads = blocks_of(dost, inv_ref, i).astype(F32)
@@ -646,10 +649,7 @@
     dkt[...] = jnp.zeros_like(dkt)
     dvt[...] = jnp.zeros_like(dvt)
 
-    mixed_sum.step(5)
-
-    @pl.loop(0, ROW // AB)
-    def _(i):
+    def attend_back(i):
         at = rows_at(i, AB)
 
         def step(j, dq, masked):
@@ -662,15 +662,20 @@
             dvt[:, k_at] += dot(doat[:, at], probs.astype(BF))
             return dq + dot(grads, ka[k_at, :])
 
-        dq = lax.fori_loop(0, i, lambda j, dq: step(j, dq, False), jnp.zeros((AB, 128), F32))
-        dqs[at, :] = step(i, dq, True) * 0.125
+        dq = jnp.zeros((AB, 128), F32)
+        for j in range(i + 1):
+            dq = step(j, dq, j == i)
+        dqs[at, :] = dq * 0.125
+
+    for i in range(ROW // AB):
+        attend_back(i)
 
     mixed_sum.step(6)
+    mixed_sum.step(5)
     column_sums(3, gdrecv, gdpair, gdland, 32)
     column_sums(4, gorecv, gopair, goland, 8)
-    column_sums(5, gurecv, gupair, guland, 128)
-
-    @pl.loop(0, 8)
+
+    @pl.loop(0, 8, unroll=4)
     def _(i):
         at = rows_at(i, QB)
         both = jnp.concatenate([dqs[at, 0:64], dkt[:, at].T], axis=1)
@@ -683,14 +688,16 @@
     def _(j):
         dcat[rows_at(j, QB), 0:256] = blocks_of(dsort, order_ref, j)
 
-    for n in range(8):
-        at = dn_sum.chip(n)
+    for k, (which, side) in enumerate(halves_of(zo) + halves_of(z)):
+        at = rows_at(which * 2 + side, 512)
         part_d[at, :] = dot_nt(dcat[at, :], wcat[...]).astype(BF)
-        dn_sum.start(n)
-        if n == 3:
-            dn_sum.step(0)
-
-    dn_sum.step(2)
+        if k == 0:
+            dn_sum.start(0)
+        elif k == 1:
+            dn_sum.start(1, 2, 3)
+    dn_sum.step(0)
+    dn_sum.start(4, 5, 6, 7)
+    column_sums(5, gurecv, gupair, guland, 128)
 
     gtq[...] = jnp.zeros_like(gtq)
 
@@ -699,10 +706,9 @@
         gtq[...] += dot_tn(dcat[at, 0:256], nrm[at, :])
 
     pl.loop(0, 2)(add_gtq)
-    dn_sum.step(1)
-    dn_sum.step(3)
     pl.loop(2, 4)(add_gtq)
 
+    dn_sum.step(2)
     sum_q = column_sum(0)
     dn_sum.step(4)
     hand_out(gtq, rawq, sum_q, 0, gqsend)
@@ -712,6 +718,9 @@
     def _(j):
         peer = lax.rem(b + j, BATCH)
         batch_copy(j, 6, gqsend.at[rows_at(peer, 128)], gqrecv.at[rows_at(b, 128)]).start()
+
+    dn_sum.step(1)
+    dn_sum.step(3)
 
     to_owners(pair_sum(5, gupair, guland, 128), gusum, gufin, 1)
     def low_half(part_of):
@@ -740,8 +749,8 @@
         peer = lax.rem(s + j, SEQ)
         seq_copy(j, 3, fsend.at[rows_at(peer, 8)], frecv.at[rows_at(s, 8)]).start()
 
+    dn_sum.step(6)
     dn_sum.step(5)
-    dn_sum.step(6)
     batch_all(6, gqrecv, 128).wait_recv()
     total = gqrecv[0:128, :].astype(F32)
     for k in range(1, BATCH):

time: 116 us -> 108 us (0.931)
  Pallas kernels: 116 us -> 107 us
    pallas_call x1, Pallas kernels: 113 us -> 105 us  [layer(): pl.pallas_call(kernel, out_shape=(jax.ShapeDtypeStruct((TOK, D), BF), jax...]
where the time goes in v4:
time: 108 us
  Pallas kernels  107 us (99%)
    pallas_call x1, Pallas kernels, layer(): pl.pallas_call(kernel, out_shape=(jax.ShapeDtypeStruct((TOK, D), BF), jax...  105 us

profile of v4, /device:TPU:1, one launch (start us, length us, event | category | flops | bytes accessed | tf_op | source)
XLA Modules:
  0.0 107.7 jit_solution(15127618018158455433)
XLA Ops:
  0.6 104.9 %shard_map.144 = (bf16[128,1024]{1,0:T(8,128)(2,1)}, bf16[128,1024]{1,0:T(8,128)(2,1)}, f32[128,256]{1,0:T(8,128)}, f32[128,256]{1,0:T(8,128)}, f32[32,1024]{1,0...) custom-call(bf16[128,1024]{1,0:T(8,128)(2,1)} %bitcast.6, bf16[128,1024]{1,0:T(8,128)(2,1)} %bitcast.7, ...), custom_call_target="tpu_custom_call" | custom-call | tf_op jit(solution)/shard_map/pallas_call | solution.py:886
  105.6 2.1 %shard_map.145 = (bf16[128,1024]{1,0:T(8,128)(2,1)}, bf16[128,1024]{1,0:T(8,128)(2,1)}, f32[1,104]{1,0:T(1,128)}, f32[8,3072]{1,0:T(8,128)}, f32[8,1024]{1,0:T(8...) custom-call(bf16[128,1024]{1,0:T(8,128)(2,1)} %get-tuple-element.21.mixed_ref, ...), custom_call_target="tpu_custom_call" | custom-call | tf_op jit(solution)/shard_map/pallas_call | solution.py:904

commit v5 on v4

--- a/solution.py
+++ b/solution.py
@@ -55,7 +55,7 @@
     mixed_ref, gtok_ref, gd_ref, go_ref, small_ref, nrm, dya, ssend, sgot, sall, wsend, wst, wbuf, wd2, wos, wo2, wob, rawq, rawu, cols, wcat, brow, drow,
     prj, act, dge, tabc, tabs, qa, ka, va, kat, vat, qat, doa, doat, dost, osort, ost,
     dcat, dkt, dvt, dsort, dqs,
-    part_m, part_d, land_m, land_d, gdpair, gdland, gopair, goland, gupair, guland,
+    part_m, part_d, land_m, land_d, gdpair, gdland, gopair, goland, gupair, guland, keptu, keptq,
     gdacc, gtq, gtu, gdsend, gosend, gdrecv, gorecv,
     gusend, gurecv, gusum, gufin, gqsend, gqrecv, gqsum, gqfin,
     flat, fsend, frecv, fsum, fall,
@@ -209,12 +209,12 @@
             if n == 0:
                 self.start(0, 1, 2, 3)
             elif n == 1:
+                self.wait(0)
+                self.start(7)
+                self.wait(1)
+                self.start(8)
                 self.wait(2)
-                self.start(4, 5, 6)
-                self.wait(0)
-                self.start(7, 9)
-                self.wait(1)
-                self.start(8, 10)
+                self.start(4, 5, 6, 9, 10)
             elif n == 2:
                 self.wait(4)
                 self.start(11, 13)
@@ -312,6 +312,7 @@
         batch_copy(j, 0, sall.at[rows_at(b, 16)], sall.at[rows_at(b, 16)]).start()
 
     weight_gather.step(1)
+    dy_gather.start(2)
 
     batch_all(0, sall, 16).wait_recv()
 
@@ -341,9 +342,8 @@
     wide = iota((1, D), 1)
     drow[...] = small_row(7 * D + wide) + small_row(12 * D + wide)
 
-    dy_gather.start(2)
+    normed_gather.step(2)
     weight_gather.step(2)
-    normed_gather.step(2)
     dy_gather.start(0, 1)
     weight_gather.step(3)
 
@@ -549,11 +549,15 @@
     def halves_of(which):
         return [(which, xo // 2), (which, 1 - xo // 2)]
 
-    for which, side in halves_of(zo) + halves_of(z):
+    for k, (which, side) in enumerate(halves_of(zo) + halves_of(z)):
         at = rows_at(which * 2 + side, 512)
         part_m[at, :] = (dot(act[at, :], wd2[...]) + dot(ost[at, :], wob[...])).astype(BF)
-    for n in range(8):
-        mixed_sum.start(n)
+        if k == 0:
+            mixed_sum.start(0)
+        elif k == 1:
+            mixed_sum.start(1, 2, 3)
+    mixed_sum.step(0)
+    mixed_sum.start(4, 5, 6, 7)
 
     dy_gather.step(4)
 
@@ -564,10 +568,7 @@
         dcat[at, 256:512] = (dot_nt(dy, wd2[...]) * dge[at, :]).astype(BF)
         dost[pl.ds(i * 8, 8)] = dot_nt(dy, wob[...]).astype(BF).reshape(8, 64, HD)
 
-    mixed_sum.step(0)
     mixed_sum.step(2)
-    mixed_sum.step(1)
-    mixed_sum.step(3)
 
     gdacc[...] = jnp.zeros_like(gdacc)
 
@@ -584,6 +585,10 @@
     column_start(3, gdsend, gdrecv, 32)
     column_start(4, gosend, gorecv, 8)
 
+    mixed_sum.step(4)
+    mixed_sum.step(1)
+    mixed_sum.step(3)
+
     def column_sum(low):
         def add(i, total):
             return total + jnp.sum(dcat[rows_at(i, QB), low : low + 256].astype(F32), axis=0, keepdims=True)
@@ -594,16 +599,11 @@
         for k in range(values.shape[1] // 128):
             flat[line + k : line + k + 1, :] = values[:, k * 128 : k * 128 + 128]
 
-    def hand_out(gt, raw, sums, k, send):
+    def hand_out(gt, kept, sums, k, send):
         for i in range(4):
             at = slice(i * 256, i * 256 + 256)
             grad = gt[0:256, at].T
-            gain = jnp.sum(grad * raw[at, :], axis=1, keepdims=True)
-            shift = jnp.sum(sums * raw[at, :], axis=1, keepdims=True)
-            lane = iota((256, 128), 1)
-            spread = jnp.where(lane == 0, gain, jnp.where(lane == 1, shift, 0.0)).T
-            to_flat(k * 8 + i * 2, spread[0:1, :])
-            to_flat(k * 8 + 8 + i * 2, spread[1:2, :])
+            kept[at, :] = grad
             grad = grad * cols[at, k : k + 1] + cols[at, k + 1 : k + 2] * sums
             for m in range(8):
                 for h in range(2):
@@ -612,6 +612,17 @@
                     send[place : place + 16, :] = jnp.concatenate(
                         [grad[first : first + 8, :], grad[second : second + 8, :]], axis=0
                     ).astype(BF)
+
+    def small_sums(kept, raw, sums, k):
+        for i in range(4):
+            at = slice(i * 256, i * 256 + 256)
+            gain = jnp.sum(kept[at, :] * raw[at, :], axis=1, keepdims=True)
+            shift = jnp.sum(sums * raw[at, :], axis=1, keepdims=True)
+            lane = iota((256, 128), 1)
+            spread = jnp.where(lane == 0, gain, jnp.where(lane == 1, shift, 0.0)).T
+            to_flat(k * 8 + i * 2, spread[0:1, :])
+            to_flat(k * 8 + 8 + i * 2, spread[1:2, :])
+
     def to_owners(total, total_ref, final, k):
         total_ref[...] = total
         final[rows_at(s, 8), :] = total_ref[rows_at(s, 8), :]
@@ -629,8 +640,7 @@
         gtu[...] += dot_tn(dcat[at, 256:512], nrm[at, :])
 
     sum_u = column_sum(256)
-    mixed_sum.step(4)
-    hand_out(gtu, rawu, sum_u, 2, gusend)
+    hand_out(gtu, keptu, sum_u, 2, gusend)
     gurecv[rows_at(y, 256), :] = gusend[rows_at(y, 256), :]
     column_start(5, gusend, gurecv, 128)
 
@@ -672,8 +682,6 @@
 
     mixed_sum.step(6)
     mixed_sum.step(5)
-    column_sums(3, gdrecv, gdpair, gdland, 32)
-    column_sums(4, gorecv, gopair, goland, 8)
 
     @pl.loop(0, 8, unroll=4)
     def _(i):
@@ -688,30 +696,25 @@
     def _(j):
         dcat[rows_at(j, QB), 0:256] = blocks_of(dsort, order_ref, j)
 
-    for k, (which, side) in enumerate(halves_of(zo) + halves_of(z)):
+    def dn_part(which, side):
         at = rows_at(which * 2 + side, 512)
         part_d[at, :] = dot_nt(dcat[at, :], wcat[...]).astype(BF)
-        if k == 0:
-            dn_sum.start(0)
-        elif k == 1:
-            dn_sum.start(1, 2, 3)
+
+    dn_part(*halves_of(zo)[0])
+    dn_sum.start(0)
+    dn_part(*halves_of(zo)[1])
+    dn_sum.start(1, 2, 3)
     dn_sum.step(0)
-    dn_sum.start(4, 5, 6, 7)
-    column_sums(5, gurecv, gupair, guland, 128)
-
     gtq[...] = jnp.zeros_like(gtq)
 
-    def add_gtq(i):
-        at = rows_at(i, 512)
+    @pl.loop(0, 2, unroll=2)
+    def _(i):
+        at = rows_at(i, 1024)
         gtq[...] += dot_tn(dcat[at, 0:256], nrm[at, :])
-
-    pl.loop(0, 2)(add_gtq)
-    pl.loop(2, 4)(add_gtq)
 
     dn_sum.step(2)
     sum_q = column_sum(0)
-    dn_sum.step(4)
-    hand_out(gtq, rawq, sum_q, 0, gqsend)
+    hand_out(gtq, keptq, sum_q, 0, gqsend)
     gqrecv[rows_at(b, 128), :] = gqsend[rows_at(b, 128), :]
 
     @pl.loop(1, BATCH)
@@ -719,10 +722,14 @@
         peer = lax.rem(b + j, BATCH)
         batch_copy(j, 6, gqsend.at[rows_at(peer, 128)], gqrecv.at[rows_at(b, 128)]).start()
 
-    dn_sum.step(1)
-    dn_sum.step(3)
-
-    to_owners(pair_sum(5, gupair, guland, 128), gusum, gufin, 1)
+    column_sums(5, gurecv, gupair, guland, 128)
+    dn_sum.step(4)
+    for which, side in halves_of(z):
+        dn_part(which, side)
+    dn_sum.start(4, 5, 6, 7)
+    small_sums(keptu, rawu, sum_u, 2)
+    small_sums(keptq, rawq, sum_q, 0)
+
     def low_half(part_of):
         return jnp.concatenate([part_of[:, 0:64], jnp.zeros((1, 64), F32)], axis=1)
 
@@ -749,13 +756,19 @@
         peer = lax.rem(s + j, SEQ)
         seq_copy(j, 3, fsend.at[rows_at(peer, 8)], frecv.at[rows_at(s, 8)]).start()
 
+    column_sums(3, gdrecv, gdpair, gdland, 32)
+    column_sums(4, gorecv, gopair, goland, 8)
+    dn_sum.step(1)
+    dn_sum.step(3)
+
     dn_sum.step(6)
-    dn_sum.step(5)
+    to_owners(pair_sum(5, gupair, guland, 128), gusum, gufin, 1)
     batch_all(6, gqrecv, 128).wait_recv()
     total = gqrecv[0:128, :].astype(F32)
     for k in range(1, BATCH):
         total = total + gqrecv[k * 128 : k * 128 + 128, :].astype(F32)
     to_owners(total, gqsum, gqfin, 2)
+    dn_sum.step(5)
     mixed_ref[...] = (mixed_sum.result() + x_ref[...].astype(F32) + drow[...]).astype(BF)
     output(0).start()
 
@@ -867,7 +880,7 @@
         ((32, 64, 256), BF), ((ROW, 128), F32),
         ((ROW, D), BF), ((ROW, D), BF),
         ((1920, D), BF), ((1920, D), BF), ((64, D), BF), ((32, D), BF), ((16, D), F32), ((8, D), F32),
-        ((256, 256), BF), ((128, 256), BF),
+        ((256, 256), BF), ((128, 256), BF), ((D, 256), F32), ((D, 256), F32),
         ((320, D), F32), ((256, D), F32), ((256, D), F32),
         ((256, D), BF), ((64, D), F32), ((256, D), BF), ((64, D), F32),
         ((D, 256), BF), ((D, 256), BF), ((128, 256), F32), ((128, 256), F32),

time: 108 us -> 103 us (0.954)
  Pallas kernels: 107 us -> 103 us
    pallas_call x1, Pallas kernels: 105 us -> 100 us  [layer(): pl.pallas_call(kernel, out_shape=(jax.ShapeDtypeStruct((TOK, D), BF), jax...]
where the time goes in v5:
time: 103 us
  Pallas kernels  103 us (100%)
    pallas_call x1, Pallas kernels, layer(): pl.pallas_call(kernel, out_shape=(jax.ShapeDtypeStruct((TOK, D), BF), jax...  100 us
    pallas_call x1, Pallas kernels, layer(): pl.pallas_call(finish, out_shape=(jax.ShapeDtypeStruct((TOK, D), BF), jax...  2.12 us

profile of v5, /device:TPU:1, one launch (start us, length us, event | category | flops | bytes accessed | tf_op | source)
XLA Modules:
  0.0 103.2 jit_solution(9798462111916790220)
XLA Ops:
  0.6 100.5 %shard_map.144 = (bf16[128,1024]{1,0:T(8,128)(2,1)}, bf16[128,1024]{1,0:T(8,128)(2,1)}, f32[128,256]{1,0:T(8,128)}, f32[128,256]{1,0:T(8,128)}, f32[32,1024]{1,0...) custom-call(bf16[128,1024]{1,0:T(8,128)(2,1)} %bitcast.6, bf16[128,1024]{1,0:T(8,128)(2,1)} %bitcast.7, ...), custom_call_target="tpu_custom_call" | custom-call | tf_op jit(solution)/shard_map/pallas_call | solution.py:899
  101.1 2.1 %shard_map.145 = (bf16[128,1024]{1,0:T(8,128)(2,1)}, bf16[128,1024]{1,0:T(8,128)(2,1)}, f32[1,104]{1,0:T(1,128)}, f32[8,3072]{1,0:T(8,128)}, f32[8,1024]{1,0:T(8...) custom-call(bf16[128,1024]{1,0:T(8,128)(2,1)} %get-tuple-element.21.mixed_ref, ...), custom_call_target="tpu_custom_call" | custom-call | tf_op jit(solution)/shard_map/pallas_call | solution.py:917

commit v6 on v5

--- a/solution.py
+++ b/solution.py
@@ -242,14 +242,14 @@
     weight_gather = Gather(
         wbuf, 2, 256, (rows_slots,), (s, yr * 2 + w), (s, yl * 2 + w), (s, y * 2 + wo_)
     )
+    normed_gather.step(0)
+
     @pl.loop(0, 32)
     def _(i):
         place = jnp.int32(0)
         for j in range(32):
             place = place + jnp.where(order_ref[j] == i, j, 0)
         inv_ref[i] = jnp.minimum(place, 31)
-
-    normed_gather.step(0)
 
     @pl.loop(1, SEQ)
     def _(j):
@@ -446,7 +446,7 @@
     dy_gather.wait(4)
     dy_gather.start(11)
     dy_gather.wait(5)
-    dy_gather.start(12, 9, 10)
+    dy_gather.start(12, 9, 10, 13, 14)
     attend(3)
 
     @pl.loop(0, 4, unroll=4)
@@ -457,8 +457,8 @@
         act[at, :] = (hidden * share).astype(BF)
         dge[at, :] = share + hidden * jnp.exp(-0.5 * hidden * hidden) * ((2.0 * np.pi) ** -0.5)
 
-    dy_gather.wait(7, 8, 11, 12)
-    dy_gather.start(13, 14, 15, 16)
+    dy_gather.wait(7, 8)
+    dy_gather.start(15)
 
     @pl.loop(0, 8)
     def _(j):
@@ -556,6 +556,8 @@
             mixed_sum.start(0)
         elif k == 1:
             mixed_sum.start(1, 2, 3)
+            dy_gather.wait(11, 12)
+            dy_gather.start(16)
     mixed_sum.step(0)
     mixed_sum.start(4, 5, 6, 7)
 
@@ -659,26 +661,21 @@
     dkt[...] = jnp.zeros_like(dkt)
     dvt[...] = jnp.zeros_like(dvt)
 
-    def attend_back(i):
-        at = rows_at(i, AB)
-
-        def step(j, dq, masked):
-            k_at = rows_at(j, AB)
-            probs = jnp.exp(dot(qa[at, :], kat[:, k_at]))
-            if masked:
-                probs = jnp.where(lower, probs, 0.0)
-            grads = (probs * dot(doa[at, :], vat[:, k_at])).astype(BF)
-            dkt[:, k_at] += dot(qat[:, at], grads)
-            dvt[:, k_at] += dot(doat[:, at], probs.astype(BF))
-            return dq + dot(grads, ka[k_at, :])
-
-        dq = jnp.zeros((AB, 128), F32)
-        for j in range(i + 1):
-            dq = step(j, dq, j == i)
-        dqs[at, :] = dq * 0.125
-
+    def attend_back(q_at, k_at, masked):
+        probs = jnp.exp(dot(qa[q_at, :], kat[:, k_at]))
+        if masked:
+            probs = jnp.where(lower, probs, 0.0)
+        grads = (probs * dot(doa[q_at, :], vat[:, k_at])).astype(BF)
+        dkt[:, k_at] += dot(qat[:, q_at], grads)
+        dvt[:, k_at] += dot(doat[:, q_at], probs.astype(BF))
+        dqs[q_at, :] += dot(grads, ka[k_at, :])
+
+    dqs[...] = jnp.zeros_like(dqs)
     for i in range(ROW // AB):
-        attend_back(i)
+        attend_back(slice(i * AB, i * AB + AB), slice(i * AB, i * AB + AB), True)
+        if i < ROW // AB - 1:
+            for k in range(i * AB, i * AB + AB, 256):
+                attend_back(slice(i * AB + AB, ROW), slice(k, k + 256), False)
 
     mixed_sum.step(6)
     mixed_sum.step(5)
@@ -686,7 +683,7 @@
     @pl.loop(0, 8, unroll=4)
     def _(i):
         at = rows_at(i, QB)
-        both = jnp.concatenate([dqs[at, 0:64], dkt[:, at].T], axis=1)
+        both = jnp.concatenate([dqs[at, 0:64] * 0.125, dkt[:, at].T], axis=1)
         both = both * tabc[at, :] - partner_of(both) * tabs[at, :]
         last = jnp.concatenate([dvt[:, at].T, jnp.zeros((QB, 64), F32)], axis=1)
         whole = jnp.concatenate([both, last], axis=1).astype(BF)
@@ -759,9 +756,8 @@
     column_sums(3, gdrecv, gdpair, gdland, 32)
     column_sums(4, gorecv, gopair, goland, 8)
     dn_sum.step(1)
+    dn_sum.step(6)
     dn_sum.step(3)
-
-    dn_sum.step(6)
     to_owners(pair_sum(5, gupair, guland, 128), gusum, gufin, 1)
     batch_all(6, gqrecv, 128).wait_recv()
     total = gqrecv[0:128, :].astype(F32)

time: 103 us -> 102 us (level)
  Pallas kernels: 103 us -> 101 us
    pallas_call x1, Pallas kernels: 100 us -> 99.4 us  [layer(): pl.pallas_call(kernel, out_shape=(jax.ShapeDtypeStruct((TOK, D), BF), jax...]
where the time goes in v6:
time: 102 us
  Pallas kernels  101 us (99%)
    pallas_call x1, Pallas kernels, layer(): pl.pallas_call(kernel, out_shape=(jax.ShapeDtypeStruct((TOK, D), BF), jax...  99.4 us
    pallas_call x1, Pallas kernels, layer(): pl.pallas_call(finish, out_shape=(jax.ShapeDtypeStruct((TOK, D), BF), jax...  2.12 us

profile of v6, /device:TPU:1, one launch (start us, length us, event | category | flops | bytes accessed | tf_op | source)
XLA Modules:
  0.0 102.1 jit_solution(14692470896514213404)
XLA Ops:
  0.6 99.4 %shard_map.144 = (bf16[128,1024]{1,0:T(8,128)(2,1)}, bf16[128,1024]{1,0:T(8,128)(2,1)}, f32[128,256]{1,0:T(8,128)}, f32[128,256]{1,0:T(8,128)}, f32[32,1024]{1,0...) custom-call(bf16[128,1024]{1,0:T(8,128)(2,1)} %bitcast.6, bf16[128,1024]{1,0:T(8,128)(2,1)} %bitcast.7, ...), custom_call_target="tpu_custom_call" | custom-call | tf_op jit(solution)/shard_map/pallas_call | solution.py:895
  100.0 2.1 %shard_map.145 = (bf16[128,1024]{1,0:T(8,128)(2,1)}, bf16[128,1024]{1,0:T(8,128)(2,1)}, f32[1,104]{1,0:T(1,128)}, f32[8,3072]{1,0:T(8,128)}, f32[8,1024]{1,0:T(8...) custom-call(bf16[128,1024]{1,0:T(8,128)(2,1)} %get-tuple-element.21.mixed_ref, ...), custom_call_target="tpu_custom_call" | custom-call | tf_op jit(solution)/shard_map/pallas_call | solution.py:913

commit v7 on v6

--- a/solution.py
+++ b/solution.py
@@ -345,7 +345,11 @@
     normed_gather.step(2)
     weight_gather.step(2)
     dy_gather.start(0, 1)
+    normed_gather.wait(7, 8)
+    normed_gather.start(15)
     weight_gather.step(3)
+    normed_gather.wait(11, 12)
+    normed_gather.start(16)
 
     @pl.loop(0, SEQ)
     def _(i):
@@ -366,7 +370,6 @@
     brow[:, 0:256] = row_q
     brow[:, 256:512] = row_u
 
-    normed_gather.step(3)
     dy_gather.wait(2)
     dy_gather.start(4, 5, 3, 6)
     normed_gather.step(4)

time: 102 us -> 102 us (level)
  no operation moved by 1% of the time
where the time goes in v7:
time: 102 us
  Pallas kernels  102 us (100%)
    pallas_call x1, Pallas kernels, layer(): pl.pallas_call(kernel, out_shape=(jax.ShapeDtypeStruct((TOK, D), BF), jax...  99.6 us
    pallas_call x1, Pallas kernels, layer(): pl.pallas_call(finish, out_shape=(jax.ShapeDtypeStruct((TOK, D), BF), jax...  2.12 us

profile of v7, /device:TPU:1, one launch (start us, length us, event | category | flops | bytes accessed | tf_op | source)
XLA Modules:
  0.0 102.3 jit_solution(8246825129862590438)
XLA Ops:
  0.6 99.6 %shard_map.144 = (bf16[128,1024]{1,0:T(8,128)(2,1)}, bf16[128,1024]{1,0:T(8,128)(2,1)}, f32[128,256]{1,0:T(8,128)}, f32[128,256]{1,0:T(8,128)}, f32[32,1024]{1,0...) custom-call(bf16[128,1024]{1,0:T(8,128)(2,1)} %bitcast.6, bf16[128,1024]{1,0:T(8,128)(2,1)} %bitcast.7, ...), custom_call_target="tpu_custom_call" | custom-call | tf_op jit(solution)/shard_map/pallas_call | solution.py:898
  100.2 2.1 %shard_map.145 = (bf16[128,1024]{1,0:T(8,128)(2,1)}, bf16[128,1024]{1,0:T(8,128)(2,1)}, f32[1,104]{1,0:T(1,128)}, f32[8,3072]{1,0:T(8,128)}, f32[8,1024]{1,0:T(8...) custom-call(bf16[128,1024]{1,0:T(8,128)(2,1)} %get-tuple-element.21.mixed_ref, ...), custom_call_target="tpu_custom_call" | custom-call | tf_op jit(solution)/shard_map/pallas_call | solution.py:916
